TPU v7x, 256 devices: a whole 4x4x8 slice. The times are simulated.
256 devices in a mesh: ens: 8 (over z), space: 32 (over x, y, core).
Axes of the slice: x: 4, y: 4, z: 8, core: 2. Of those that a mesh axis runs over, the one named last changes fastest.
Arguments:
- initial_state: float32 [3, 256, 128, 1024], P(None, 'space', 'ens'), may hold values from -6 to 6
- depth_field: float32 [256, 1024], P('space'), may hold values from 0.5 to 1.5
- obs_index: int32 [256, 64], P('space', 'ens'), may hold values from 0 to 127
- obs_value: float32 [256, 64], P('space', 'ens'), may hold values from -6 to 6
- obs_var: float32 [256, 64], P('space', 'ens'), may hold values from 0.5 to 4
- cotangent: float32 [3, 256, 128, 1024], P(None, 'space', 'ens'), may hold values from -6 to 6
Outputs:
- state_grad: float32 [3, 256, 128, 1024], P(None, 'space', 'ens')
- depth_grad: float32 [256, 1024], P('space')
Inputs may be any that keep to these rules, and one draw needn't show every extreme that they name: `obs_index`: observation j of a row lies in the block of columns j // 8; several observations may share a column.
All inputs are finite; a program needn't handle non-finite values.
Results may differ from a plain program's by a relative error of at most 0.00011.
Values sent between devices are 32-bit elements; how exact they have to be, the bound alone decides.
No kernel may reach another device: no remote copies, remote signals or barrier semaphores. Data moves between devices by JAX's collectives and lax.ppermute only.
A program may use at most 128 MiB of HBM per device.

v0:
```python
import functools
import math

import jax
import jax.numpy as jnp
from jax import lax
from jax.experimental import pallas as pl
from jax.experimental.pallas import tpu as pltpu
from jax.sharding import PartitionSpec as P

WAVE_COEF = 0.3
SPIN_COEF = 0.1
HALO = 4
HIGHEST = lax.Precision.HIGHEST
STATE_EDGE = ((0, 4), (1, 3), (2, 3))
ADJOINT_EDGE = ((0, 4), (2, 3), (1, 2))
VMEM = pl.BlockSpec(memory_space=pltpu.VMEM)
SMEM = pl.BlockSpec(memory_space=pltpu.SMEM)


def kernel_call(body, outs, ins, scratch=(), flops=0, name=None):
    moved = sum(math.prod(o) for o in outs) * 4 + sum(i.size for i in ins) * 4
    result = pl.pallas_call(
        body,
        out_shape=[jax.ShapeDtypeStruct(o, jnp.float32) for o in outs],
        in_specs=[SMEM if i.ndim == 1 else VMEM for i in ins],
        out_specs=[VMEM] * len(outs),
        scratch_shapes=[pltpu.VMEM(s, jnp.float32) for s in scratch],
        compiler_params=pltpu.CompilerParams(vmem_limit_bytes=40 * 2**20),
        cost_estimate=pl.CostEstimate(flops=flops, bytes_accessed=moved, transcendentals=0),
        name=name,
    )(*ins)
    return result


def exchanged(blocks):
    return lax.all_to_all(blocks, "ens", 0, 0, tiled=False)


def gathered(block, axis):
    count = lax.axis_size(axis)
    copies = jnp.broadcast_to(block[None], (count,) + block.shape)
    return lax.all_to_all(copies, axis, 0, 0, tiled=False)


def summed(block, axis):
    count = lax.axis_size(axis)
    distance = 1
    while distance < count:
        block = block + lax.ppermute(block, axis, [(i, i ^ distance) for i in range(count)])
        distance *= 2
    return block


def from_above(rows_sent):
    count = lax.axis_size("space")
    return lax.ppermute(rows_sent, "space", [(i, i + 1) for i in range(count - 1)])


def from_below(rows_sent):
    count = lax.axis_size("space")
    return lax.ppermute(rows_sent, "space", [(i + 1, i) for i in range(count - 1)])


def cols(field):
    width = field.shape[1]
    return pltpu.roll(field, width - 1, 1) - pltpu.roll(field, 1, 1)


def dot(a, b, dims=((1,), (0,))):
    return lax.dot_general(
        a, b, (dims, ((), ())), precision=HIGHEST, preferred_element_type=jnp.float32
    )


def spread_kernel(in_ref, out_ref):
    out_ref[0] = in_ref[...]


def by_columns(field_rows, groups):
    n, width = field_rows.shape
    part = width // groups
    return pl.pallas_call(
        spread_kernel,
        grid=(groups,),
        out_shape=jax.ShapeDtypeStruct((groups, n, part), jnp.float32),
        in_specs=[pl.BlockSpec((n, part), lambda j: (0, j))],
        out_specs=pl.BlockSpec((1, n, part), lambda j: (j, 0, 0)),
        name="spread",
    )(field_rows)


def padded_rows(edges, size, own_row, above, below):
    start = {}
    at = 0
    for f, n in edges:
        start[f] = (at, n)
        at += n * size

    def row(f, p, own_rows):
        first, n = start[f]
        if p < HALO:
            return above(first + (p - (HALO - n)) * size)
        if p < HALO + own_rows:
            return own_row(f, p - HALO)
        return below(first + (p - HALO - own_rows) * size)

    return row, at


def forward_kernel(
    inside_ref, state_ref, depth_ref, above_ref, below_ref,
    spread_ref, height_ref, east1_ref, north1_ref, east2_ref, north2_ref,
    e1, n1, h1, n2, depth,
):
    own, size, width = height_ref.shape
    groups = spread_ref.shape[0]
    part = width // groups
    low, high = HALO, HALO + own
    row, at = padded_rows(
        STATE_EDGE,
        size,
        lambda f, r: state_ref[f, r],
        lambda i: above_ref[i : i + size],
        lambda i: below_ref[i : i + size],
    )
    row = functools.partial(row, own_rows=own)
    depth[:HALO] = above_ref[at : at + HALO]
    depth[low:high] = depth_ref[...]
    depth[high:] = below_ref[at : at + HALO]

    def d(p):
        return depth[p : p + 1]

    for p in range(low - 3, high + 3):
        n1[p] = row(2, p) - WAVE_COEF * (row(0, p + 1) - row(0, p - 1)) - SPIN_COEF * row(1, p)
    for p in range(low - 2, high + 2):
        new_east = row(1, p) - WAVE_COEF * cols(row(0, p)) + SPIN_COEF * row(2, p)
        e1[p] = new_east
        flow = cols(d(p) * new_east) + (d(p + 1) * n1[p + 1] - d(p - 1) * n1[p - 1])
        h1[p] = (row(0, p) - WAVE_COEF * flow) * inside_ref[p]
    for p in range(low - 1, high + 1):
        n2[p] = n1[p] - WAVE_COEF * (h1[p + 1] - h1[p - 1]) - SPIN_COEF * e1[p]
    for p in range(low, high):
        r = p - low
        new_east = e1[p] - WAVE_COEF * cols(h1[p]) + SPIN_COEF * n1[p]
        flow = cols(d(p) * new_east) + (d(p + 1) * n2[p + 1] - d(p - 1) * n2[p - 1])
        new_height = h1[p] - WAVE_COEF * flow
        new_north = n2[p]
        height_ref[r] = new_height
        east1_ref[r] = e1[p]
        north1_ref[r] = n1[p]
        east2_ref[r] = new_east
        north2_ref[r] = new_north
        for f, field in enumerate((new_height, new_east, new_north)):
            for j in range(groups):
                spread_ref[j, f * own + r] = field[:, j * part : (j + 1) * part]


def backward_kernel(
    inside_ref, back_ref, above_ref, below_ref, seen_ref, depth_ref,
    east1_ref, north1_ref, east2_ref, north2_ref,
    depth_grad_ref, state_grad_ref,
    h2, h1, e1, n1, nt,
):
    own, size, width = east1_ref.shape
    groups = back_ref.shape[0]
    low, high = HALO, HALO + own
    wide = lambda ref, at: jnp.concatenate([ref[j, at] for j in range(groups)], axis=1)
    row, _ = padded_rows(
        ADJOINT_EDGE,
        size,
        lambda f, r: wide(back_ref, f * own + r),
        lambda i: wide(above_ref, slice(i, i + size)),
        lambda i: wide(below_ref, slice(i, i + size)),
    )
    row = functools.partial(row, own_rows=own)

    def d(p):
        return depth_ref[p : p + 1]

    for p in range(0, high + HALO):
        h2[p] = row(0, p) + seen_ref[p]
    for p in range(low - 3, high + 3):
        along = WAVE_COEF * (h2[p + 1] - h2[p - 1])
        nt[p] = row(2, p) + d(p) * along
    for p in range(low - 2, high + 2):
        across = WAVE_COEF * cols(h2[p])
        total = row(1, p) + d(p) * across
        h1[p] = (h2[p] + WAVE_COEF * (cols(total) + (nt[p + 1] - nt[p - 1]))) * inside_ref[p]
        if low - 1 <= p < high + 1:
            n1[p] = nt[p] + SPIN_COEF * total
        if low <= p < high:
            r = p - low
            e1[p] = total - SPIN_COEF * nt[p]
            along = WAVE_COEF * (h2[p + 1] - h2[p - 1])
            depth_grad_ref[r : r + 1] = jnp.sum(
                east2_ref[r] * across + north2_ref[r] * along, axis=0, keepdims=True
            )
    for p in range(low - 1, high + 1):
        along = WAVE_COEF * (h1[p + 1] - h1[p - 1])
        nt[p] = n1[p] + d(p) * along
    for p in range(low, high):
        r = p - low
        across = WAVE_COEF * cols(h1[p])
        along = WAVE_COEF * (h1[p + 1] - h1[p - 1])
        total = e1[p] + d(p) * across
        depth_grad_ref[r : r + 1] += jnp.sum(
            east1_ref[r] * across + north1_ref[r] * along, axis=0, keepdims=True
        )
        state_grad_ref[0, r] = h1[p] + WAVE_COEF * (cols(total) + (nt[p + 1] - nt[p - 1]))
        state_grad_ref[1, r] = total - SPIN_COEF * nt[p]
        state_grad_ref[2, r] = nt[p] + SPIN_COEF * total


def gram_kernel(observed_ref, params_ref, scaled_ref, extra_ref, gram_ref):
    groups, pairs, size, lanes = observed_ref.shape
    members = groups * size
    gram = jnp.zeros((members, members), jnp.float32)
    proj = jnp.zeros((8, members), jnp.float32)
    for q in range(pairs):
        seen = observed_ref[:, q].reshape(members, lanes)
        mean = jnp.mean(seen, axis=0, keepdims=True)
        value, var = params_ref[1, q : q + 1], params_ref[2, q : q + 1]
        inv_sd = 1.0 / jnp.sqrt(var)
        obs_scale = 1.0 / jnp.sqrt(var * (members - 1))
        scaled = (seen - mean) * obs_scale
        innovation = (value - mean) * inv_sd
        scaled_ref[q] = scaled
        extra_ref[q] = jnp.concatenate(
            [innovation, obs_scale, inv_sd, params_ref[0, q : q + 1]]
            + [jnp.zeros((4, lanes), jnp.float32)],
            axis=0,
        )
        gram += dot(scaled, scaled, ((1,), (1,)))
        lead = jnp.concatenate([innovation, jnp.zeros((7, lanes), jnp.float32)], axis=0)
        proj += dot(lead, scaled, ((1,), (1,)))
    gram_ref[:members] = gram
    gram_ref[members:] = proj


def factor_kernel(gram_ref, inverse_ref, mixing_ref, mean_ref):
    members = inverse_ref.shape[0]
    step = 8
    blocks = members // step
    lane = lax.broadcasted_iota(jnp.int32, (step, members), 1)
    sub = lax.broadcasted_iota(jnp.int32, (step, members), 0)
    left, right = [], []
    for i in range(blocks):
        eye = (lane == sub + i * step).astype(jnp.float32)
        left.append(gram_ref[i * step : (i + 1) * step] + eye)
        right.append(eye)
    for k in range(members):
        i0, s = divmod(k, step)
        top_left, top_right = left[i0][s : s + 1], right[i0][s : s + 1]
        pivot = top_left[:, k : k + 1]
        inverse_ref[k : k + 1] = top_right * (1.0 / jnp.sqrt(pivot))
        if k == members - 1:
            break
        turned = 1.0 / pivot
        scaled_left, scaled_right = top_left * turned, top_right * turned
        for i in range(i0, blocks):
            factor = left[i][:, k : k + 1]
            if i == i0:
                factor = jnp.where(sub[:, :1] > s, factor, 0.0)
            left[i] = left[i] - factor * scaled_left
            right[i] = right[i] - factor * scaled_right
    inverse = inverse_ref[...]
    proj = gram_ref[members:]
    mean = dot(dot(proj, inverse, ((1,), (1,))), inverse)
    mean_ref[...] = mean
    root = math.sqrt(members - 1)
    turned = inverse + mean[:1] / root
    turned = turned - jnp.mean(turned, axis=1, keepdims=True) + 1.0 / members
    mixing_ref[...] = turned.T


def cross_kernel(state_ref, cot_ref, out_ref):
    groups, sites, size, part = state_ref.shape
    members = groups * size
    total = jnp.zeros((members, members), jnp.float32)
    for at in range(0, sites, 2):
        pick = lambda ref: jnp.concatenate(
            [ref[:, at + i].reshape(members, part) for i in range(2)], axis=1
        )
        total += dot(pick(state_ref), pick(cot_ref), ((1,), (1,)))
    out_ref[...] = total


def mix_kernel(mixing_ref, cot_ref, out_ref):
    groups, sites, size, part = cot_ref.shape
    members = groups * size
    mixing = mixing_ref[...]
    for at in range(0, sites, 2):
        both = jnp.concatenate(
            [cot_ref[:, at + i].reshape(members, part) for i in range(2)], axis=1
        )
        mixed = dot(mixing, both)
        for i in range(2):
            out_ref[:, at + i] = mixed[:, i * part : (i + 1) * part].reshape(groups, size, part)


def per_device(initial_state, depth_field, obs_index, obs_value, obs_var, cotangent):
    groups = lax.axis_size("ens")
    ens_place = lax.axis_index("ens")
    space_place = lax.axis_index("space")
    fields, own_rows, own_members, width = initial_state.shape
    members = own_members * groups
    block_cols = width // groups
    tall = own_rows + 2 * HALO
    band = own_rows * lax.axis_size("space")
    sites = fields * own_rows
    half = own_rows // 2

    def edge(take):
        parts = [initial_state[f, take(n)].reshape(-1, width) for f, n in STATE_EDGE]
        return jnp.concatenate(parts + [depth_field[take(HALO)]])

    tail = edge(lambda n: slice(own_rows - n, own_rows))
    head = edge(lambda n: slice(0, n))
    above, below = from_above(tail), from_below(head)
    cot_in, _, _ = lax.optimization_barrier((cotangent, tail, head))
    cot_out = by_columns(cot_in.reshape(-1, width), groups)
    cot = exchanged(cot_out).reshape(groups, sites, own_members, block_cols)

    packed = jnp.stack([obs_index.astype(jnp.float32), obs_value, obs_var])
    params = gathered(packed, "ens").transpose(1, 2, 0, 3).reshape(3, own_rows, -1)
    observations = params.shape[2]

    row_number = space_place * own_rows - HALO + jnp.arange(tall)
    inside = ((row_number >= 0) & (row_number < band)).astype(jnp.float32)
    shape = (own_rows, own_members, width)
    padded = (tall, own_members, width)
    spread, height, east1, north1, east2, north2 = kernel_call(
        forward_kernel,
        [(groups, sites, own_members, block_cols)] + [shape] * 5,
        [inside, initial_state, depth_field, above, below],
        [padded] * 4 + [(tall, width)],
        flops=10**8,
        name="forward",
    )

    def selector(index_rows):
        n = index_rows.shape[0]
        offset = (jnp.arange(observations) // (observations // groups)) * block_cols
        place = index_rows.astype(jnp.int32) + offset[None]
        return (
            place[:, :, None] == lax.broadcasted_iota(jnp.int32, (n, observations, width), 2)
        ).astype(jnp.float32)

    def paired(a):
        return jnp.concatenate([a[..., :half, :, :], a[..., half:, :, :]], axis=-1)

    def unpaired(a):
        return jnp.concatenate([a[..., :observations], a[..., observations:]], axis=0)

    observed = jnp.einsum("rmc,roc->rmo", height, selector(params[0]), precision=HIGHEST)
    observed = gathered(paired(observed), "ens")
    spread, _ = lax.optimization_barrier((spread, observed))
    forecast = exchanged(spread)
    params_paired = jnp.concatenate([params[:, :half], params[:, half:]], axis=-1)
    scaled, extra, gram = kernel_call(
        gram_kernel,
        [(half, members, 2 * observations), (half, 8, 2 * observations), (members + 8, members)],
        [observed, params_paired],
        flops=4 * 2 * 6 * members**3,
        name="gram",
    )
    gram = summed(gram, "space")
    inverse, mixing, mean_weights = kernel_call(
        factor_kernel,
        [(members, members), (members, members), (8, members)],
        [gram],
        flops=10**9,
        name="factor",
    )
    mean_weights = mean_weights[0]
    scaled, extra, _ = lax.optimization_barrier((scaled, extra, gram))
    obs_pack = unpaired(jnp.concatenate([scaled, extra], axis=1))
    obs_tall = jnp.concatenate(
        [from_above(obs_pack[own_rows - HALO :]), obs_pack, from_below(obs_pack[:HALO])]
    )

    (own_cross,) = kernel_call(
        cross_kernel, [(members, members)], [forecast, cot], flops=10**10, name="cross"
    )
    (mixed,) = kernel_call(
        mix_kernel, [cot.shape], [mixing, cot], flops=10**10, name="mix"
    )
    back = exchanged(mixed)

    cross = jnp.sum(exchanged(own_cross.reshape(groups, own_members, members)), axis=0)
    cross = jnp.sum(gathered(cross, "space"), axis=0)
    cross = gathered(cross, "ens").reshape(members, members)
    cross = cross - jnp.mean(cross, axis=0, keepdims=True)
    identity = jnp.eye(members, dtype=jnp.float32)
    mean_grad = jnp.sum(cross, axis=1) / math.sqrt(members - 1)
    proj_grad = jnp.dot(
        inverse.T, jnp.dot(inverse, mean_grad, precision=HIGHEST), precision=HIGHEST
    )
    product = jnp.dot(cross.T, inverse.T, precision=HIGHEST)
    strict = jnp.tril(product, -1)
    mirrored = strict + strict.T + identity * product
    inner_grad = jnp.dot(
        inverse.T, jnp.dot(mirrored, inverse, precision=HIGHEST), precision=HIGHEST
    )
    outer = proj_grad[:, None] * mean_weights[None, :]
    gram_grad = -(inner_grad + outer + outer.T)
    both = jnp.concatenate([gram_grad, proj_grad[:, None]], axis=1)
    both = both - jnp.mean(both, axis=0, keepdims=True)
    own_both = lax.dynamic_slice_in_dim(both, ens_place * own_members, own_members, 0)

    obs_grad = jnp.einsum(
        "km,rmo->rko", own_both, obs_tall[:, : members + 1], precision=HIGHEST
    )
    innov_grad = jnp.einsum("m,rmo->ro", proj_grad, obs_tall[:, :members], precision=HIGHEST)
    obs_grad = (
        obs_grad * obs_tall[:, members + 1][:, None, :]
        - (innov_grad * obs_tall[:, members + 2] / members)[:, None, :]
    )
    seen = jnp.einsum(
        "rko,roc->rkc", obs_grad, selector(obs_tall[:, members + 3]), precision=HIGHEST
    )

    by_field = back.reshape(groups, fields, own_rows, own_members, block_cols)

    def adjoint_edge(take):
        parts = [
            by_field[:, f, take(n)].reshape(groups, -1, block_cols) for f, n in ADJOINT_EDGE
        ]
        return jnp.concatenate(parts, axis=1)

    adjoint_above = from_above(adjoint_edge(lambda n: slice(own_rows - n, own_rows)))
    adjoint_below = from_below(adjoint_edge(lambda n: slice(0, n)))
    depth_tall = jnp.concatenate([above[-HALO:], depth_field, below[-HALO:]])
    depth_grad, state_grad = kernel_call(
        backward_kernel,
        [(own_rows, width), (fields,) + shape],
        [
            inside, back, adjoint_above, adjoint_below, seen, depth_tall,
            east1, north1, east2, north2,
        ],
        [padded] * 5,
        flops=10**8,
        name="backward",
    )
    depth_grad = jnp.sum(gathered(depth_grad, "ens"), axis=0)
    return (state_grad, depth_grad)


def solution(mesh):
    in_specs = (
        P(None, "space", "ens", None),
        P("space", None),
        P("space", "ens"),
        P("space", "ens"),
        P("space", "ens"),
        P(None, "space", "ens", None),
    )
    out_specs = (P(None, "space", "ens", None), P("space", None))
    return jax.shard_map(
        per_device, mesh=mesh, in_specs=in_specs, out_specs=out_specs, check_vma=False
    )
```

profile of v0, /device:TPU:6, one launch (start us, length us, event | category | flops | bytes accessed | tf_op | source)
XLA Modules:
  0.0 274.5 jit_solution(251570054154817045)
XLA Ops:
  2.8 8.5 %all-to-all-start = ((f32[8,1,192]{2,1,0:T(1,128)}), f32[8,1,192]{2,1,0:T(1,128)S(1)}, u32[]{:S(2)}, u32[]{:S(2)}) async-start(f32[8,1,192]{2,1,0:T(1,128)} %reshape.113), calls=%async_computation | async-start | bytes 16384 | tf_op jit(solution)/shard_map/all_to_all | solution.py:43
  11.2 1.1 fusion.37
  12.3 1.3 fusion.38
  14.5 4.3 %collective-permute-start.1 = (f32[164,1024]{1,0:T(8,128)}, f32[164,1024]{1,0:T(8,128)S(1)}, u32[]{:S(2)}, u32[]{:S(2)}) collective-permute-start(f32[164,1024]{1,0:T(8,128)} %pad_maximum_fusion.2), channel_id=1, source_target_pairs={{1,0},{2,1},{3,2},{4,3},{5,4},{6,5},{7,6},{8,7},{9,8},{10,9},{11,1... | collective-permute-start | bytes 2015240 | tf_op jit(solution)/shard_map/ppermute | solution.py:62
  19.8 1.9 collective-permute-start
  23.1 4.5 %collective-permute-done.1.below_ref = f32[164,1024]{1,0:T(8,128)S(1)} collective-permute-done((f32[164,1024]{1,0:T(8,128)}, f32[164,1024]{1,0:T(8,128)S(1)}, u32[]{:S(2)}, u32[]{:S(2)}) %collective-permute-start.1) | collective-permute-done | bytes 671776 | tf_op jit(solution)/shard_map/ppermute | solution.py:62
  27.6 6.7 %collective-permute-done.above_ref = f32[164,1024]{1,0:T(8,128)S(1)} collective-permute-done((f32[164,1024]{1,0:T(8,128)}, f32[164,1024]{1,0:T(8,128)S(1)}, u32[]{:S(2)}, u32[]{:S(2)}) %collective-permute-start) | collective-permute-done | bytes 671776 | tf_op jit(solution)/shard_map/ppermute | solution.py:57
  34.3 4.6 %forward.1 = (f32[8,24,16,128]{3,2,1,0:T(8,128)}, f32[8,16,1024]{2,1,0:T(8,128)S(1)}, f32[8,16,1024]{2,1,0:T(8,128)S(1)}, f32[8,16,1024]{2,1,0:T(8,128)S(1)}, f3...) custom-call(f32[16]{0:T(128)S(1)} %and_convert_fusion.inside_ref, f32[3,8,16,1024]{3,2,1,0:T(8,128)S(1)} %copy-done, ...), custom_call_target="tpu_custom_call" | custom-call | flops 100000000 | bytes 7143488 | tf_op jit(solution)/shard_map/forward/pallas_call | solution.py:23
  41.3 1.2 fusion.2
  43.3 6.9 %all-to-all-start.1 = ((f32[8,4,16,128]{3,2,1,0:T(8,128)}), f32[8,4,16,128]{3,2,1,0:T(8,128)S(1)}, u32[]{:S(2)}, u32[]{:S(2)}) async-start(f32[8,4,16,128]{3,2,1,0:T(8,128)} %broadcast_in_dim.16), calls=%async_computation.1 | async-start | bytes 524288 | tf_op jit(solution)/shard_map/all_to_all | solution.py:43
  50.3 5.4 %spread.1 = f32[8,384,128]{2,1,0:T(8,128)} custom-call(f32[384,1024]{1,0:T(8,128)} %bitcast.83), custom_call_target="tpu_custom_call" | custom-call | tf_op jit(solution)/shard_map/spread/pallas_call | solution.py:83
  55.7 5.1 %all-to-all-done.1.observed_ref = f32[8,4,16,128]{3,2,1,0:T(8,128)S(1)} async-done(((f32[8,4,16,128]{3,2,1,0:T(8,128)}), f32[8,4,16,128]{3,2,1,0:T(8,128)S(1)}, u32[]{:S(2)}, u32[]{:S(2)}) %all-to-all-start.1) | async-done | bytes 262176 | tf_op jit(solution)/shard_map/all_to_all | solution.py:43
  61.5 3.6 %all-to-all-start.2 = ((f32[8,384,128]{2,1,0:T(8,128)}), f32[8,384,128]{2,1,0:T(8,128)S(1)}, u32[]{:S(2)}, u32[]{:S(2)}) async-start(f32[8,384,128]{2,1,0:T(8,128)} %spread.1), calls=%async_computation.2 | async-start | bytes 3145728 | tf_op jit(solution)/shard_map/all_to_all | solution.py:37
  65.1 34.0 %all-to-all-done.2 = f32[8,384,128]{2,1,0:T(8,128)S(1)} async-done(((f32[8,384,128]{2,1,0:T(8,128)}), f32[8,384,128]{2,1,0:T(8,128)S(1)}, u32[]{:S(2)}, u32[]{:S(2)}) %all-to-all-start.2) | async-done | bytes 1572896 | tf_op jit(solution)/shard_map/all_to_all | solution.py:37
  99.1 3.6 %all-to-all-start.4 = ((f32[8,24,16,128]{3,2,1,0:T(8,128)}), f32[8,24,16,128]{3,2,1,0:T(8,128)S(1)}, u32[]{:S(2)}, u32[]{:S(2)}) async-start(f32[8,24,16,128]{3,2,1,0:T(8,128)} %get-tuple-element.30), calls=%async_computation.4 | async-start | bytes 3145728 | tf_op jit(solution)/shard_map/all_to_all | solution.py:37
  103.9 1.0 gram.1
  105.0 1.2 collective-permute-done.2
  106.2 2.4 collective-permute-start.3
  108.7 2.5 collective-permute-done.3
  111.8 2.5 collective-permute-start.4
  114.3 3.6 %collective-permute-done.4 = f32[136,128]{1,0:T(8,128)} collective-permute-done((f32[136,128]{1,0:T(8,128)}, f32[136,128]{1,0:T(8,128)}, u32[]{:S(2)}, u32[]{:S(2)}) %collective-permute-start.4) | collective-permute-done | bytes 69664 | tf_op jit(solution)/shard_map/ppermute | solution.py:50
  118.9 3.9 %collective-permute-start.5 = (f32[136,128]{1,0:T(8,128)S(1)}, f32[136,128]{1,0:T(8,128)S(1)}, u32[]{:S(2)}, u32[]{:S(2)}) collective-permute-start(f32[136,128]{1,0:T(8,128)S(1)} %add.83), channel_id=1, source_target_pairs={{0,8},{1,9},{2,10},{3,11},{4,12},{5,13},{6,14},{7,15},{8,0},{9,1},... | collective-permute-start | bytes 208904 | tf_op jit(solution)/shard_map/ppermute | solution.py:50
  123.4 1.7 collective-permute-done.5
  125.1 2.7 collective-permute-start.6
  127.8 3.2 %collective-permute-done.6 = f32[136,128]{1,0:T(8,128)S(1)} collective-permute-done((f32[136,128]{1,0:T(8,128)S(1)}, f32[136,128]{1,0:T(8,128)S(1)}, u32[]{:S(2)}, u32[]{:S(2)}) %collective-permute-start.6) | collective-permute-done | bytes 69664 | tf_op jit(solution)/shard_map/ppermute | solution.py:50
  133.0 4.7 %all-to-all-done.4.state_ref = f32[8,24,16,128]{3,2,1,0:T(8,128)S(1)} async-done(((f32[8,24,16,128]{3,2,1,0:T(8,128)}), f32[8,24,16,128]{3,2,1,0:T(8,128)S(1)}, u32[]{:S(2)}, u32[]{:S(2)}) %all-to-all-start.4) | async-done | bytes 1572896 | tf_op jit(solution)/shard_map/all_to_all | solution.py:37
  137.7 2.1 cross.1
  139.8 3.5 %all-to-all-start.5 = ((f32[8,16,128]{2,1,0:T(8,128)}), f32[8,16,128]{2,1,0:T(8,128)S(1)}, u32[]{:S(2)}, u32[]{:S(2)}) async-start(f32[8,16,128]{2,1,0:T(8,128)} %bitcast.19), calls=%async_computation.5 | async-start | bytes 131072 | tf_op jit(solution)/shard_map/all_to_all | solution.py:37
  143.3 1.2 fusion.39
  144.5 7.1 %all-to-all-done.5 = f32[8,16,128]{2,1,0:T(8,128)S(1)} async-done(((f32[8,16,128]{2,1,0:T(8,128)}), f32[8,16,128]{2,1,0:T(8,128)S(1)}, u32[]{:S(2)}, u32[]{:S(2)}) %all-to-all-start.5) | async-done | bytes 65568 | tf_op jit(solution)/shard_map/all_to_all | solution.py:37
  152.3 15.1 %all-to-all-start.6 = ((f32[32,16,128]{2,1,0:T(8,128)}), f32[32,16,128]{2,1,0:T(8,128)S(1)}, u32[]{:S(2)}, u32[]{:S(2)}) async-start(f32[32,16,128]{2,1,0:T(8,128)} %broadcast_in_dim.17), calls=%async_computation.6 | async-start | bytes 524288 | tf_op jit(solution)/shard_map/all_to_all | solution.py:43
  167.4 11.4 %factor.1 = (f32[128,128]{1,0:T(8,128)S(1)}, f32[128,128]{1,0:T(8,128)S(1)}, f32[8,128]{1,0:T(8,128)S(1)}) custom-call(f32[136,128]{1,0:T(8,128)S(1)} %copy-done.14), custom_call_target="tpu_custom_call" | custom-call | flops 1000000000 | bytes 204800 | tf_op jit(solution)/shard_map/factor/pallas_call | solution.py:23
  178.8 2.1 collective-permute-start.9
  180.8 5.6 %collective-permute-start.10 = (f32[4,136,64]{2,1,0:T(8,128)S(1)}, f32[4,136,64]{2,1,0:T(8,128)}, u32[]{:S(2)}, u32[]{:S(2)}) collective-permute-start(f32[4,136,64]{2,1,0:T(8,128)S(1)} %get-tuple-element.54), channel_id=1, source_target_pairs={{1,0},{2,1},{3,2},{4,3},{5,4},{6,5},{7,6},{8,7},{9,8},{10,9},{11,1... | collective-permute-start | bytes 417800 | tf_op jit(solution)/shard_map/ppermute | solution.py:62
  187.2 3.3 %all-to-all-start.7 = ((f32[8,16,128]{2,1,0:T(8,128)}), f32[8,16,128]{2,1,0:T(8,128)S(1)}, u32[]{:S(2)}, u32[]{:S(2)}) async-start(f32[8,16,128]{2,1,0:T(8,128)} %broadcast_in_dim.18), calls=%async_computation.7 | async-start | bytes 131072 | tf_op jit(solution)/shard_map/all_to_all | solution.py:43
  190.5 2.5 mix.1
  193.0 5.8 %all-to-all-done.7 = f32[8,16,128]{2,1,0:T(8,128)S(1)} async-done(((f32[8,16,128]{2,1,0:T(8,128)}), f32[8,16,128]{2,1,0:T(8,128)S(1)}, u32[]{:S(2)}, u32[]{:S(2)}) %all-to-all-start.7) | async-done | bytes 65568 | tf_op jit(solution)/shard_map/all_to_all | solution.py:43
  198.8 3.6 %all-to-all-start.3 = ((f32[8,24,16,128]{3,2,1,0:T(8,128)}), f32[8,24,16,128]{3,2,1,0:T(8,128)S(1)}, u32[]{:S(2)}, u32[]{:S(2)}) async-start(f32[8,24,16,128]{3,2,1,0:T(8,128)} %mix.1), calls=%async_computation.3 | async-start | bytes 3145728 | tf_op jit(solution)/shard_map/all_to_all | solution.py:37
  203.2 1.2 pad_maximum_fusion
  204.3 1.5 maximum_convert_fusion
  208.1 31.3 %all-to-all-done.3.back_ref = f32[8,24,16,128]{3,2,1,0:T(8,128)S(1)} async-done(((f32[8,24,16,128]{3,2,1,0:T(8,128)}), f32[8,24,16,128]{3,2,1,0:T(8,128)S(1)}, u32[]{:S(2)}, u32[]{:S(2)}) %all-to-all-start.3) | async-done | bytes 1572896 | tf_op jit(solution)/shard_map/all_to_all | solution.py:37
  239.6 1.9 collective-permute-start.7
  241.6 6.1 %collective-permute-start.8 = (f32[8,144,128]{2,1,0:T(8,128)S(1)}, f32[8,144,128]{2,1,0:T(8,128)S(1)}, u32[]{:S(2)}, u32[]{:S(2)}) collective-permute-start(f32[8,144,128]{2,1,0:T(8,128)S(1)} %pad_maximum_fusion.4), channel_id=1, source_target_pairs={{1,0},{2,1},{3,2},{4,3},{5,4},{6,5},{7,6},{8,7},{9,8},{10,9},{11,1... | collective-permute-start | bytes 1769480 | tf_op jit(solution)/shard_map/ppermute | solution.py:62
  248.6 1.5 fusion.seen_ref
  250.0 2.9 %collective-permute-done.7.above_ref = f32[8,144,128]{2,1,0:T(8,128)S(1)} collective-permute-done((f32[8,144,128]{2,1,0:T(8,128)S(1)}, f32[8,144,128]{2,1,0:T(8,128)S(1)}, u32[]{:S(2)}, u32[]{:S(2)}) %collective-permute-start.7) | collective-permute-done | bytes 589856 | tf_op jit(solution)/shard_map/ppermute | solution.py:57
  252.9 2.0 collective-permute-done.8.below_ref
  254.9 4.6 %backward.1 = (f32[8,1024]{1,0:T(8,128)S(1)}, f32[3,8,16,1024]{3,2,1,0:T(8,128)}) custom-call(f32[16]{0:T(128)S(1)} %copy-done.16, f32[8,24,16,128]{3,2,1,0:T(8,128)S(1)} %all-to-all-done.3.back_ref, f32[8,144,128]{2,1,0:T(8,128)S(1)} %collective-permute-done.7.above_ref, f32[8,144,128]{2,1,0:T(8,128)S(1)} %collective-permute-done.8.below_ref, ...), custom_call_target="tpu_custom_call" | custom-call | flops 100000000 | bytes 7569472 | tf_op jit(solution)/shard_map/backward/pallas_call | solution.py:23
  259.5 14.3 %all_to_all.45 = f32[8,8,1024]{2,1,0:T(8,128)S(1)} all-to-all(f32[8,8,1024]{2,1,0:T(8,128)S(1)} %broadcast_in_dim.22), channel_id=1, replica_groups=mesh['ens'=8,'space'=32] {'ens'}, dimensions={0} | all-to-all | bytes 524288 | tf_op jit(solution)/shard_map/all_to_all | solution.py:43
  (117 shorter events, 20.8 us)
Async XLA Ops:
  0.6 12.9 %copy-start.11 = (f32[8,1024]{1,0:T(8,128)S(1)}, f32[8,1024]{1,0:T(8,128)}, u32[]{:S(2)}) copy-start(f32[8,1024]{1,0:T(8,128)} %depth_ref.1) | copy-start | bytes 98308
  2.8 19.0 %all-to-all-start = ((f32[8,1,192]{2,1,0:T(1,128)}), f32[8,1,192]{2,1,0:T(1,128)S(1)}, u32[]{:S(2)}, u32[]{:S(2)}) async-start(f32[8,1,192]{2,1,0:T(1,128)} %reshape.113), calls=%async_computation | async-start | bytes 16384 | tf_op jit(solution)/shard_map/all_to_all | solution.py:43
  13.6 20.8 %copy-start = (f32[3,8,16,1024]{3,2,1,0:T(8,128)S(1)}, f32[3,8,16,1024]{3,2,1,0:T(8,128)}, u32[]{:S(2)}) copy-start(f32[3,8,16,1024]{3,2,1,0:T(8,128)} %state_ref.1) | copy-start | bytes 4718596
  14.5 13.1 %collective-permute-start.1 = (f32[164,1024]{1,0:T(8,128)}, f32[164,1024]{1,0:T(8,128)S(1)}, u32[]{:S(2)}, u32[]{:S(2)}) collective-permute-start(f32[164,1024]{1,0:T(8,128)} %pad_maximum_fusion.2), channel_id=1, source_target_pairs={{1,0},{2,1},{3,2},{4,3},{5,4},{6,5},{7,6},{8,7},{9,8},{10,9},{11,1... | collective-permute-start | bytes 2015240 | tf_op jit(solution)/shard_map/ppermute | solution.py:62
  19.8 14.6 %collective-permute-start = (f32[164,1024]{1,0:T(8,128)}, f32[164,1024]{1,0:T(8,128)S(1)}, u32[]{:S(2)}, u32[]{:S(2)}) collective-permute-start(f32[164,1024]{1,0:T(8,128)} %pad_maximum_fusion.1), channel_id=1, source_target_pairs={{0,1},{1,2},{2,3},{3,4},{4,5},{5,6},{6,7},{7,8},{8,9},{9,10},{10,1... | collective-permute-start | bytes 2015240 | tf_op jit(solution)/shard_map/ppermute | solution.py:57
  21.7 17.2 %copy-start.21 = (s32[64]{0:T(128)}, s32[64]{0:T(128)S(1)}, u32[]{:S(2)}) copy-start(s32[64]{0:T(128)S(1)} %fusion.29) | copy-start | bytes 772
  21.7 17.2 %copy-start.15 = (f32[16]{0:T(128)}, f32[16]{0:T(128)S(1)}, u32[]{:S(2)}) copy-start(f32[16]{0:T(128)S(1)} %and_convert_fusion.inside_ref) | copy-start | bytes 196
  27.6 14.9 %copy-start.1 = (f32[164,1024]{1,0:T(8,128)}, f32[164,1024]{1,0:T(8,128)S(1)}, u32[]{:S(2)}) copy-start(f32[164,1024]{1,0:T(8,128)S(1)} %collective-permute-done.1.below_ref) | copy-start | bytes 2015236
  34.3 8.2 %copy-start.2 = (f32[164,1024]{1,0:T(8,128)}, f32[164,1024]{1,0:T(8,128)S(1)}, u32[]{:S(2)}) copy-start(f32[164,1024]{1,0:T(8,128)S(1)} %collective-permute-done.above_ref) | copy-start | bytes 2015236
  38.9 0.8 copy-start.5
  39.7 0.8 copy-start.7
  40.5 0.8 copy-start.9
  41.3 1.2 copy-start.3
  43.3 17.4 %all-to-all-start.1 = ((f32[8,4,16,128]{3,2,1,0:T(8,128)}), f32[8,4,16,128]{3,2,1,0:T(8,128)S(1)}, u32[]{:S(2)}, u32[]{:S(2)}) async-start(f32[8,4,16,128]{3,2,1,0:T(8,128)} %broadcast_in_dim.16), calls=%async_computation.1 | async-start | bytes 524288 | tf_op jit(solution)/shard_map/all_to_all | solution.py:43
  60.8 0.7 copy-start.12
  61.5 37.6 %all-to-all-start.2 = ((f32[8,384,128]{2,1,0:T(8,128)}), f32[8,384,128]{2,1,0:T(8,128)S(1)}, u32[]{:S(2)}, u32[]{:S(2)}) async-start(f32[8,384,128]{2,1,0:T(8,128)} %spread.1), calls=%async_computation.2 | async-start | bytes 3145728 | tf_op jit(solution)/shard_map/all_to_all | solution.py:37
  99.1 38.6 %all-to-all-start.4 = ((f32[8,24,16,128]{3,2,1,0:T(8,128)}), f32[8,24,16,128]{3,2,1,0:T(8,128)S(1)}, u32[]{:S(2)}, u32[]{:S(2)}) async-start(f32[8,24,16,128]{3,2,1,0:T(8,128)} %get-tuple-element.30), calls=%async_computation.4 | async-start | bytes 3145728 | tf_op jit(solution)/shard_map/all_to_all | solution.py:37
  102.7 25.1 %slice-start = ((f32[164,1024]{1,0:T(8,128)}), f32[4,1024]{1,0:T(4,128)S(1)}, s32[]{:S(2)}) async-start(f32[164,1024]{1,0:T(8,128)} %copy-done.1), calls=%async_computation.9 | async-start | bytes 32768 | tf_op jit(solution)/shard_map/slice | solution.py:435
  102.7 25.1 %slice-start.1 = ((f32[164,1024]{1,0:T(8,128)}), f32[4,1024]{1,0:T(4,128)S(1)}, s32[]{:S(2)}) async-start(f32[164,1024]{1,0:T(8,128)} %copy-done.2), calls=%async_computation.10 | async-start | bytes 32768 | tf_op jit(solution)/shard_map/slice | solution.py:435
  102.9 1.0 copy-start.13
  104.9 1.3 collective-permute-start.2
  106.2 4.9 %collective-permute-start.3 = (f32[136,128]{1,0:T(8,128)S(1)}, f32[136,128]{1,0:T(8,128)S(1)}, u32[]{:S(2)}, u32[]{:S(2)}) collective-permute-start(f32[136,128]{1,0:T(8,128)S(1)} %add.81), channel_id=1, source_target_pairs={{0,2},{1,3},{2,0},{3,1},{4,6},{5,7},{6,4},{7,5},{8,10},{9,11},{10,... | collective-permute-start | bytes 208904 | tf_op jit(solution)/shard_map/ppermute | solution.py:50
  111.8 6.1 %collective-permute-start.4 = (f32[136,128]{1,0:T(8,128)}, f32[136,128]{1,0:T(8,128)}, u32[]{:S(2)}, u32[]{:S(2)}) collective-permute-start(f32[136,128]{1,0:T(8,128)} %add.82), channel_id=1, source_target_pairs={{0,4},{1,5},{2,6},{3,7},{4,0},{5,1},{6,2},{7,3},{8,12},{9,13},{10,... | collective-permute-start | bytes 208904 | tf_op jit(solution)/shard_map/ppermute | solution.py:50
  118.9 6.2 %collective-permute-start.5 = (f32[136,128]{1,0:T(8,128)S(1)}, f32[136,128]{1,0:T(8,128)S(1)}, u32[]{:S(2)}, u32[]{:S(2)}) collective-permute-start(f32[136,128]{1,0:T(8,128)S(1)} %add.83), channel_id=1, source_target_pairs={{0,8},{1,9},{2,10},{3,11},{4,12},{5,13},{6,14},{7,15},{8,0},{9,1},... | collective-permute-start | bytes 208904 | tf_op jit(solution)/shard_map/ppermute | solution.py:50
  125.1 5.9 %collective-permute-start.6 = (f32[136,128]{1,0:T(8,128)S(1)}, f32[136,128]{1,0:T(8,128)S(1)}, u32[]{:S(2)}, u32[]{:S(2)}) collective-permute-start(f32[136,128]{1,0:T(8,128)S(1)} %add.84), channel_id=1, source_target_pairs={{0,16},{1,17},{2,18},{3,19},{4,20},{5,21},{6,22},{7,23},{8,24},{9,... | collective-permute-start | bytes 208904 | tf_op jit(solution)/shard_map/ppermute | solution.py:50
  139.8 27.6 %copy-start.14 = (f32[136,128]{1,0:T(8,128)S(1)}, f32[136,128]{1,0:T(8,128)}, u32[]{:S(2)}) copy-start(f32[136,128]{1,0:T(8,128)} %add.85.gram_ref) | copy-start | bytes 208900
  139.8 11.8 %all-to-all-start.5 = ((f32[8,16,128]{2,1,0:T(8,128)}), f32[8,16,128]{2,1,0:T(8,128)S(1)}, u32[]{:S(2)}, u32[]{:S(2)}) async-start(f32[8,16,128]{2,1,0:T(8,128)} %bitcast.19), calls=%async_computation.5 | async-start | bytes 131072 | tf_op jit(solution)/shard_map/all_to_all | solution.py:37
  152.3 34.2 %all-to-all-start.6 = ((f32[32,16,128]{2,1,0:T(8,128)}), f32[32,16,128]{2,1,0:T(8,128)S(1)}, u32[]{:S(2)}, u32[]{:S(2)}) async-start(f32[32,16,128]{2,1,0:T(8,128)} %broadcast_in_dim.17), calls=%async_computation.6 | async-start | bytes 524288 | tf_op jit(solution)/shard_map/all_to_all | solution.py:43
  178.8 23.7 %collective-permute-start.9 = (f32[4,136,64]{2,1,0:T(8,128)S(1)}, f32[4,136,64]{2,1,0:T(8,128)S(1)}, u32[]{:S(2)}, u32[]{:S(2)}) collective-permute-start(f32[4,136,64]{2,1,0:T(8,128)S(1)} %get-tuple-element.53), channel_id=1, source_target_pairs={{0,1},{1,2},{2,3},{3,4},{4,5},{5,6},{6,7},{7,8},{8,9},{9,10},{10,1... | collective-permute-start | bytes 417800 | tf_op jit(solution)/shard_map/ppermute | solution.py:57
  180.8 22.3 %collective-permute-start.10 = (f32[4,136,64]{2,1,0:T(8,128)S(1)}, f32[4,136,64]{2,1,0:T(8,128)}, u32[]{:S(2)}, u32[]{:S(2)}) collective-permute-start(f32[4,136,64]{2,1,0:T(8,128)S(1)} %get-tuple-element.54), channel_id=1, source_target_pairs={{1,0},{2,1},{3,2},{4,3},{5,4},{6,5},{7,6},{8,7},{9,8},{10,9},{11,1... | collective-permute-start | bytes 417800 | tf_op jit(solution)/shard_map/ppermute | solution.py:62
  187.2 11.7 %all-to-all-start.7 = ((f32[8,16,128]{2,1,0:T(8,128)}), f32[8,16,128]{2,1,0:T(8,128)S(1)}, u32[]{:S(2)}, u32[]{:S(2)}) async-start(f32[8,16,128]{2,1,0:T(8,128)} %broadcast_in_dim.18), calls=%async_computation.7 | async-start | bytes 131072 | tf_op jit(solution)/shard_map/all_to_all | solution.py:43
  198.8 40.6 %all-to-all-start.3 = ((f32[8,24,16,128]{3,2,1,0:T(8,128)}), f32[8,24,16,128]{3,2,1,0:T(8,128)S(1)}, u32[]{:S(2)}, u32[]{:S(2)}) async-start(f32[8,24,16,128]{3,2,1,0:T(8,128)} %mix.1), calls=%async_computation.3 | async-start | bytes 3145728 | tf_op jit(solution)/shard_map/all_to_all | solution.py:37
  202.4 3.4 %copy-start.22 = (s32[64]{0:T(128)S(1)}, s32[64]{0:T(128)}, u32[]{:S(2)}) copy-start(s32[64]{0:T(128)} %copy-done.21) | copy-start | bytes 772
  202.4 4.4 %copy-start.20 = (s32[128]{0:T(128)S(1)}, s32[128]{0:T(128)}, u32[]{:S(2)}) copy-start(s32[128]{0:T(128)} %iota_add_fusion) | copy-start | bytes 1540
  202.4 0.7 copy-start.17
  203.2 1.2 copy-start.18
  239.5 8.3 %copy-start.19 = (f32[16,1,64]{2,1,0:T(1,128)S(1)}, f32[16,1,64]{2,1,0:T(1,128)}, u32[]{:S(2)}) copy-start(f32[16,1,64]{2,1,0:T(1,128)} %get-tuple-element.52) | copy-start | bytes 12292
  239.6 13.3 %collective-permute-start.7 = (f32[8,144,128]{2,1,0:T(8,128)S(1)}, f32[8,144,128]{2,1,0:T(8,128)S(1)}, u32[]{:S(2)}, u32[]{:S(2)}) collective-permute-start(f32[8,144,128]{2,1,0:T(8,128)S(1)} %pad_maximum_fusion.3), channel_id=1, source_target_pairs={{0,1},{1,2},{2,3},{3,4},{4,5},{5,6},{6,7},{7,8},{8,9},{9,10},{10,1... | collective-permute-start | bytes 1769480 | tf_op jit(solution)/shard_map/ppermute | solution.py:57
  241.5 13.4 %copy-start.4 = (f32[8,16,1024]{2,1,0:T(8,128)S(1)}, f32[8,16,1024]{2,1,0:T(8,128)}, u32[]{:S(2)}) copy-start(f32[8,16,1024]{2,1,0:T(8,128)} %copy-done.3) | copy-start | bytes 1572868
  241.5 13.4 %copy-start.6 = (f32[8,16,1024]{2,1,0:T(8,128)S(1)}, f32[8,16,1024]{2,1,0:T(8,128)}, u32[]{:S(2)}) copy-start(f32[8,16,1024]{2,1,0:T(8,128)} %copy-done.5) | copy-start | bytes 1572868
  241.5 13.4 %copy-start.8 = (f32[8,16,1024]{2,1,0:T(8,128)S(1)}, f32[8,16,1024]{2,1,0:T(8,128)}, u32[]{:S(2)}) copy-start(f32[8,16,1024]{2,1,0:T(8,128)} %copy-done.7) | copy-start | bytes 1572868
  241.5 13.3 %copy-start.10 = (f32[8,16,1024]{2,1,0:T(8,128)S(1)}, f32[8,16,1024]{2,1,0:T(8,128)}, u32[]{:S(2)}) copy-start(f32[8,16,1024]{2,1,0:T(8,128)} %copy-done.9) | copy-start | bytes 1572868
  241.6 13.3 %copy-start.16 = (f32[16]{0:T(128)S(1)}, f32[16]{0:T(128)}, u32[]{:S(2)}) copy-start(f32[16]{0:T(128)} %copy-done.15) | copy-start | bytes 196
  241.6 13.3 %collective-permute-start.8 = (f32[8,144,128]{2,1,0:T(8,128)S(1)}, f32[8,144,128]{2,1,0:T(8,128)S(1)}, u32[]{:S(2)}, u32[]{:S(2)}) collective-permute-start(f32[8,144,128]{2,1,0:T(8,128)S(1)} %pad_maximum_fusion.4), channel_id=1, source_target_pairs={{1,0},{2,1},{3,2},{4,3},{5,4},{6,5},{7,6},{8,7},{9,8},{10,9},{11,1... | collective-permute-start | bytes 1769480 | tf_op jit(solution)/shard_map/ppermute | solution.py:62
where the time goes:
time: 276 us; the launch traced here: 274 us
  waiting for transfers between devices  116 us (42%)
  starting transfers between devices  81.6 us (30%)
  Pallas kernels  31.6 us (11%)
  blocking collectives  14.3 us (5%)
  local copies, waits for them, and re-layouts  13.6 us (5%)
  other arithmetic  10.5 us (4%)
  matrix products  5.28 us (2%)
    all_to_all x4, waiting for transfers between devices, exchanged(): return lax.all_to_all(blocks, 'ens', 0, 0, tiled=False)  77.2 us
    all_to_all x4, starting transfers between devices, gathered(): return lax.all_to_all(copies, axis, 0, 0, tiled=False)  33.8 us
    pallas_call x6, Pallas kernels, kernel_call(): pl.pallas_call(body, out_shape=[jax.ShapeDtypeStruct(o, jnp.float32) for...  26.2 us
    ppermute x3, starting transfers between devices, from_below(): lax.ppermute(rows_sent, 'space', [(i + 1, i) for i in range(count - 1)])  16.1 us
    all_to_all x1, blocking collectives, gathered(): return lax.all_to_all(copies, axis, 0, 0, tiled=False)  14.3 us
    all_to_all x4, starting transfers between devices, exchanged(): return lax.all_to_all(blocks, 'ens', 0, 0, tiled=False)  14.2 us
    ppermute x5, waiting for transfers between devices, summed(): lax.ppermute(block, axis, [(i, i ^ distance) for i in range(count)])  12.3 us
    ppermute x5, starting transfers between devices, summed(): lax.ppermute(block, axis, [(i, i ^ distance) for i in range(count)])  11.6 us
  transfers between devices with their start and end apart: 19, of which 15 were waited for; matrix products, arithmetic and copies ran while one was open for 7% of the time, Pallas kernels for 7%

commit v1 on v0

--- a/solution.py
+++ b/solution.py
@@ -15,22 +15,29 @@
 STATE_EDGE = ((0, 4), (1, 3), (2, 3))
 ADJOINT_EDGE = ((0, 4), (2, 3), (1, 2))
 VMEM = pl.BlockSpec(memory_space=pltpu.VMEM)
+HBM = pl.BlockSpec(memory_space=pltpu.HBM)
 SMEM = pl.BlockSpec(memory_space=pltpu.SMEM)
 
 
-def kernel_call(body, outs, ins, scratch=(), flops=0, name=None):
+def kernel_call(body, outs, ins, scratch=(), copies=0, far_outs=(), far_ins=(), flops=0, name=None):
     moved = sum(math.prod(o) for o in outs) * 4 + sum(i.size for i in ins) * 4
-    result = pl.pallas_call(
+    near = lambda i, a: SMEM if a.ndim == 1 else HBM if i in far_ins else VMEM
+    made = lambda i, o: (pltpu.HBM if i in far_outs else jax.ShapeDtypeStruct)(o, jnp.float32)
+    ins = [
+        pltpu.with_memory_space_constraint(a, pltpu.HBM) if i in far_ins else a
+        for i, a in enumerate(ins)
+    ]
+    return pl.pallas_call(
         body,
-        out_shape=[jax.ShapeDtypeStruct(o, jnp.float32) for o in outs],
-        in_specs=[SMEM if i.ndim == 1 else VMEM for i in ins],
-        out_specs=[VMEM] * len(outs),
-        scratch_shapes=[pltpu.VMEM(s, jnp.float32) for s in scratch],
-        compiler_params=pltpu.CompilerParams(vmem_limit_bytes=40 * 2**20),
+        out_shape=[made(i, o) for i, o in enumerate(outs)],
+        in_specs=[near(i, a) for i, a in enumerate(ins)],
+        out_specs=[HBM if i in far_outs else VMEM for i in range(len(outs))],
+        scratch_shapes=[pltpu.VMEM(s, jnp.float32) for s in scratch]
+        + ([pltpu.SemaphoreType.DMA((copies,))] if copies else []),
+        compiler_params=pltpu.CompilerParams(vmem_limit_bytes=20 * 2**20),
         cost_estimate=pl.CostEstimate(flops=flops, bytes_accessed=moved, transcendentals=0),
         name=name,
     )(*ins)
-    return result
 
 
 def exchanged(blocks):
@@ -41,6 +48,11 @@
     count = lax.axis_size(axis)
     copies = jnp.broadcast_to(block[None], (count,) + block.shape)
     return lax.all_to_all(copies, axis, 0, 0, tiled=False)
+
+
+def turned(block, distance):
+    count = lax.axis_size("ens")
+    return lax.ppermute(block, "ens", [(i, (i + distance) % count) for i in range(count)])
 
 
 def summed(block, axis):
@@ -73,21 +85,43 @@
     )
 
 
-def spread_kernel(in_ref, out_ref):
-    out_ref[0] = in_ref[...]
-
-
-def by_columns(field_rows, groups):
-    n, width = field_rows.shape
-    part = width // groups
-    return pl.pallas_call(
-        spread_kernel,
-        grid=(groups,),
-        out_shape=jax.ShapeDtypeStruct((groups, n, part), jnp.float32),
-        in_specs=[pl.BlockSpec((n, part), lambda j: (0, j))],
-        out_specs=pl.BlockSpec((1, n, part), lambda j: (j, 0, 0)),
-        name="spread",
-    )(field_rows)
+def prepare_kernel(
+    state_ref, depth_ref, cot_ref, tail_ref, head_ref, out_ref, tail, head, cot, spread, sems
+):
+    own = state_ref.shape[1]
+    groups, sites, part = spread.shape
+    copies = []
+
+    def send(source, target):
+        copies.append(pltpu.make_async_copy(source, target, sems.at[len(copies)]))
+        copies[-1].start()
+
+    fields = len(STATE_EDGE)
+    piece = sites // fields
+    at = 0
+    for f, n in STATE_EDGE:
+        send(state_ref.at[f, pl.ds(own - n, n)], tail.at[pl.ds(at, n)])
+        send(state_ref.at[f, pl.ds(0, n)], head.at[pl.ds(at, n)])
+        at += n
+    for edge in (tail, head):
+        send(depth_ref, edge.at[at, pl.ds(0, own)])
+    for f in range(fields):
+        send(cot_ref.at[pl.ds(f * piece, piece)], cot.at[pl.ds(f * piece, piece)])
+    for copy in copies[: 2 * fields + 2]:
+        copy.wait()
+    tail[at, own:] = tail[at, :own]
+    head[at, own:] = head[at, :own]
+    send(tail, tail_ref)
+    send(head, head_ref)
+    for f in range(fields):
+        copies[2 * fields + 2 + f].wait()
+        for j in range(groups):
+            spread[j, f * piece : (f + 1) * piece] = cot[
+                f * piece : (f + 1) * piece, j * part : (j + 1) * part
+            ]
+        send(spread.at[:, pl.ds(f * piece, piece)], out_ref.at[:, pl.ds(f * piece, piece)])
+    for copy in copies[3 * fields + 2 :]:
+        copy.wait()
 
 
 def padded_rows(edges, size, own_row, above, below):
@@ -109,25 +143,25 @@
 
 
 def forward_kernel(
-    inside_ref, state_ref, depth_ref, above_ref, below_ref,
-    spread_ref, height_ref, east1_ref, north1_ref, east2_ref, north2_ref,
-    e1, n1, h1, n2, depth,
+    inside_ref, state_ref, depth_ref, above_ref, below_ref, index_ref,
+    out_ref, observed_ref, east1_ref, north1_ref, east2_ref, north2_ref,
+    e1, n1, h1, n2, h2, e2, depth, spread, sems,
 ):
-    own, size, width = height_ref.shape
-    groups = spread_ref.shape[0]
+    own, size, width = east1_ref.shape
+    groups = spread.shape[0]
     part = width // groups
     low, high = HALO, HALO + own
     row, at = padded_rows(
         STATE_EDGE,
-        size,
+        1,
         lambda f, r: state_ref[f, r],
-        lambda i: above_ref[i : i + size],
-        lambda i: below_ref[i : i + size],
+        lambda i: above_ref[i],
+        lambda i: below_ref[i],
     )
     row = functools.partial(row, own_rows=own)
-    depth[:HALO] = above_ref[at : at + HALO]
+    depth[:HALO] = above_ref[at, own - HALO : own]
     depth[low:high] = depth_ref[...]
-    depth[high:] = below_ref[at : at + HALO]
+    depth[high:] = below_ref[at, :HALO]
 
     def d(p):
         return depth[p : p + 1]
@@ -139,6 +173,14 @@
         e1[p] = new_east
         flow = cols(d(p) * new_east) + (d(p + 1) * n1[p + 1] - d(p - 1) * n1[p - 1])
         h1[p] = (row(0, p) - WAVE_COEF * flow) * inside_ref[p]
+    copies = []
+
+    def send(source, target):
+        copies.append(pltpu.make_async_copy(source, target, sems.at[len(copies)]))
+        copies[-1].start()
+
+    send(e1.at[pl.ds(low, own)], east1_ref)
+    send(n1.at[pl.ds(low, own)], north1_ref)
     for p in range(low - 1, high + 1):
         n2[p] = n1[p] - WAVE_COEF * (h1[p + 1] - h1[p - 1]) - SPIN_COEF * e1[p]
     for p in range(low, high):
@@ -147,14 +189,30 @@
         flow = cols(d(p) * new_east) + (d(p + 1) * n2[p + 1] - d(p - 1) * n2[p - 1])
         new_height = h1[p] - WAVE_COEF * flow
         new_north = n2[p]
-        height_ref[r] = new_height
-        east1_ref[r] = e1[p]
-        north1_ref[r] = n1[p]
-        east2_ref[r] = new_east
-        north2_ref[r] = new_north
+        h2[r] = new_height
+        e2[r] = new_east
         for f, field in enumerate((new_height, new_east, new_north)):
             for j in range(groups):
-                spread_ref[j, f * own + r] = field[:, j * part : (j + 1) * part]
+                spread[j, f * own + r] = field[:, j * part : (j + 1) * part]
+    send(spread, out_ref)
+    send(e2, east2_ref)
+    send(n2.at[pl.ds(low, own)], north2_ref)
+    pairs, lanes = index_ref.shape
+    many = 2 * groups * size
+    sub = lax.broadcasted_iota(jnp.int32, (part, lanes), 0)
+    source = lax.broadcasted_iota(jnp.int32, (many, lanes), 0) // size
+    target = lax.broadcasted_iota(jnp.int32, (many, lanes), 1) // (lanes // 2 // groups)
+    for q in range(pairs):
+        index = index_ref[q : q + 1].astype(jnp.int32)
+        hit = (sub == index).astype(jnp.float32)
+        stacked = jnp.concatenate(
+            [h2[q + h * pairs, :, j * part : (j + 1) * part] for h in range(2) for j in range(groups)],
+            axis=0,
+        )
+        seen = jnp.where(source == target, dot(stacked, hit), 0.0)
+        observed_ref[q] = seen.reshape(2 * groups, size, lanes).sum(0)
+    for copy in copies:
+        copy.wait()
 
 
 def backward_kernel(
@@ -213,8 +271,16 @@
         state_grad_ref[2, r] = nt[p] + SPIN_COEF * total
 
 
-def gram_kernel(observed_ref, params_ref, scaled_ref, extra_ref, gram_ref):
+def gram_kernel(place_ref, params_ref, *refs):
+    *observed_refs, scaled_ref, extra_ref, gram_ref, observed_ref, sems = refs
     groups, pairs, size, lanes = observed_ref.shape
+    copies = []
+    for d, ref in enumerate(observed_refs):
+        there = observed_ref.at[lax.rem(place_ref[0] + groups - d, groups)]
+        copies.append(pltpu.make_async_copy(ref, there, sems.at[d]))
+        copies[-1].start()
+    for copy in copies:
+        copy.wait()
     members = groups * size
     gram = jnp.zeros((members, members), jnp.float32)
     proj = jnp.zeros((8, members), jnp.float32)
@@ -275,6 +341,73 @@
     mixing_ref[...] = turned.T
 
 
+def pullback_kernel(place_ref, cross_ref, inverse_ref, mean_ref, *refs):
+    *parts, grad, column = refs
+    members = inverse_ref.shape[0]
+    groups = len(parts)
+    size = members // groups
+    inverse = inverse_ref[...]
+    cross = cross_ref[...]
+    cross = cross - jnp.mean(cross, axis=0, keepdims=True)
+    first = lax.broadcasted_iota(jnp.int32, (8, members), 0) == 0
+    ones = jnp.where(first, 1.0, 0.0)
+    mean_grad = dot(ones, cross, ((1,), (1,))) / math.sqrt(members - 1)
+    proj_grad = dot(dot(mean_grad, inverse, ((1,), (1,))), inverse)
+    product = dot(inverse, cross)
+    row = lax.broadcasted_iota(jnp.int32, (members, members), 0)
+    col = lax.broadcasted_iota(jnp.int32, (members, members), 1)
+    upper = jnp.where(row < col, product, 0.0)
+    mirrored = jnp.where(row == col, product, 0.0) + upper + upper.T
+    inner_grad = dot(inverse.T, dot(mirrored, inverse))
+    every = jnp.broadcast_to(proj_grad[:1], (members, members)).T
+    outer = every * mean_ref[:1]
+    gram_grad = -(inner_grad + outer + outer.T)
+    grad[...] = gram_grad - jnp.mean(gram_grad, axis=0, keepdims=True)
+    column[...] = every - jnp.mean(every, axis=0, keepdims=True)
+    for d, part in enumerate(parts):
+        there = lax.rem(place_ref[0] + d, groups)
+        rows_there = pl.ds(pl.multiple_of(there * size, size), size)
+        part[:size] = grad[rows_there]
+        part[size : 2 * size] = column[rows_there]
+        part[2 * size :] = proj_grad
+
+
+def observe_kernel(*refs):
+    *part_refs, obs_ref, seen_ref, parts, sems = refs
+    tall, size, width = seen_ref.shape
+    pairs, high, lanes = obs_ref.shape
+    members = high - 8
+    part = lanes
+    groups = width // part
+    copies = []
+    for d, ref in enumerate(part_refs):
+        copies.append(pltpu.make_async_copy(ref, parts.at[d], sems.at[d]))
+        copies[-1].start()
+    for copy in copies:
+        copy.wait()
+    whole = parts[...].sum(0)
+    own_grad, own_proj, proj_grad = whole[:size], whole[size : 2 * size], whole[2 * size :]
+    lane = lax.broadcasted_iota(jnp.int32, (size, lanes), 1)
+    sub = lax.broadcasted_iota(jnp.int32, (part, lanes), 0)
+    block = lanes // 2 // groups
+    for t in range(pairs):
+        scaled = obs_ref[t, :members]
+        innovation, obs_scale, inv_sd, index = (
+            obs_ref[t, members + i : members + i + 1] for i in range(4)
+        )
+        obs_grad = (dot(own_grad, scaled) + own_proj * innovation) * obs_scale
+        obs_grad = obs_grad - dot(proj_grad, scaled)[:1] * inv_sd / members
+        apart = jnp.concatenate(
+            [jnp.where(lane // block == i, obs_grad, 0.0) for i in range(2 * groups)], axis=0
+        )
+        hit = (sub == index.astype(jnp.int32)).astype(jnp.float32)
+        put = dot(apart, hit, ((1,), (1,)))
+        for h in range(2):
+            for j in range(groups):
+                at = (h * groups + j) * size
+                seen_ref[t + h * pairs, :, j * part : (j + 1) * part] = put[at : at + size]
+
+
 def cross_kernel(state_ref, cot_ref, out_ref):
     groups, sites, size, part = state_ref.shape
     members = groups * size
@@ -287,17 +420,29 @@
     out_ref[...] = total
 
 
-def mix_kernel(mixing_ref, cot_ref, out_ref):
+def mix_kernel(mixing_ref, cot_ref, out_ref, mixed_ref, sems):
     groups, sites, size, part = cot_ref.shape
     members = groups * size
     mixing = mixing_ref[...]
+    copies = []
+    pieces = sems.shape[0]
     for at in range(0, sites, 2):
         both = jnp.concatenate(
             [cot_ref[:, at + i].reshape(members, part) for i in range(2)], axis=1
         )
         mixed = dot(mixing, both)
         for i in range(2):
-            out_ref[:, at + i] = mixed[:, i * part : (i + 1) * part].reshape(groups, size, part)
+            mixed_ref[:, at + i] = mixed[:, i * part : (i + 1) * part].reshape(groups, size, part)
+        if (at + 2) % (sites // pieces) == 0:
+            done = pl.ds(at + 2 - sites // pieces, sites // pieces)
+            copies.append(
+                pltpu.make_async_copy(
+                    mixed_ref.at[:, done], out_ref.at[:, done], sems.at[len(copies)]
+                )
+            )
+            copies[-1].start()
+    for copy in copies:
+        copy.wait()
 
 
 def per_device(initial_state, depth_field, obs_index, obs_value, obs_var, cotangent):
@@ -312,60 +457,58 @@
     sites = fields * own_rows
     half = own_rows // 2
 
-    def edge(take):
-        parts = [initial_state[f, take(n)].reshape(-1, width) for f, n in STATE_EDGE]
-        return jnp.concatenate(parts + [depth_field[take(HALO)]])
-
-    tail = edge(lambda n: slice(own_rows - n, own_rows))
-    head = edge(lambda n: slice(0, n))
+    packed = jnp.concatenate([obs_index.T.astype(jnp.float32), obs_value.T, obs_var.T])
+    packed = jnp.pad(packed, ((0, 0), (0, block_cols - packed.shape[1])))
+    params = gathered(packed, "ens")
+    edge = (sum(n for _, n in STATE_EDGE) + 1, own_members, width)
+    blocks = (groups, sites * own_members, block_cols)
+    tail, head, cot_out = kernel_call(
+        prepare_kernel,
+        [edge, edge, blocks],
+        [initial_state, depth_field, cotangent.reshape(-1, width)],
+        [edge, edge, (sites * own_members, width), blocks],
+        copies=4 * fields + 4,
+        far_outs=(0, 1, 2),
+        far_ins=(0, 1, 2),
+        name="prepare",
+    )
     above, below = from_above(tail), from_below(head)
-    cot_in, _, _ = lax.optimization_barrier((cotangent, tail, head))
-    cot_out = by_columns(cot_in.reshape(-1, width), groups)
+    cot_out, params = lax.optimization_barrier((cot_out, params))
     cot = exchanged(cot_out).reshape(groups, sites, own_members, block_cols)
-
-    packed = jnp.stack([obs_index.astype(jnp.float32), obs_value, obs_var])
-    params = gathered(packed, "ens").transpose(1, 2, 0, 3).reshape(3, own_rows, -1)
-    observations = params.shape[2]
+    per_block = obs_index.shape[1]
+    observations = per_block * groups
+    params = params[:, :, :own_rows].reshape(groups, 3, per_block, 2, half)
+    params = params.transpose(1, 4, 3, 0, 2).reshape(3, half, 2 * observations)
 
     row_number = space_place * own_rows - HALO + jnp.arange(tall)
     inside = ((row_number >= 0) & (row_number < band)).astype(jnp.float32)
     shape = (own_rows, own_members, width)
     padded = (tall, own_members, width)
-    spread, height, east1, north1, east2, north2 = kernel_call(
+    spread, observed, east1, north1, east2, north2 = kernel_call(
         forward_kernel,
-        [(groups, sites, own_members, block_cols)] + [shape] * 5,
-        [inside, initial_state, depth_field, above, below],
-        [padded] * 4 + [(tall, width)],
+        [(groups, sites, own_members, block_cols), (half, own_members, 2 * observations)]
+        + [shape] * 4,
+        [inside, initial_state, depth_field, above, below, params[0]],
+        [padded] * 4 + [shape, shape, (tall, width), (groups, sites, own_members, block_cols)],
+        copies=5,
+        far_outs=(0, 2, 3, 4, 5),
         flops=10**8,
         name="forward",
     )
-
-    def selector(index_rows):
-        n = index_rows.shape[0]
-        offset = (jnp.arange(observations) // (observations // groups)) * block_cols
-        place = index_rows.astype(jnp.int32) + offset[None]
-        return (
-            place[:, :, None] == lax.broadcasted_iota(jnp.int32, (n, observations, width), 2)
-        ).astype(jnp.float32)
-
-    def paired(a):
-        return jnp.concatenate([a[..., :half, :, :], a[..., half:, :, :]], axis=-1)
-
-    def unpaired(a):
-        return jnp.concatenate([a[..., :observations], a[..., observations:]], axis=0)
-
-    observed = jnp.einsum("rmc,roc->rmo", height, selector(params[0]), precision=HIGHEST)
-    observed = gathered(paired(observed), "ens")
-    spread, _ = lax.optimization_barrier((spread, observed))
-    forecast = exchanged(spread)
-    params_paired = jnp.concatenate([params[:, :half], params[:, half:]], axis=-1)
+    observed = [observed] + [turned(observed, d) for d in range(1, groups)]
+    place = ens_place.astype(jnp.int32)[None]
     scaled, extra, gram = kernel_call(
         gram_kernel,
         [(half, members, 2 * observations), (half, 8, 2 * observations), (members + 8, members)],
-        [observed, params_paired],
+        [place, params] + observed,
+        [(groups,) + observed[0].shape],
+        copies=groups,
+        far_ins=tuple(range(2, 2 + groups)),
         flops=4 * 2 * 6 * members**3,
         name="gram",
     )
+    spread, gram = lax.optimization_barrier((spread, gram))
+    forecast = exchanged(spread)
     gram = summed(gram, "space")
     inverse, mixing, mean_weights = kernel_call(
         factor_kernel,
@@ -374,53 +517,53 @@
         flops=10**9,
         name="factor",
     )
-    mean_weights = mean_weights[0]
     scaled, extra, _ = lax.optimization_barrier((scaled, extra, gram))
-    obs_pack = unpaired(jnp.concatenate([scaled, extra], axis=1))
+    obs_pack = jnp.concatenate([scaled, extra], axis=1)
+    left, right = obs_pack[..., :observations], obs_pack[..., observations:]
     obs_tall = jnp.concatenate(
-        [from_above(obs_pack[own_rows - HALO :]), obs_pack, from_below(obs_pack[:HALO])]
+        [
+            jnp.concatenate([from_above(right), right], axis=-1),
+            jnp.concatenate([left, from_below(left)], axis=-1),
+        ]
     )
 
     (own_cross,) = kernel_call(
         cross_kernel, [(members, members)], [forecast, cot], flops=10**10, name="cross"
     )
+    mixing, obs_tall = lax.optimization_barrier((mixing, obs_tall))
     (mixed,) = kernel_call(
-        mix_kernel, [cot.shape], [mixing, cot], flops=10**10, name="mix"
-    )
+        mix_kernel,
+        [cot.shape],
+        [mixing, cot],
+        [cot.shape],
+        copies=fields,
+        far_outs=(0,),
+        flops=10**10,
+        name="mix",
+    )
+    mixed, own_cross = lax.optimization_barrier((mixed, own_cross))
     back = exchanged(mixed)
 
-    cross = jnp.sum(exchanged(own_cross.reshape(groups, own_members, members)), axis=0)
-    cross = jnp.sum(gathered(cross, "space"), axis=0)
-    cross = gathered(cross, "ens").reshape(members, members)
-    cross = cross - jnp.mean(cross, axis=0, keepdims=True)
-    identity = jnp.eye(members, dtype=jnp.float32)
-    mean_grad = jnp.sum(cross, axis=1) / math.sqrt(members - 1)
-    proj_grad = jnp.dot(
-        inverse.T, jnp.dot(inverse, mean_grad, precision=HIGHEST), precision=HIGHEST
-    )
-    product = jnp.dot(cross.T, inverse.T, precision=HIGHEST)
-    strict = jnp.tril(product, -1)
-    mirrored = strict + strict.T + identity * product
-    inner_grad = jnp.dot(
-        inverse.T, jnp.dot(mirrored, inverse, precision=HIGHEST), precision=HIGHEST
-    )
-    outer = proj_grad[:, None] * mean_weights[None, :]
-    gram_grad = -(inner_grad + outer + outer.T)
-    both = jnp.concatenate([gram_grad, proj_grad[:, None]], axis=1)
-    both = both - jnp.mean(both, axis=0, keepdims=True)
-    own_both = lax.dynamic_slice_in_dim(both, ens_place * own_members, own_members, 0)
-
-    obs_grad = jnp.einsum(
-        "km,rmo->rko", own_both, obs_tall[:, : members + 1], precision=HIGHEST
-    )
-    innov_grad = jnp.einsum("m,rmo->ro", proj_grad, obs_tall[:, :members], precision=HIGHEST)
-    obs_grad = (
-        obs_grad * obs_tall[:, members + 1][:, None, :]
-        - (innov_grad * obs_tall[:, members + 2] / members)[:, None, :]
-    )
-    seen = jnp.einsum(
-        "rko,roc->rkc", obs_grad, selector(obs_tall[:, members + 3]), precision=HIGHEST
-    )
+    parts = kernel_call(
+        pullback_kernel,
+        [(2 * own_members + 8, members)] * groups,
+        [place, summed(own_cross, "space"), inverse, mean_weights],
+        [(members, members)] * 2,
+        flops=10**9,
+        name="pullback",
+    )
+    parts = [parts[0]] + [turned(parts[d], d) for d in range(1, groups)]
+    (seen,) = kernel_call(
+        observe_kernel,
+        [padded],
+        parts + [obs_tall],
+        [(groups,) + parts[0].shape],
+        copies=groups,
+        far_ins=tuple(range(groups)),
+        flops=10**9,
+        name="observe",
+    )
+    back, parts = lax.optimization_barrier((back, parts))
 
     by_field = back.reshape(groups, fields, own_rows, own_members, block_cols)
 
@@ -432,7 +575,7 @@
 
     adjoint_above = from_above(adjoint_edge(lambda n: slice(own_rows - n, own_rows)))
     adjoint_below = from_below(adjoint_edge(lambda n: slice(0, n)))
-    depth_tall = jnp.concatenate([above[-HALO:], depth_field, below[-HALO:]])
+    depth_tall = jnp.concatenate([above[-1, half:own_rows], depth_field, below[-1, :half]])
     depth_grad, state_grad = kernel_call(
         backward_kernel,
         [(own_rows, width), (fields,) + shape],

time: 276 us -> 211 us (0.76)
  waiting for transfers between devices: 116 us -> 61.2 us
  local copies, waits for them, and re-layouts: 13.6 us -> 4.02 us
  starting transfers between devices: 81.6 us -> 90.3 us
  other arithmetic: 10.5 us -> 3.32 us
  matrix products: 5.28 us -> 0 us
  Pallas kernels: 31.6 us -> 34.8 us
    all_to_all x4 -> x3, waiting for transfers between devices: 77.2 us -> 0.01 us  [exchanged(): return lax.all_to_all(blocks, 'ens', 0, 0, tiled=False)]
    ppermute x0 -> x14, starting transfers between devices: none -> 32 us  [turned(): lax.ppermute(block, 'ens', [(i, (i + distance) % count) for i in range(co...]
    all_to_all x4 -> x1, starting transfers between devices: 33.8 us -> 8.47 us  [gathered(): return lax.all_to_all(copies, axis, 0, 0, tiled=False)]
    ppermute x5 -> x10, waiting for transfers between devices: 12.3 us -> 34.6 us  [summed(): lax.ppermute(block, axis, [(i, i ^ distance) for i in range(count)])]
    ppermute x0 -> x14, waiting for transfers between devices: none -> 9.94 us  [turned(): lax.ppermute(block, 'ens', [(i, (i + distance) % count) for i in range(co...]
    all_to_all x4 -> x1, waiting for transfers between devices: 10.8 us -> 5.41 us  [gathered(): return lax.all_to_all(copies, axis, 0, 0, tiled=False)]
    dot_general x9 -> x0, matrix products: 5.28 us -> none  [the longest x1 1.48 us: per_device(): jnp.einsum('rko,roc->rkc', obs_grad, selector(obs_tall[:, members + 3]),...]
    unnamed x49 -> x48, local copies, waits for them, and re-layouts: 6.38 us -> 1.12 us
  transfers between devices with their start and end apart: 19 -> 34, of which waited for: 15 -> 18; matrix products, arithmetic and copies ran while one was open for 7% -> 2% of each run, Pallas kernels for 7% -> 14%
where the time goes in v1:
time: 211 us; the launch traced here: 210 us
  starting transfers between devices  90.3 us (43%)
  waiting for transfers between devices  61.2 us (29%)
  Pallas kernels  34.8 us (16%)
  blocking collectives  15.4 us (7%)
  local copies, waits for them, and re-layouts  4.02 us (2%)
  other arithmetic  3.32 us (2%)
    pallas_call x9, Pallas kernels, kernel_call(): pl.pallas_call(body, out_shape=[made(i, o) for i, o in enumerate(outs)],...  34.8 us
    ppermute x10, waiting for transfers between devices, summed(): lax.ppermute(block, axis, [(i, i ^ distance) for i in range(count)])  34.6 us
    ppermute x14, starting transfers between devices, turned(): lax.ppermute(block, 'ens', [(i, (i + distance) % count) for i in range(co...  32 us
    ppermute x3, starting transfers between devices, from_below(): lax.ppermute(rows_sent, 'space', [(i + 1, i) for i in range(count - 1)])  17.3 us
    all_to_all x3, starting transfers between devices, exchanged(): return lax.all_to_all(blocks, 'ens', 0, 0, tiled=False)  16.9 us
    all_to_all x1, blocking collectives, gathered(): return lax.all_to_all(copies, axis, 0, 0, tiled=False)  15.4 us
    ppermute x14, waiting for transfers between devices, turned(): lax.ppermute(block, 'ens', [(i, (i + distance) % count) for i in range(co...  9.94 us
    ppermute x10, starting transfers between devices, summed(): lax.ppermute(block, axis, [(i, i ^ distance) for i in range(count)])  9.9 us
  transfers between devices with their start and end apart: 34, of which 18 were waited for; matrix products, arithmetic and copies ran while one was open for 2% of the time, Pallas kernels for 14%

profile of v1, /device:TPU:6, one launch (start us, length us, event | category | flops | bytes accessed | tf_op | source)
XLA Modules:
  0.0 210.2 jit_solution(1222123492777382768)
XLA Ops:
  2.8 8.5 %all-to-all-start = ((f32[8,24,128]{2,1,0:T(8,128)}), f32[8,24,128]{2,1,0:T(8,128)S(1)}, u32[]{:S(2)}, u32[]{:S(2)}) async-start(f32[8,24,128]{2,1,0:T(8,128)} %broadcast_in_dim.6), calls=%async_computation | async-start | bytes 196608 | tf_op jit(solution)/shard_map/all_to_all | solution.py:50
  11.3 3.3 %prepare.1 = (f32[11,16,1024]{2,1,0:T(8,128)}, f32[11,16,1024]{2,1,0:T(8,128)}, f32[8,384,128]{2,1,0:T(8,128)}) custom-call(f32[3,8,16,1024]{3,2,1,0:T(8,128)} %state_ref.3, f32[8,1024]{1,0:T(8,128)} %depth_ref.3, f32[384,1024]{1,0:T(8,128)} %bitcast.43), custom_call_target="tpu_custom_call" | custom-call | bytes 6193152 | tf_op jit(solution)/shard_map/prepare/pallas_call | solution.py:30
  14.6 5.4 %all-to-all-done = f32[8,24,128]{2,1,0:T(8,128)S(1)} async-done(((f32[8,24,128]{2,1,0:T(8,128)}), f32[8,24,128]{2,1,0:T(8,128)S(1)}, u32[]{:S(2)}, u32[]{:S(2)}) %all-to-all-start) | async-done | bytes 98336 | tf_op jit(solution)/shard_map/all_to_all | solution.py:50
  20.0 3.7 %all-to-all-start.1 = ((f32[8,384,128]{2,1,0:T(8,128)}), f32[8,384,128]{2,1,0:T(8,128)S(1)}, u32[]{:S(2)}, u32[]{:S(2)}) async-start(f32[8,384,128]{2,1,0:T(8,128)} %get-tuple-element.52), calls=%async_computation.1 | async-start | bytes 3145728 | tf_op jit(solution)/shard_map/all_to_all | solution.py:44
  23.7 1.9 collective-permute-start
  25.7 5.8 %collective-permute-start.1 = (f32[11,16,1024]{2,1,0:T(8,128)}, f32[11,16,1024]{2,1,0:T(8,128)}, u32[]{:S(2)}, u32[]{:S(2)}) collective-permute-start(f32[11,16,1024]{2,1,0:T(8,128)} %get-tuple-element.39), channel_id=1, source_target_pairs={{1,0},{2,1},{3,2},{4,3},{5,4},{6,5},{7,6},{8,7},{9,8},{10,9},{11,1... | collective-permute-start | bytes 2162696 | tf_op jit(solution)/shard_map/ppermute | solution.py:74
  31.8 7.0 %collective-permute-done.above_ref = f32[11,16,1024]{2,1,0:T(8,128)} collective-permute-done((f32[11,16,1024]{2,1,0:T(8,128)}, f32[11,16,1024]{2,1,0:T(8,128)}, u32[]{:S(2)}, u32[]{:S(2)}) %collective-permute-start) | collective-permute-done | bytes 720928 | tf_op jit(solution)/shard_map/ppermute | solution.py:69
  38.8 1.8 collective-permute-done.1.below_ref
  40.5 5.2 %forward.1 = (f32[8,24,16,128]{3,2,1,0:T(8,128)}, f32[4,16,128]{2,1,0:T(8,128)S(1)}, f32[8,16,1024]{2,1,0:T(8,128)}, f32[8,16,1024]{2,1,0:T(8,128)}, f32[8,16,1024]{2,1,0:T(8,128)}, /*index=5*/f32[8,16,1024]{2,1,0:T(8,128)}) custom-call(f32[16]{0:T(128)S(1)} %and_convert_fusion.inside_ref, f32[3,8,16,1024]{3,2,1,0:T(8,128)S(1)} %copy-done, ...), custom_call_target="tpu_custom_call" | custom-call | flops 100000000 | bytes 6752320 | tf_op jit(solution)/shard_map/forward/pallas_call | solution.py:30
  45.8 3.2 %collective-permute-start.8 = (f32[4,16,128]{2,1,0:T(8,128)S(1)}, f32[4,16,128]{2,1,0:T(8,128)S(1)}, u32[]{:S(2)}, u32[]{:S(2)}) collective-permute-start(f32[4,16,128]{2,1,0:T(8,128)S(1)} %get-tuple-element.43.refs_0_), channel_id=1, source_target_pairs={{0,224},{32,0},{64,32},{96,64},{128,96},{160,128},{192,160},{224,1... | collective-permute-start | bytes 98312 | tf_op jit(solution)/shard_map/ppermute | solution.py:55
  49.0 2.3 %collective-permute-start.7 = (f32[4,16,128]{2,1,0:T(8,128)S(1)}, f32[4,16,128]{2,1,0:T(8,128)S(1)}, u32[]{:S(2)}, u32[]{:S(2)}) collective-permute-start(f32[4,16,128]{2,1,0:T(8,128)S(1)} %get-tuple-element.43.refs_0_), channel_id=1, source_target_pairs={{0,192},{32,224},{64,0},{96,32},{128,64},{160,96},{192,128},{224,1... | collective-permute-start | bytes 98312 | tf_op jit(solution)/shard_map/ppermute | solution.py:55
  51.4 1.4 collective-permute-start.6
  52.8 3.6 %collective-permute-start.5 = (f32[4,16,128]{2,1,0:T(8,128)S(1)}, f32[4,16,128]{2,1,0:T(8,128)S(1)}, u32[]{:S(2)}, u32[]{:S(2)}) collective-permute-start(f32[4,16,128]{2,1,0:T(8,128)S(1)} %get-tuple-element.43.refs_0_), channel_id=1, source_target_pairs={{0,128},{32,160},{64,192},{96,224},{128,0},{160,32},{192,64},{224,... | collective-permute-start | bytes 98312 | tf_op jit(solution)/shard_map/ppermute | solution.py:55
  56.6 5.8 %collective-permute-done.8.refs_7_ = f32[4,16,128]{2,1,0:T(8,128)S(1)} collective-permute-done((f32[4,16,128]{2,1,0:T(8,128)S(1)}, f32[4,16,128]{2,1,0:T(8,128)S(1)}, u32[]{:S(2)}, u32[]{:S(2)}) %collective-permute-start.8) | collective-permute-done | bytes 32800 | tf_op jit(solution)/shard_map/ppermute | solution.py:55
  62.5 4.0 %collective-permute-start.2 = (f32[4,16,128]{2,1,0:T(8,128)S(1)}, f32[4,16,128]{2,1,0:T(8,128)S(1)}, u32[]{:S(2)}, u32[]{:S(2)}) collective-permute-start(f32[4,16,128]{2,1,0:T(8,128)S(1)} %get-tuple-element.43.refs_0_), channel_id=1, source_target_pairs={{0,32},{32,64},{64,96},{96,128},{128,160},{160,192},{192,224},{224... | collective-permute-start | bytes 98312 | tf_op jit(solution)/shard_map/ppermute | solution.py:55
  66.7 1.8 collective-permute-done.3.refs_2_
  69.1 2.0 gram.1
  71.1 5.9 %all-to-all-start.2 = ((f32[8,24,16,128]{3,2,1,0:T(8,128)}), f32[8,24,16,128]{3,2,1,0:T(8,128)S(1)}, u32[]{:S(2)}, u32[]{:S(2)}) async-start(f32[8,24,16,128]{3,2,1,0:T(8,128)} %get-tuple-element.53), calls=%async_computation.2 | async-start | bytes 3145728 | tf_op jit(solution)/shard_map/all_to_all | solution.py:44
  78.3 1.7 collective-permute-start.10
  80.0 2.7 %collective-permute-done.10 = f32[136,128]{1,0:T(8,128)S(1)} collective-permute-done((f32[136,128]{1,0:T(8,128)S(1)}, f32[136,128]{1,0:T(8,128)S(1)}, u32[]{:S(2)}, u32[]{:S(2)}) %collective-permute-start.10) | collective-permute-done | bytes 69664 | tf_op jit(solution)/shard_map/ppermute | solution.py:62
  82.7 3.3 %collective-permute-start.11 = (f32[136,128]{1,0:T(8,128)S(1)}, f32[136,128]{1,0:T(8,128)S(1)}, u32[]{:S(2)}, u32[]{:S(2)}) collective-permute-start(f32[136,128]{1,0:T(8,128)S(1)} %add.42), channel_id=1, source_target_pairs={{0,4},{1,5},{2,6},{3,7},{4,0},{5,1},{6,2},{7,3},{8,12},{9,13},{10,... | collective-permute-start | bytes 208904 | tf_op jit(solution)/shard_map/ppermute | solution.py:62
  86.0 2.6 %collective-permute-done.11 = f32[136,128]{1,0:T(8,128)S(1)} collective-permute-done((f32[136,128]{1,0:T(8,128)S(1)}, f32[136,128]{1,0:T(8,128)S(1)}, u32[]{:S(2)}, u32[]{:S(2)}) %collective-permute-start.11) | collective-permute-done | bytes 69664 | tf_op jit(solution)/shard_map/ppermute | solution.py:62
  89.6 3.8 %collective-permute-done.12 = f32[136,128]{1,0:T(8,128)S(1)} collective-permute-done((f32[136,128]{1,0:T(8,128)S(1)}, f32[136,128]{1,0:T(8,128)S(1)}, u32[]{:S(2)}, u32[]{:S(2)}) %collective-permute-start.12) | collective-permute-done | bytes 69664 | tf_op jit(solution)/shard_map/ppermute | solution.py:62
  94.7 4.7 %collective-permute-done.13 = f32[136,128]{1,0:T(8,128)S(1)} collective-permute-done((f32[136,128]{1,0:T(8,128)S(1)}, f32[136,128]{1,0:T(8,128)S(1)}, u32[]{:S(2)}, u32[]{:S(2)}) %collective-permute-start.13) | collective-permute-done | bytes 69664 | tf_op jit(solution)/shard_map/ppermute | solution.py:62
  99.6 1.9 collective-permute-start.14
  101.5 5.8 %collective-permute-start.15 = (f32[4,136,64]{2,1,0:T(8,128)S(1)}, f32[4,136,64]{2,1,0:T(8,128)S(1)}, u32[]{:S(2)}, u32[]{:S(2)}) collective-permute-start(f32[4,136,64]{2,1,0:T(8,128)S(1)} %get-tuple-element.81), channel_id=1, source_target_pairs={{1,0},{2,1},{3,2},{4,3},{5,4},{6,5},{7,6},{8,7},{9,8},{10,9},{11,1... | collective-permute-start | bytes 417800 | tf_op jit(solution)/shard_map/ppermute | solution.py:74
  107.3 11.4 %factor.1 = (f32[128,128]{1,0:T(8,128)S(1)}, f32[128,128]{1,0:T(8,128)S(1)}, f32[8,128]{1,0:T(8,128)S(1)}) custom-call(f32[136,128]{1,0:T(8,128)S(1)} %add.45.gram_ref), custom_call_target="tpu_custom_call" | custom-call | flops 1000000000 | bytes 204800 | tf_op jit(solution)/shard_map/factor/pallas_call | solution.py:30
  119.7 2.2 %mix.1 = f32[8,24,16,128]{3,2,1,0:T(8,128)} custom-call(f32[128,128]{1,0:T(8,128)S(1)} %get-tuple-element.51.mixing_ref, f32[8,24,16,128]{3,2,1,0:T(8,128)S(1)} %bitcast.41), custom_call_target="tpu_custom_call" | custom-call | flops 10000000000 | bytes 3211264 | tf_op jit(solution)/shard_map/mix/pallas_call | solution.py:30
  121.9 1.5 cross.1
  123.5 7.2 %all-to-all-start.3 = ((f32[8,24,16,128]{3,2,1,0:T(8,128)}), f32[8,24,16,128]{3,2,1,0:T(8,128)S(1)}, u32[]{:S(2)}, u32[]{:S(2)}) async-start(f32[8,24,16,128]{3,2,1,0:T(8,128)} %mix.1), calls=%async_computation.3 | async-start | bytes 3145728 | tf_op jit(solution)/shard_map/all_to_all | solution.py:44
  132.1 4.3 %collective-permute-done.17 = f32[128,128]{1,0:T(8,128)S(1)} collective-permute-done((f32[128,128]{1,0:T(8,128)S(1)}, f32[128,128]{1,0:T(8,128)S(1)}, u32[]{:S(2)}, u32[]{:S(2)}) %collective-permute-start.17) | collective-permute-done | bytes 65568 | tf_op jit(solution)/shard_map/ppermute | solution.py:62
  137.5 4.7 %collective-permute-done.18 = f32[128,128]{1,0:T(8,128)S(1)} collective-permute-done((f32[128,128]{1,0:T(8,128)S(1)}, f32[128,128]{1,0:T(8,128)S(1)}, u32[]{:S(2)}, u32[]{:S(2)}) %collective-permute-start.18) | collective-permute-done | bytes 65568 | tf_op jit(solution)/shard_map/ppermute | solution.py:62
  142.9 4.2 %collective-permute-done.19 = f32[128,128]{1,0:T(8,128)S(1)} collective-permute-done((f32[128,128]{1,0:T(8,128)S(1)}, f32[128,128]{1,0:T(8,128)S(1)}, u32[]{:S(2)}, u32[]{:S(2)}) %collective-permute-start.19) | collective-permute-done | bytes 65568 | tf_op jit(solution)/shard_map/ppermute | solution.py:62
  147.8 5.1 %collective-permute-done.20 = f32[128,128]{1,0:T(8,128)S(1)} collective-permute-done((f32[128,128]{1,0:T(8,128)S(1)}, f32[128,128]{1,0:T(8,128)S(1)}, u32[]{:S(2)}, u32[]{:S(2)}) %collective-permute-start.20) | collective-permute-done | bytes 65568 | tf_op jit(solution)/shard_map/ppermute | solution.py:62
  154.2 2.1 collective-permute-start.21
  156.3 2.2 %collective-permute-start.22 = (f32[40,128]{1,0:T(8,128)S(1)}, f32[40,128]{1,0:T(8,128)S(1)}, u32[]{:S(2)}, u32[]{:S(2)}) collective-permute-start(f32[40,128]{1,0:T(8,128)S(1)} %get-tuple-element.60), channel_id=1, source_target_pairs={{0,64},{32,96},{64,128},{96,160},{128,192},{160,224},{192,0},{224,... | collective-permute-start | bytes 61448 | tf_op jit(solution)/shard_map/ppermute | solution.py:55
  158.6 2.8 %collective-permute-start.23 = (f32[40,128]{1,0:T(8,128)S(1)}, f32[40,128]{1,0:T(8,128)S(1)}, u32[]{:S(2)}, u32[]{:S(2)}) collective-permute-start(f32[40,128]{1,0:T(8,128)S(1)} %get-tuple-element.61), channel_id=1, source_target_pairs={{0,96},{32,128},{64,160},{96,192},{128,224},{160,0},{192,32},{224,... | collective-permute-start | bytes 61448 | tf_op jit(solution)/shard_map/ppermute | solution.py:55
  161.4 2.4 %collective-permute-start.24 = (f32[40,128]{1,0:T(8,128)S(1)}, f32[40,128]{1,0:T(8,128)S(1)}, u32[]{:S(2)}, u32[]{:S(2)}) collective-permute-start(f32[40,128]{1,0:T(8,128)S(1)} %get-tuple-element.62), channel_id=1, source_target_pairs={{0,128},{32,160},{64,192},{96,224},{128,0},{160,32},{192,64},{224,... | collective-permute-start | bytes 61448 | tf_op jit(solution)/shard_map/ppermute | solution.py:55
  163.7 2.5 %collective-permute-start.25 = (f32[40,128]{1,0:T(8,128)S(1)}, f32[40,128]{1,0:T(8,128)S(1)}, u32[]{:S(2)}, u32[]{:S(2)}) collective-permute-start(f32[40,128]{1,0:T(8,128)S(1)} %get-tuple-element.63), channel_id=1, source_target_pairs={{0,160},{32,192},{64,224},{96,0},{128,32},{160,64},{192,96},{224,1... | collective-permute-start | bytes 61448 | tf_op jit(solution)/shard_map/ppermute | solution.py:55
  166.3 3.7 %collective-permute-start.26 = (f32[40,128]{1,0:T(8,128)S(1)}, f32[40,128]{1,0:T(8,128)S(1)}, u32[]{:S(2)}, u32[]{:S(2)}) collective-permute-start(f32[40,128]{1,0:T(8,128)S(1)} %get-tuple-element.64), channel_id=1, source_target_pairs={{0,192},{32,224},{64,0},{96,32},{128,64},{160,96},{192,128},{224,1... | collective-permute-start | bytes 61448 | tf_op jit(solution)/shard_map/ppermute | solution.py:55
  170.0 1.5 collective-permute-start.27
  171.5 2.3 %collective-permute-done.27.refs_7_ = f32[40,128]{1,0:T(8,128)S(1)} collective-permute-done((f32[40,128]{1,0:T(8,128)S(1)}, f32[40,128]{1,0:T(8,128)S(1)}, u32[]{:S(2)}, u32[]{:S(2)}) %collective-permute-start.27) | collective-permute-done | bytes 20512 | tf_op jit(solution)/shard_map/ppermute | solution.py:55
  174.4 1.9 collective-permute-start.28
  176.4 5.8 %collective-permute-start.29 = (f32[8,144,128]{2,1,0:T(8,128)S(1)}, f32[8,144,128]{2,1,0:T(8,128)S(1)}, u32[]{:S(2)}, u32[]{:S(2)}) collective-permute-start(f32[8,144,128]{2,1,0:T(8,128)S(1)} %pad_maximum_fusion.1), channel_id=1, source_target_pairs={{1,0},{2,1},{3,2},{4,3},{5,4},{6,5},{7,6},{8,7},{9,8},{10,9},{11,1... | collective-permute-start | bytes 1769480 | tf_op jit(solution)/shard_map/ppermute | solution.py:74
  183.7 3.2 %observe.1.seen_ref = f32[16,16,1024]{2,1,0:T(8,128)S(1)} custom-call(f32[40,128]{1,0:T(8,128)} %copy-done.8, f32[40,128]{1,0:T(8,128)} %copy-done.16, f32[40,128]{1,0:T(8,128)} %copy-done.17, f32[40,128]{1,0:T(8,128)} %copy-done.18, f32[40,128]{1,0:T(8,128)} %copy-done.19, f32[40,128]{1,0:T(8,128)} %copy-done.20, f32[40,128]{1,0:T(8,128)} %copy-done.21, ...), custom_call_target="tpu_custom_call" | custom-call | flops 1000000000 | bytes 1769472 | tf_op jit(solution)/shard_map/observe/pallas_call | solution.py:30
  187.7 1.8 collective-permute-done.29.below_ref
  189.5 4.6 %backward.1 = (f32[8,1024]{1,0:T(8,128)S(1)}, f32[3,8,16,1024]{3,2,1,0:T(8,128)}) custom-call(f32[16]{0:T(128)S(1)} %and_convert_fusion.inside_ref, f32[8,24,16,128]{3,2,1,0:T(8,128)S(1)} %all-to-all-done.3.back_ref, f32[8,144,128]{2,1,0:T(8,128)S(1)} %collective-permute-done.28.above_ref, f32[8,144,128]{2,1,0:T(8,128)S(1)} %collective-permute-done.29.below_ref, ...), custom_call_target="tpu_custom_call" | custom-call | flops 100000000 | bytes 7569472 | tf_op jit(solution)/shard_map/backward/pallas_call | solution.py:30
  194.2 15.4 %all_to_all.25 = f32[8,8,1024]{2,1,0:T(8,128)S(1)} all-to-all(f32[8,8,1024]{2,1,0:T(8,128)S(1)} %broadcast_in_dim.8), channel_id=1, replica_groups=mesh['ens'=8,'space'=32] {'ens'}, dimensions={0} | all-to-all | bytes 524288 | tf_op jit(solution)/shard_map/all_to_all | solution.py:50
  (113 shorter events, 17.1 us)
Async XLA Ops:
  2.8 17.2 %all-to-all-start = ((f32[8,24,128]{2,1,0:T(8,128)}), f32[8,24,128]{2,1,0:T(8,128)S(1)}, u32[]{:S(2)}, u32[]{:S(2)}) async-start(f32[8,24,128]{2,1,0:T(8,128)} %broadcast_in_dim.6), calls=%async_computation | async-start | bytes 196608 | tf_op jit(solution)/shard_map/all_to_all | solution.py:50
  20.0 20.5 %copy-start = (f32[3,8,16,1024]{3,2,1,0:T(8,128)S(1)}, f32[3,8,16,1024]{3,2,1,0:T(8,128)}, u32[]{:S(2)}) copy-start(f32[3,8,16,1024]{3,2,1,0:T(8,128)} %state_ref.3) | copy-start | bytes 4718596
  20.0 20.5 %copy-start.6 = (f32[8,1024]{1,0:T(8,128)S(1)}, f32[8,1024]{1,0:T(8,128)}, u32[]{:S(2)}) copy-start(f32[8,1024]{1,0:T(8,128)} %depth_ref.3) | copy-start | bytes 98308
  20.0 51.1 %all-to-all-start.1 = ((f32[8,384,128]{2,1,0:T(8,128)}), f32[8,384,128]{2,1,0:T(8,128)S(1)}, u32[]{:S(2)}, u32[]{:S(2)}) async-start(f32[8,384,128]{2,1,0:T(8,128)} %get-tuple-element.52), calls=%async_computation.1 | async-start | bytes 3145728 | tf_op jit(solution)/shard_map/all_to_all | solution.py:44
  23.7 15.0 %collective-permute-start = (f32[11,16,1024]{2,1,0:T(8,128)}, f32[11,16,1024]{2,1,0:T(8,128)}, u32[]{:S(2)}, u32[]{:S(2)}) collective-permute-start(f32[11,16,1024]{2,1,0:T(8,128)} %get-tuple-element.38), channel_id=1, source_target_pairs={{0,1},{1,2},{2,3},{3,4},{4,5},{5,6},{6,7},{7,8},{8,9},{9,10},{10,1... | collective-permute-start | bytes 2162696 | tf_op jit(solution)/shard_map/ppermute | solution.py:69
  25.7 14.9 %collective-permute-start.1 = (f32[11,16,1024]{2,1,0:T(8,128)}, f32[11,16,1024]{2,1,0:T(8,128)}, u32[]{:S(2)}, u32[]{:S(2)}) collective-permute-start(f32[11,16,1024]{2,1,0:T(8,128)} %get-tuple-element.39), channel_id=1, source_target_pairs={{1,0},{2,1},{3,2},{4,3},{5,4},{6,5},{7,6},{8,7},{9,8},{10,9},{11,1... | collective-permute-start | bytes 2162696 | tf_op jit(solution)/shard_map/ppermute | solution.py:74
  45.8 22.7 %copy-start.7 = (f32[4,16,128]{2,1,0:T(8,128)}, f32[4,16,128]{2,1,0:T(8,128)S(1)}, u32[]{:S(2)}) copy-start(f32[4,16,128]{2,1,0:T(8,128)S(1)} %get-tuple-element.43.refs_0_) | copy-start | bytes 98308
  45.8 16.7 %collective-permute-start.8 = (f32[4,16,128]{2,1,0:T(8,128)S(1)}, f32[4,16,128]{2,1,0:T(8,128)S(1)}, u32[]{:S(2)}, u32[]{:S(2)}) collective-permute-start(f32[4,16,128]{2,1,0:T(8,128)S(1)} %get-tuple-element.43.refs_0_), channel_id=1, source_target_pairs={{0,224},{32,0},{64,32},{96,64},{128,96},{160,128},{192,160},{224,1... | collective-permute-start | bytes 98312 | tf_op jit(solution)/shard_map/ppermute | solution.py:55
  49.0 13.4 %collective-permute-start.7 = (f32[4,16,128]{2,1,0:T(8,128)S(1)}, f32[4,16,128]{2,1,0:T(8,128)S(1)}, u32[]{:S(2)}, u32[]{:S(2)}) collective-permute-start(f32[4,16,128]{2,1,0:T(8,128)S(1)} %get-tuple-element.43.refs_0_), channel_id=1, source_target_pairs={{0,192},{32,224},{64,0},{96,32},{128,64},{160,96},{192,128},{224,1... | collective-permute-start | bytes 98312 | tf_op jit(solution)/shard_map/ppermute | solution.py:55
  51.4 15.2 %collective-permute-start.6 = (f32[4,16,128]{2,1,0:T(8,128)S(1)}, f32[4,16,128]{2,1,0:T(8,128)S(1)}, u32[]{:S(2)}, u32[]{:S(2)}) collective-permute-start(f32[4,16,128]{2,1,0:T(8,128)S(1)} %get-tuple-element.43.refs_0_), channel_id=1, source_target_pairs={{0,160},{32,192},{64,224},{96,0},{128,32},{160,64},{192,96},{224,1... | collective-permute-start | bytes 98312 | tf_op jit(solution)/shard_map/ppermute | solution.py:55
  52.8 13.8 %collective-permute-start.5 = (f32[4,16,128]{2,1,0:T(8,128)S(1)}, f32[4,16,128]{2,1,0:T(8,128)S(1)}, u32[]{:S(2)}, u32[]{:S(2)}) collective-permute-start(f32[4,16,128]{2,1,0:T(8,128)S(1)} %get-tuple-element.43.refs_0_), channel_id=1, source_target_pairs={{0,128},{32,160},{64,192},{96,224},{128,0},{160,32},{192,64},{224,... | collective-permute-start | bytes 98312 | tf_op jit(solution)/shard_map/ppermute | solution.py:55
  56.4 10.2 %collective-permute-start.4 = (f32[4,16,128]{2,1,0:T(8,128)S(1)}, f32[4,16,128]{2,1,0:T(8,128)S(1)}, u32[]{:S(2)}, u32[]{:S(2)}) collective-permute-start(f32[4,16,128]{2,1,0:T(8,128)S(1)} %get-tuple-element.43.refs_0_), channel_id=1, source_target_pairs={{0,96},{32,128},{64,160},{96,192},{128,224},{160,0},{192,32},{224,... | collective-permute-start | bytes 98312 | tf_op jit(solution)/shard_map/ppermute | solution.py:55
  62.5 6.0 %copy-start.9 = (f32[4,16,128]{2,1,0:T(8,128)}, f32[4,16,128]{2,1,0:T(8,128)S(1)}, u32[]{:S(2)}) copy-start(f32[4,16,128]{2,1,0:T(8,128)S(1)} %collective-permute-done.8.refs_7_) | copy-start | bytes 98308
  62.5 6.0 %collective-permute-start.3 = (f32[4,16,128]{2,1,0:T(8,128)S(1)}, f32[4,16,128]{2,1,0:T(8,128)S(1)}, u32[]{:S(2)}, u32[]{:S(2)}) collective-permute-start(f32[4,16,128]{2,1,0:T(8,128)S(1)} %get-tuple-element.43.refs_0_), channel_id=1, source_target_pairs={{0,64},{32,96},{64,128},{96,160},{128,192},{160,224},{192,0},{224,... | collective-permute-start | bytes 98312 | tf_op jit(solution)/shard_map/ppermute | solution.py:55
  62.5 6.0 %copy-start.10 = (f32[4,16,128]{2,1,0:T(8,128)}, f32[4,16,128]{2,1,0:T(8,128)S(1)}, u32[]{:S(2)}) copy-start(f32[4,16,128]{2,1,0:T(8,128)S(1)} %collective-permute-done.7.refs_6_) | copy-start | bytes 98308
  62.5 6.0 %collective-permute-start.2 = (f32[4,16,128]{2,1,0:T(8,128)S(1)}, f32[4,16,128]{2,1,0:T(8,128)S(1)}, u32[]{:S(2)}, u32[]{:S(2)}) collective-permute-start(f32[4,16,128]{2,1,0:T(8,128)S(1)} %get-tuple-element.43.refs_0_), channel_id=1, source_target_pairs={{0,32},{32,64},{64,96},{96,128},{128,160},{160,192},{192,224},{224... | collective-permute-start | bytes 98312 | tf_op jit(solution)/shard_map/ppermute | solution.py:55
  71.1 50.8 %all-to-all-start.2 = ((f32[8,24,16,128]{3,2,1,0:T(8,128)}), f32[8,24,16,128]{3,2,1,0:T(8,128)S(1)}, u32[]{:S(2)}, u32[]{:S(2)}) async-start(f32[8,24,16,128]{3,2,1,0:T(8,128)} %get-tuple-element.53), calls=%async_computation.2 | async-start | bytes 3145728 | tf_op jit(solution)/shard_map/all_to_all | solution.py:44
  77.0 1.3 collective-permute-start.9
  78.3 4.4 %collective-permute-start.10 = (f32[136,128]{1,0:T(8,128)S(1)}, f32[136,128]{1,0:T(8,128)S(1)}, u32[]{:S(2)}, u32[]{:S(2)}) collective-permute-start(f32[136,128]{1,0:T(8,128)S(1)} %add.41), channel_id=1, source_target_pairs={{0,2},{1,3},{2,0},{3,1},{4,6},{5,7},{6,4},{7,5},{8,10},{9,11},{10,... | collective-permute-start | bytes 208904 | tf_op jit(solution)/shard_map/ppermute | solution.py:62
  82.7 5.9 %collective-permute-start.11 = (f32[136,128]{1,0:T(8,128)S(1)}, f32[136,128]{1,0:T(8,128)S(1)}, u32[]{:S(2)}, u32[]{:S(2)}) collective-permute-start(f32[136,128]{1,0:T(8,128)S(1)} %add.42), channel_id=1, source_target_pairs={{0,4},{1,5},{2,6},{3,7},{4,0},{5,1},{6,2},{7,3},{8,12},{9,13},{10,... | collective-permute-start | bytes 208904 | tf_op jit(solution)/shard_map/ppermute | solution.py:62
  88.6 4.7 %collective-permute-start.12 = (f32[136,128]{1,0:T(8,128)S(1)}, f32[136,128]{1,0:T(8,128)S(1)}, u32[]{:S(2)}, u32[]{:S(2)}) collective-permute-start(f32[136,128]{1,0:T(8,128)S(1)} %add.43), channel_id=1, source_target_pairs={{0,8},{1,9},{2,10},{3,11},{4,12},{5,13},{6,14},{7,15},{8,0},{9,1},... | collective-permute-start | bytes 208904 | tf_op jit(solution)/shard_map/ppermute | solution.py:62
  93.3 6.1 %collective-permute-start.13 = (f32[136,128]{1,0:T(8,128)S(1)}, f32[136,128]{1,0:T(8,128)S(1)}, u32[]{:S(2)}, u32[]{:S(2)}) collective-permute-start(f32[136,128]{1,0:T(8,128)S(1)} %add.44), channel_id=1, source_target_pairs={{0,16},{1,17},{2,18},{3,19},{4,20},{5,21},{6,22},{7,23},{8,24},{9,... | collective-permute-start | bytes 208904 | tf_op jit(solution)/shard_map/ppermute | solution.py:62
  99.6 19.1 %collective-permute-start.14 = (f32[4,136,64]{2,1,0:T(8,128)S(1)}, f32[4,136,64]{2,1,0:T(8,128)S(1)}, u32[]{:S(2)}, u32[]{:S(2)}) collective-permute-start(f32[4,136,64]{2,1,0:T(8,128)S(1)} %get-tuple-element.80), channel_id=1, source_target_pairs={{0,1},{1,2},{2,3},{3,4},{4,5},{5,6},{6,7},{7,8},{8,9},{9,10},{10,1... | collective-permute-start | bytes 417800 | tf_op jit(solution)/shard_map/ppermute | solution.py:69
  101.5 17.2 %collective-permute-start.15 = (f32[4,136,64]{2,1,0:T(8,128)S(1)}, f32[4,136,64]{2,1,0:T(8,128)S(1)}, u32[]{:S(2)}, u32[]{:S(2)}) collective-permute-start(f32[4,136,64]{2,1,0:T(8,128)S(1)} %get-tuple-element.81), channel_id=1, source_target_pairs={{1,0},{2,1},{3,2},{4,3},{5,4},{6,5},{7,6},{8,7},{9,8},{10,9},{11,1... | collective-permute-start | bytes 417800 | tf_op jit(solution)/shard_map/ppermute | solution.py:74
  123.5 50.3 %all-to-all-start.3 = ((f32[8,24,16,128]{3,2,1,0:T(8,128)}), f32[8,24,16,128]{3,2,1,0:T(8,128)S(1)}, u32[]{:S(2)}, u32[]{:S(2)}) async-start(f32[8,24,16,128]{3,2,1,0:T(8,128)} %mix.1), calls=%async_computation.3 | async-start | bytes 3145728 | tf_op jit(solution)/shard_map/all_to_all | solution.py:44
  130.7 1.3 collective-permute-start.16
  132.0 4.4 %collective-permute-start.17 = (f32[128,128]{1,0:T(8,128)S(1)}, f32[128,128]{1,0:T(8,128)S(1)}, u32[]{:S(2)}, u32[]{:S(2)}) collective-permute-start(f32[128,128]{1,0:T(8,128)S(1)} %add.46), channel_id=1, source_target_pairs={{0,2},{1,3},{2,0},{3,1},{4,6},{5,7},{6,4},{7,5},{8,10},{9,11},{10,... | collective-permute-start | bytes 196616 | tf_op jit(solution)/shard_map/ppermute | solution.py:62
  136.3 5.9 %collective-permute-start.18 = (f32[128,128]{1,0:T(8,128)S(1)}, f32[128,128]{1,0:T(8,128)S(1)}, u32[]{:S(2)}, u32[]{:S(2)}) collective-permute-start(f32[128,128]{1,0:T(8,128)S(1)} %add.47), channel_id=1, source_target_pairs={{0,4},{1,5},{2,6},{3,7},{4,0},{5,1},{6,2},{7,3},{8,12},{9,13},{10,... | collective-permute-start | bytes 196616 | tf_op jit(solution)/shard_map/ppermute | solution.py:62
  142.2 4.9 %collective-permute-start.19 = (f32[128,128]{1,0:T(8,128)S(1)}, f32[128,128]{1,0:T(8,128)S(1)}, u32[]{:S(2)}, u32[]{:S(2)}) collective-permute-start(f32[128,128]{1,0:T(8,128)S(1)} %add.48), channel_id=1, source_target_pairs={{0,8},{1,9},{2,10},{3,11},{4,12},{5,13},{6,14},{7,15},{8,0},{9,1},... | collective-permute-start | bytes 196616 | tf_op jit(solution)/shard_map/ppermute | solution.py:62
  147.1 5.9 %collective-permute-start.20 = (f32[128,128]{1,0:T(8,128)S(1)}, f32[128,128]{1,0:T(8,128)S(1)}, u32[]{:S(2)}, u32[]{:S(2)}) collective-permute-start(f32[128,128]{1,0:T(8,128)S(1)} %add.49), channel_id=1, source_target_pairs={{0,16},{1,17},{2,18},{3,19},{4,20},{5,21},{6,22},{7,23},{8,24},{9,... | collective-permute-start | bytes 196616 | tf_op jit(solution)/shard_map/ppermute | solution.py:62
  154.2 19.7 %copy-start.8 = (f32[40,128]{1,0:T(8,128)}, f32[40,128]{1,0:T(8,128)S(1)}, u32[]{:S(2)}) copy-start(f32[40,128]{1,0:T(8,128)S(1)} %get-tuple-element.58.refs_0_) | copy-start | bytes 61444
  154.2 12.0 %collective-permute-start.21 = (f32[40,128]{1,0:T(8,128)S(1)}, f32[40,128]{1,0:T(8,128)S(1)}, u32[]{:S(2)}, u32[]{:S(2)}) collective-permute-start(f32[40,128]{1,0:T(8,128)S(1)} %get-tuple-element.59), channel_id=1, source_target_pairs={{0,32},{32,64},{64,96},{96,128},{128,160},{160,192},{192,224},{224... | collective-permute-start | bytes 61448 | tf_op jit(solution)/shard_map/ppermute | solution.py:55
  156.3 13.7 %collective-permute-start.22 = (f32[40,128]{1,0:T(8,128)S(1)}, f32[40,128]{1,0:T(8,128)S(1)}, u32[]{:S(2)}, u32[]{:S(2)}) collective-permute-start(f32[40,128]{1,0:T(8,128)S(1)} %get-tuple-element.60), channel_id=1, source_target_pairs={{0,64},{32,96},{64,128},{96,160},{128,192},{160,224},{192,0},{224,... | collective-permute-start | bytes 61448 | tf_op jit(solution)/shard_map/ppermute | solution.py:55
  158.6 12.9 %collective-permute-start.23 = (f32[40,128]{1,0:T(8,128)S(1)}, f32[40,128]{1,0:T(8,128)S(1)}, u32[]{:S(2)}, u32[]{:S(2)}) collective-permute-start(f32[40,128]{1,0:T(8,128)S(1)} %get-tuple-element.61), channel_id=1, source_target_pairs={{0,96},{32,128},{64,160},{96,192},{128,224},{160,0},{192,32},{224,... | collective-permute-start | bytes 61448 | tf_op jit(solution)/shard_map/ppermute | solution.py:55
  161.4 10.1 %collective-permute-start.24 = (f32[40,128]{1,0:T(8,128)S(1)}, f32[40,128]{1,0:T(8,128)S(1)}, u32[]{:S(2)}, u32[]{:S(2)}) collective-permute-start(f32[40,128]{1,0:T(8,128)S(1)} %get-tuple-element.62), channel_id=1, source_target_pairs={{0,128},{32,160},{64,192},{96,224},{128,0},{160,32},{192,64},{224,... | collective-permute-start | bytes 61448 | tf_op jit(solution)/shard_map/ppermute | solution.py:55
  163.7 7.8 %collective-permute-start.25 = (f32[40,128]{1,0:T(8,128)S(1)}, f32[40,128]{1,0:T(8,128)S(1)}, u32[]{:S(2)}, u32[]{:S(2)}) collective-permute-start(f32[40,128]{1,0:T(8,128)S(1)} %get-tuple-element.63), channel_id=1, source_target_pairs={{0,160},{32,192},{64,224},{96,0},{128,32},{160,64},{192,96},{224,1... | collective-permute-start | bytes 61448 | tf_op jit(solution)/shard_map/ppermute | solution.py:55
  166.3 7.7 %copy-start.16 = (f32[40,128]{1,0:T(8,128)}, f32[40,128]{1,0:T(8,128)S(1)}, u32[]{:S(2)}) copy-start(f32[40,128]{1,0:T(8,128)S(1)} %collective-permute-done.21.refs_1_) | copy-start | bytes 61444
  166.3 5.2 %collective-permute-start.26 = (f32[40,128]{1,0:T(8,128)S(1)}, f32[40,128]{1,0:T(8,128)S(1)}, u32[]{:S(2)}, u32[]{:S(2)}) collective-permute-start(f32[40,128]{1,0:T(8,128)S(1)} %get-tuple-element.64), channel_id=1, source_target_pairs={{0,192},{32,224},{64,0},{96,32},{128,64},{160,96},{192,128},{224,1... | collective-permute-start | bytes 61448 | tf_op jit(solution)/shard_map/ppermute | solution.py:55
  170.0 4.0 %copy-start.17 = (f32[40,128]{1,0:T(8,128)}, f32[40,128]{1,0:T(8,128)S(1)}, u32[]{:S(2)}) copy-start(f32[40,128]{1,0:T(8,128)S(1)} %collective-permute-done.22.refs_2_) | copy-start | bytes 61444
  170.0 3.8 %collective-permute-start.27 = (f32[40,128]{1,0:T(8,128)S(1)}, f32[40,128]{1,0:T(8,128)S(1)}, u32[]{:S(2)}, u32[]{:S(2)}) collective-permute-start(f32[40,128]{1,0:T(8,128)S(1)} %get-tuple-element.65), channel_id=1, source_target_pairs={{0,224},{32,0},{64,32},{96,64},{128,96},{160,128},{192,160},{224,1... | collective-permute-start | bytes 61448 | tf_op jit(solution)/shard_map/ppermute | solution.py:55
  171.5 2.5 %copy-start.18 = (f32[40,128]{1,0:T(8,128)}, f32[40,128]{1,0:T(8,128)S(1)}, u32[]{:S(2)}) copy-start(f32[40,128]{1,0:T(8,128)S(1)} %collective-permute-done.23.refs_3_) | copy-start | bytes 61444
  173.9 9.8 %copy-start.1 = (f32[8,136,128]{2,1,0:T(8,128)S(1)}, f32[8,136,128]{2,1,0:T(8,128)}, u32[]{:S(2)}) copy-start(f32[8,136,128]{2,1,0:T(8,128)} %maximum_maximum_fusion.refs_8_) | copy-start | bytes 1671172
  174.4 13.3 %collective-permute-start.28 = (f32[8,144,128]{2,1,0:T(8,128)S(1)}, f32[8,144,128]{2,1,0:T(8,128)S(1)}, u32[]{:S(2)}, u32[]{:S(2)}) collective-permute-start(f32[8,144,128]{2,1,0:T(8,128)S(1)} %pad_maximum_fusion), channel_id=1, source_target_pairs={{0,1},{1,2},{2,3},{3,4},{4,5},{5,6},{6,7},{7,8},{8,9},{9,10},{10,1... | collective-permute-start | bytes 1769480 | tf_op jit(solution)/shard_map/ppermute | solution.py:69
  176.4 13.1 %collective-permute-start.29 = (f32[8,144,128]{2,1,0:T(8,128)S(1)}, f32[8,144,128]{2,1,0:T(8,128)S(1)}, u32[]{:S(2)}, u32[]{:S(2)}) collective-permute-start(f32[8,144,128]{2,1,0:T(8,128)S(1)} %pad_maximum_fusion.1), channel_id=1, source_target_pairs={{1,0},{2,1},{3,2},{4,3},{5,4},{6,5},{7,6},{8,7},{9,8},{10,9},{11,1... | collective-permute-start | bytes 1769480 | tf_op jit(solution)/shard_map/ppermute | solution.py:74
  183.7 5.8 %copy-start.2 = (f32[8,16,1024]{2,1,0:T(8,128)S(1)}, f32[8,16,1024]{2,1,0:T(8,128)}, u32[]{:S(2)}) copy-start(f32[8,16,1024]{2,1,0:T(8,128)} %get-tuple-element.68.east1_ref) | copy-start | bytes 1572868
  183.7 5.8 %copy-start.3 = (f32[8,16,1024]{2,1,0:T(8,128)S(1)}, f32[8,16,1024]{2,1,0:T(8,128)}, u32[]{:S(2)}) copy-start(f32[8,16,1024]{2,1,0:T(8,128)} %get-tuple-element.69.north1_ref) | copy-start | bytes 1572868
  183.7 5.8 %copy-start.4 = (f32[8,16,1024]{2,1,0:T(8,128)S(1)}, f32[8,16,1024]{2,1,0:T(8,128)}, u32[]{:S(2)}) copy-start(f32[8,16,1024]{2,1,0:T(8,128)} %get-tuple-element.70.east2_ref) | copy-start | bytes 1572868
  183.7 5.8 %copy-start.5 = (f32[8,16,1024]{2,1,0:T(8,128)S(1)}, f32[8,16,1024]{2,1,0:T(8,128)}, u32[]{:S(2)}) copy-start(f32[8,16,1024]{2,1,0:T(8,128)} %get-tuple-element.71.north2_ref) | copy-start | bytes 1572868
  (9 other events, 15.0 us)

commit v2 on v1

--- a/solution.py
+++ b/solution.py
@@ -55,12 +55,21 @@
     return lax.ppermute(block, "ens", [(i, (i + distance) % count) for i in range(count)])
 
 
-def summed(block, axis):
-    count = lax.axis_size(axis)
+def summed(block):
+    count = lax.axis_size("space")
+
+    def other(distance):
+        return lax.ppermute(block, "space", [(i, i ^ distance) for i in range(count)])
+
     distance = 1
     while distance < count:
-        block = block + lax.ppermute(block, axis, [(i, i ^ distance) for i in range(count)])
-        distance *= 2
+        if distance > 1 and 2 * distance < count:
+            near, far, both = other(distance), other(2 * distance), other(3 * distance)
+            block = (block + near) + (far + both)
+            distance *= 4
+        else:
+            block = block + other(distance)
+            distance *= 2
     return block
 
 
@@ -218,7 +227,7 @@
 def backward_kernel(
     inside_ref, back_ref, above_ref, below_ref, seen_ref, depth_ref,
     east1_ref, north1_ref, east2_ref, north2_ref,
-    depth_grad_ref, state_grad_ref,
+    depth_grad_ref, height_ref, east_ref, north_ref,
     h2, h1, e1, n1, nt,
 ):
     own, size, width = east1_ref.shape
@@ -258,17 +267,27 @@
     for p in range(low - 1, high + 1):
         along = WAVE_COEF * (h1[p + 1] - h1[p - 1])
         nt[p] = n1[p] + d(p) * along
+    height_ref[...] = h1[low - 1 : high + 1]
     for p in range(low, high):
         r = p - low
         across = WAVE_COEF * cols(h1[p])
         along = WAVE_COEF * (h1[p + 1] - h1[p - 1])
-        total = e1[p] + d(p) * across
+        east_ref[r] = e1[p] + d(p) * across
         depth_grad_ref[r : r + 1] += jnp.sum(
             east1_ref[r] * across + north1_ref[r] * along, axis=0, keepdims=True
         )
-        state_grad_ref[0, r] = h1[p] + WAVE_COEF * (cols(total) + (nt[p + 1] - nt[p - 1]))
-        state_grad_ref[1, r] = total - SPIN_COEF * nt[p]
-        state_grad_ref[2, r] = nt[p] + SPIN_COEF * total
+    north_ref[...] = nt[low - 1 : high + 1]
+
+
+def finish_kernel(height_ref, east_ref, north_ref, state_grad_ref):
+    own = east_ref.shape[0]
+    for r in range(own):
+        total, north = east_ref[r], north_ref[r + 1]
+        state_grad_ref[0, r] = height_ref[r + 1] + WAVE_COEF * (
+            cols(total) + (north_ref[r + 2] - north_ref[r])
+        )
+        state_grad_ref[1, r] = total - SPIN_COEF * north
+        state_grad_ref[2, r] = north + SPIN_COEF * total
 
 
 def gram_kernel(place_ref, params_ref, *refs):
@@ -311,26 +330,35 @@
     blocks = members // step
     lane = lax.broadcasted_iota(jnp.int32, (step, members), 1)
     sub = lax.broadcasted_iota(jnp.int32, (step, members), 0)
-    left, right = [], []
-    for i in range(blocks):
-        eye = (lane == sub + i * step).astype(jnp.float32)
-        left.append(gram_ref[i * step : (i + 1) * step] + eye)
-        right.append(eye)
-    for k in range(members):
+    row_lane = lane[:1]
+    body = [
+        gram_ref[i * step : (i + 1) * step] + (lane == sub + i * step).astype(jnp.float32)
+        for i in range(blocks)
+    ]
+    for k in range(0, members, 2):
         i0, s = divmod(k, step)
-        top_left, top_right = left[i0][s : s + 1], right[i0][s : s + 1]
-        pivot = top_left[:, k : k + 1]
-        inverse_ref[k : k + 1] = top_right * (1.0 / jnp.sqrt(pivot))
-        if k == members - 1:
+        row0, row1 = body[i0][s : s + 1], body[i0][s + 1 : s + 2]
+        a, b, c = row0[:, k : k + 1], row0[:, k + 1 : k + 2], row1[:, k + 1 : k + 2]
+        over_a = 1.0 / a
+        over_c = a * (1.0 / (a * c - b * b))
+        ratio = b * over_a
+        first, second = row_lane == k, row_lane == k + 1
+        row0 = jnp.where(first, 1.0, jnp.where(second, 0.0, row0))
+        row1 = jnp.where(second, 1.0, jnp.where(first, 0.0, row1)) - ratio * row0
+        inverse_ref[k : k + 1] = jnp.where(row_lane <= k, row0 * jnp.sqrt(over_a), 0.0)
+        inverse_ref[k + 1 : k + 2] = jnp.where(row_lane <= k + 1, row1 * jnp.sqrt(over_c), 0.0)
+        if k + 2 == members:
             break
-        turned = 1.0 / pivot
-        scaled_left, scaled_right = top_left * turned, top_right * turned
+        turned1 = row1 * over_c
+        turned0 = row0 * over_a - ratio * turned1
+        used = (lane == k) | (lane == k + 1)
         for i in range(i0, blocks):
-            factor = left[i][:, k : k + 1]
-            if i == i0:
-                factor = jnp.where(sub[:, :1] > s, factor, 0.0)
-            left[i] = left[i] - factor * scaled_left
-            right[i] = right[i] - factor * scaled_right
+            if i == i0 and s + 2 == step:
+                continue
+            factor0 = jnp.broadcast_to(body[i][:, k : k + 1], (step, members))
+            factor1 = jnp.broadcast_to(body[i][:, k + 1 : k + 2], (step, members))
+            update = jnp.where(used, 0.0, body[i]) - factor0 * turned0 - factor1 * turned1
+            body[i] = jnp.where(sub > s + 1, update, body[i]) if i == i0 else update
     inverse = inverse_ref[...]
     proj = gram_ref[members:]
     mean = dot(dot(proj, inverse, ((1,), (1,))), inverse)
@@ -457,9 +485,6 @@
     sites = fields * own_rows
     half = own_rows // 2
 
-    packed = jnp.concatenate([obs_index.T.astype(jnp.float32), obs_value.T, obs_var.T])
-    packed = jnp.pad(packed, ((0, 0), (0, block_cols - packed.shape[1])))
-    params = gathered(packed, "ens")
     edge = (sum(n for _, n in STATE_EDGE) + 1, own_members, width)
     blocks = (groups, sites * own_members, block_cols)
     tail, head, cot_out = kernel_call(
@@ -472,6 +497,9 @@
         far_ins=(0, 1, 2),
         name="prepare",
     )
+    packed = jnp.concatenate([obs_index.T.astype(jnp.float32), obs_value.T, obs_var.T])
+    packed = jnp.pad(packed, ((0, 0), (0, block_cols - packed.shape[1])))
+    params = gathered(packed, "ens")
     above, below = from_above(tail), from_below(head)
     cot_out, params = lax.optimization_barrier((cot_out, params))
     cot = exchanged(cot_out).reshape(groups, sites, own_members, block_cols)
@@ -496,6 +524,8 @@
         name="forward",
     )
     observed = [observed] + [turned(observed, d) for d in range(1, groups)]
+    spread, observed = lax.optimization_barrier((spread, observed))
+    forecast = exchanged(spread)
     place = ens_place.astype(jnp.int32)[None]
     scaled, extra, gram = kernel_call(
         gram_kernel,
@@ -507,9 +537,7 @@
         flops=4 * 2 * 6 * members**3,
         name="gram",
     )
-    spread, gram = lax.optimization_barrier((spread, gram))
-    forecast = exchanged(spread)
-    gram = summed(gram, "space")
+    gram = summed(gram)
     inverse, mixing, mean_weights = kernel_call(
         factor_kernel,
         [(members, members), (members, members), (8, members)],
@@ -530,7 +558,6 @@
     (own_cross,) = kernel_call(
         cross_kernel, [(members, members)], [forecast, cot], flops=10**10, name="cross"
     )
-    mixing, obs_tall = lax.optimization_barrier((mixing, obs_tall))
     (mixed,) = kernel_call(
         mix_kernel,
         [cot.shape],
@@ -541,18 +568,19 @@
         flops=10**10,
         name="mix",
     )
-    mixed, own_cross = lax.optimization_barrier((mixed, own_cross))
     back = exchanged(mixed)
+    cross, obs_tall = lax.optimization_barrier((summed(own_cross), obs_tall))
 
     parts = kernel_call(
         pullback_kernel,
         [(2 * own_members + 8, members)] * groups,
-        [place, summed(own_cross, "space"), inverse, mean_weights],
+        [place, cross, inverse, mean_weights],
         [(members, members)] * 2,
         flops=10**9,
         name="pullback",
     )
     parts = [parts[0]] + [turned(parts[d], d) for d in range(1, groups)]
+    back, parts = lax.optimization_barrier((back, parts))
     (seen,) = kernel_call(
         observe_kernel,
         [padded],
@@ -563,7 +591,6 @@
         flops=10**9,
         name="observe",
     )
-    back, parts = lax.optimization_barrier((back, parts))
 
     by_field = back.reshape(groups, fields, own_rows, own_members, block_cols)
 
@@ -576,9 +603,10 @@
     adjoint_above = from_above(adjoint_edge(lambda n: slice(own_rows - n, own_rows)))
     adjoint_below = from_below(adjoint_edge(lambda n: slice(0, n)))
     depth_tall = jnp.concatenate([above[-1, half:own_rows], depth_field, below[-1, :half]])
-    depth_grad, state_grad = kernel_call(
+    wider = (own_rows + 2, own_members, width)
+    depth_grad, *remaining = kernel_call(
         backward_kernel,
-        [(own_rows, width), (fields,) + shape],
+        [(own_rows, width), wider, shape, wider],
         [
             inside, back, adjoint_above, adjoint_below, seen, depth_tall,
             east1, north1, east2, north2,
@@ -586,6 +614,9 @@
         [padded] * 5,
         flops=10**8,
         name="backward",
+    )
+    (state_grad,) = kernel_call(
+        finish_kernel, [(fields,) + shape], remaining, flops=10**7, name="finish"
     )
     depth_grad = jnp.sum(gathered(depth_grad, "ens"), axis=0)
     return (state_grad, depth_grad)

time: 211 us -> 198 us (0.938)
  blocking collectives: 15.4 us -> 0 us
  waiting for transfers between devices: 61.2 us -> 51.1 us
  starting transfers between devices: 90.3 us -> 99.9 us
  local copies, waits for them, and re-layouts: 4.02 us -> 7.89 us
    ppermute x10 -> x14, waiting for transfers between devices: 34.6 us -> 13.9 us  [other(): lax.ppermute(block, 'space', [(i, i ^ distance) for i in range(count)])]
    all_to_all x1 -> x0, blocking collectives: 15.4 us -> none  [gathered(): return lax.all_to_all(copies, axis, 0, 0, tiled=False)]
    all_to_all x1 -> x2, waiting for transfers between devices: 5.41 us -> 14.4 us  [gathered(): return lax.all_to_all(copies, axis, 0, 0, tiled=False)]
    ppermute x10 -> x14, starting transfers between devices: 9.9 us -> 17.1 us  [other(): lax.ppermute(block, 'space', [(i, i ^ distance) for i in range(count)])]
    all_to_all x1 -> x2, starting transfers between devices: 8.47 us -> 12.4 us  [gathered(): return lax.all_to_all(copies, axis, 0, 0, tiled=False)]
    unnamed x48 -> x50, local copies, waits for them, and re-layouts: 1.12 us -> 4.29 us
    pallas_call x9 -> x10, Pallas kernels: 34.8 us -> 34.3 us  [kernel_call(): pl.pallas_call(body, out_shape=[made(i, o) for i, o in enumerate(outs)],...]
  transfers between devices with their start and end apart: 34 -> 39, of which waited for: 18 -> 20; matrix products, arithmetic and copies ran while one was open for 2% -> 1% of each run, Pallas kernels for 14% -> 16%
where the time goes in v2:
time: 198 us; the launch traced here: 197 us
  starting transfers between devices  99.9 us (50%)
  waiting for transfers between devices  51.1 us (26%)
  Pallas kernels  34.3 us (17%)
  local copies, waits for them, and re-layouts  7.89 us (4%)
  other arithmetic  2.5 us (1%)
    pallas_call x10, Pallas kernels, kernel_call(): pl.pallas_call(body, out_shape=[made(i, o) for i, o in enumerate(outs)],...  34.3 us
    ppermute x14, starting transfers between devices, turned(): lax.ppermute(block, 'ens', [(i, (i + distance) % count) for i in range(co...  32 us
    ppermute x3, starting transfers between devices, from_below(): lax.ppermute(rows_sent, 'space', [(i + 1, i) for i in range(count - 1)])  17.3 us
    ppermute x14, starting transfers between devices, other(): lax.ppermute(block, 'space', [(i, i ^ distance) for i in range(count)])  17.1 us
    all_to_all x3, starting transfers between devices, exchanged(): return lax.all_to_all(blocks, 'ens', 0, 0, tiled=False)  15.4 us
    all_to_all x2, waiting for transfers between devices, gathered(): return lax.all_to_all(copies, axis, 0, 0, tiled=False)  14.4 us
    ppermute x14, waiting for transfers between devices, other(): lax.ppermute(block, 'space', [(i, i ^ distance) for i in range(count)])  13.9 us
    all_to_all x2, starting transfers between devices, gathered(): return lax.all_to_all(copies, axis, 0, 0, tiled=False)  12.4 us
  transfers between devices with their start and end apart: 39, of which 20 were waited for; matrix products, arithmetic and copies ran while one was open for 1% of the time, Pallas kernels for 16%

profile of v2, /device:TPU:6, one launch (start us, length us, event | category | flops | bytes accessed | tf_op | source)
XLA Modules:
  0.0 196.9 jit_solution(9913041714903916401)
XLA Ops:
  2.8 8.5 %all-to-all-start = ((f32[8,24,128]{2,1,0:T(8,128)}), f32[8,24,128]{2,1,0:T(8,128)S(1)}, u32[]{:S(2)}, u32[]{:S(2)}) async-start(f32[8,24,128]{2,1,0:T(8,128)} %broadcast_in_dim.7), calls=%async_computation | async-start | bytes 196608 | tf_op jit(solution)/shard_map/all_to_all | solution.py:50
  11.3 3.3 %prepare.1 = (f32[11,16,1024]{2,1,0:T(8,128)}, f32[11,16,1024]{2,1,0:T(8,128)}, f32[8,384,128]{2,1,0:T(8,128)}) custom-call(f32[3,8,16,1024]{3,2,1,0:T(8,128)} %state_ref.3, f32[8,1024]{1,0:T(8,128)} %depth_ref.3, f32[384,1024]{1,0:T(8,128)} %bitcast.43), custom_call_target="tpu_custom_call" | custom-call | bytes 6193152 | tf_op jit(solution)/shard_map/prepare/pallas_call | solution.py:30
  14.6 5.4 %all-to-all-done = f32[8,24,128]{2,1,0:T(8,128)S(1)} async-done(((f32[8,24,128]{2,1,0:T(8,128)}), f32[8,24,128]{2,1,0:T(8,128)S(1)}, u32[]{:S(2)}, u32[]{:S(2)}) %all-to-all-start) | async-done | bytes 98336 | tf_op jit(solution)/shard_map/all_to_all | solution.py:50
  20.0 3.7 %all-to-all-start.1 = ((f32[8,384,128]{2,1,0:T(8,128)}), f32[8,384,128]{2,1,0:T(8,128)S(1)}, u32[]{:S(2)}, u32[]{:S(2)}) async-start(f32[8,384,128]{2,1,0:T(8,128)} %get-tuple-element.69), calls=%async_computation.1 | async-start | bytes 3145728 | tf_op jit(solution)/shard_map/all_to_all | solution.py:44
  23.7 1.9 collective-permute-start
  25.7 5.8 %collective-permute-start.1 = (f32[11,16,1024]{2,1,0:T(8,128)}, f32[11,16,1024]{2,1,0:T(8,128)}, u32[]{:S(2)}, u32[]{:S(2)}) collective-permute-start(f32[11,16,1024]{2,1,0:T(8,128)} %get-tuple-element.56), channel_id=1, source_target_pairs={{1,0},{2,1},{3,2},{4,3},{5,4},{6,5},{7,6},{8,7},{9,8},{10,9},{11,1... | collective-permute-start | bytes 2162696 | tf_op jit(solution)/shard_map/ppermute | solution.py:83
  31.8 7.0 %collective-permute-done.above_ref = f32[11,16,1024]{2,1,0:T(8,128)} collective-permute-done((f32[11,16,1024]{2,1,0:T(8,128)}, f32[11,16,1024]{2,1,0:T(8,128)}, u32[]{:S(2)}, u32[]{:S(2)}) %collective-permute-start) | collective-permute-done | bytes 720928 | tf_op jit(solution)/shard_map/ppermute | solution.py:78
  38.8 1.8 collective-permute-done.1.below_ref
  40.5 5.3 %forward.1 = (f32[8,24,16,128]{3,2,1,0:T(8,128)}, f32[4,16,128]{2,1,0:T(8,128)S(1)}, f32[8,16,1024]{2,1,0:T(8,128)}, f32[8,16,1024]{2,1,0:T(8,128)}, f32[8,16,1024]{2,1,0:T(8,128)}, /*index=5*/f32[8,16,1024]{2,1,0:T(8,128)}) custom-call(f32[16]{0:T(128)S(1)} %and_convert_fusion.inside_ref, f32[3,8,16,1024]{3,2,1,0:T(8,128)S(1)} %copy-done, ...), custom_call_target="tpu_custom_call" | custom-call | flops 100000000 | bytes 6752320 | tf_op jit(solution)/shard_map/forward/pallas_call | solution.py:30
  45.8 3.2 %collective-permute-start.8 = (f32[4,16,128]{2,1,0:T(8,128)S(1)}, f32[4,16,128]{2,1,0:T(8,128)S(1)}, u32[]{:S(2)}, u32[]{:S(2)}) collective-permute-start(f32[4,16,128]{2,1,0:T(8,128)S(1)} %get-tuple-element.59.refs_0_), channel_id=1, source_target_pairs={{0,224},{32,0},{64,32},{96,64},{128,96},{160,128},{192,160},{224,1... | collective-permute-start | bytes 98312 | tf_op jit(solution)/shard_map/ppermute | solution.py:55
  49.1 2.3 %collective-permute-start.7 = (f32[4,16,128]{2,1,0:T(8,128)S(1)}, f32[4,16,128]{2,1,0:T(8,128)S(1)}, u32[]{:S(2)}, u32[]{:S(2)}) collective-permute-start(f32[4,16,128]{2,1,0:T(8,128)S(1)} %get-tuple-element.59.refs_0_), channel_id=1, source_target_pairs={{0,192},{32,224},{64,0},{96,32},{128,64},{160,96},{192,128},{224,1... | collective-permute-start | bytes 98312 | tf_op jit(solution)/shard_map/ppermute | solution.py:55
  51.4 1.4 collective-permute-start.6
  52.8 3.6 %collective-permute-start.5 = (f32[4,16,128]{2,1,0:T(8,128)S(1)}, f32[4,16,128]{2,1,0:T(8,128)S(1)}, u32[]{:S(2)}, u32[]{:S(2)}) collective-permute-start(f32[4,16,128]{2,1,0:T(8,128)S(1)} %get-tuple-element.59.refs_0_), channel_id=1, source_target_pairs={{0,128},{32,160},{64,192},{96,224},{128,0},{160,32},{192,64},{224,... | collective-permute-start | bytes 98312 | tf_op jit(solution)/shard_map/ppermute | solution.py:55
  56.7 5.8 %collective-permute-done.8.refs_7_ = f32[4,16,128]{2,1,0:T(8,128)S(1)} collective-permute-done((f32[4,16,128]{2,1,0:T(8,128)S(1)}, f32[4,16,128]{2,1,0:T(8,128)S(1)}, u32[]{:S(2)}, u32[]{:S(2)}) %collective-permute-start.8) | collective-permute-done | bytes 32800 | tf_op jit(solution)/shard_map/ppermute | solution.py:55
  62.5 4.0 %collective-permute-start.2 = (f32[4,16,128]{2,1,0:T(8,128)S(1)}, f32[4,16,128]{2,1,0:T(8,128)S(1)}, u32[]{:S(2)}, u32[]{:S(2)}) collective-permute-start(f32[4,16,128]{2,1,0:T(8,128)S(1)} %get-tuple-element.59.refs_0_), channel_id=1, source_target_pairs={{0,32},{32,64},{64,96},{96,128},{128,160},{160,192},{192,224},{224... | collective-permute-start | bytes 98312 | tf_op jit(solution)/shard_map/ppermute | solution.py:55
  66.5 2.0 %collective-permute-done.3.refs_2_ = f32[4,16,128]{2,1,0:T(8,128)S(1)} collective-permute-done((f32[4,16,128]{2,1,0:T(8,128)S(1)}, f32[4,16,128]{2,1,0:T(8,128)S(1)}, u32[]{:S(2)}, u32[]{:S(2)}) %collective-permute-start.3) | collective-permute-done | bytes 32800 | tf_op jit(solution)/shard_map/ppermute | solution.py:55
  69.7 5.9 %all-to-all-start.3 = ((f32[8,24,16,128]{3,2,1,0:T(8,128)}), f32[8,24,16,128]{3,2,1,0:T(8,128)S(1)}, u32[]{:S(2)}, u32[]{:S(2)}) async-start(f32[8,24,16,128]{3,2,1,0:T(8,128)} %get-tuple-element.70), calls=%async_computation.3 | async-start | bytes 3145728 | tf_op jit(solution)/shard_map/all_to_all | solution.py:44
  75.8 2.0 gram.1
  79.1 3.0 %collective-permute-start.12 = (f32[136,128]{1,0:T(8,128)S(1)}, f32[136,128]{1,0:T(8,128)S(1)}, u32[]{:S(2)}, u32[]{:S(2)}) collective-permute-start(f32[136,128]{1,0:T(8,128)S(1)} %add.53), channel_id=1, source_target_pairs={{0,6},{1,7},{2,4},{3,5},{4,2},{5,3},{6,0},{7,1},{8,14},{9,15},{10,... | collective-permute-start | bytes 208904 | tf_op jit(solution)/shard_map/ppermute | solution.py:62
  83.3 2.1 %collective-permute-done.12 = f32[136,128]{1,0:T(8,128)S(1)} collective-permute-done((f32[136,128]{1,0:T(8,128)S(1)}, f32[136,128]{1,0:T(8,128)S(1)}, u32[]{:S(2)}, u32[]{:S(2)}) %collective-permute-start.12) | collective-permute-done | bytes 69664 | tf_op jit(solution)/shard_map/ppermute | solution.py:62
  85.5 2.9 %collective-permute-done.11 = f32[136,128]{1,0:T(8,128)S(1)} collective-permute-done((f32[136,128]{1,0:T(8,128)S(1)}, f32[136,128]{1,0:T(8,128)S(1)}, u32[]{:S(2)}, u32[]{:S(2)}) %collective-permute-start.11) | collective-permute-done | bytes 69664 | tf_op jit(solution)/shard_map/ppermute | solution.py:62
  89.2 2.4 %collective-permute-start.14 = (f32[136,128]{1,0:T(8,128)S(1)}, f32[136,128]{1,0:T(8,128)S(1)}, u32[]{:S(2)}, u32[]{:S(2)}) collective-permute-start(f32[136,128]{1,0:T(8,128)S(1)} %add_add_fusion.1), channel_id=1, source_target_pairs={{0,16},{1,17},{2,18},{3,19},{4,20},{5,21},{6,22},{7,23},{8,24},{9,... | collective-permute-start | bytes 208904 | tf_op jit(solution)/shard_map/ppermute | solution.py:62
  95.9 11.2 %factor.1 = (f32[128,128]{1,0:T(8,128)S(1)}, f32[128,128]{1,0:T(8,128)S(1)}, f32[8,128]{1,0:T(8,128)S(1)}) custom-call(f32[136,128]{1,0:T(8,128)S(1)} %add_add_fusion.gram_ref), custom_call_target="tpu_custom_call" | custom-call | flops 1000000000 | bytes 204800 | tf_op jit(solution)/shard_map/factor/pallas_call | solution.py:30
  107.2 2.2 %mix.1 = f32[8,24,16,128]{3,2,1,0:T(8,128)} custom-call(f32[128,128]{1,0:T(8,128)S(1)} %get-tuple-element.68.mixing_ref, f32[8,24,16,128]{3,2,1,0:T(8,128)S(1)} %bitcast.41), custom_call_target="tpu_custom_call" | custom-call | flops 10000000000 | bytes 3211264 | tf_op jit(solution)/shard_map/mix/pallas_call | solution.py:30
  109.4 1.4 all-to-all-done.3.state_ref
  112.0 5.8 %all-to-all-start.2 = ((f32[8,24,16,128]{3,2,1,0:T(8,128)}), f32[8,24,16,128]{3,2,1,0:T(8,128)S(1)}, u32[]{:S(2)}, u32[]{:S(2)}) async-start(f32[8,24,16,128]{3,2,1,0:T(8,128)} %mix.1), calls=%async_computation.2 | async-start | bytes 3145728 | tf_op jit(solution)/shard_map/all_to_all | solution.py:44
  119.2 1.5 cross.1
  124.7 1.6 collective-permute-start.17
  126.5 1.9 collective-permute-start.23
  128.4 5.8 %collective-permute-start.24 = (f32[4,136,64]{2,1,0:T(8,128)S(1)}, f32[4,136,64]{2,1,0:T(8,128)S(1)}, u32[]{:S(2)}, u32[]{:S(2)}) collective-permute-start(f32[4,136,64]{2,1,0:T(8,128)S(1)} %get-tuple-element.111), channel_id=1, source_target_pairs={{1,0},{2,1},{3,2},{4,3},{5,4},{6,5},{7,6},{8,7},{9,8},{10,9},{11,1... | collective-permute-start | bytes 417800 | tf_op jit(solution)/shard_map/ppermute | solution.py:83
  134.3 3.2 %collective-permute-start.21 = (f32[128,128]{1,0:T(8,128)S(1)}, f32[128,128]{1,0:T(8,128)S(1)}, u32[]{:S(2)}, u32[]{:S(2)}) collective-permute-start(f32[128,128]{1,0:T(8,128)S(1)} %add_add_fusion.3), channel_id=1, source_target_pairs={{0,16},{1,17},{2,18},{3,19},{4,20},{5,21},{6,22},{7,23},{8,24},{9,... | collective-permute-start | bytes 196616 | tf_op jit(solution)/shard_map/ppermute | solution.py:62
  139.8 1.9 collective-permute-done.21
  143.1 2.1 %collective-permute-start.25 = (f32[40,128]{1,0:T(8,128)S(1)}, f32[40,128]{1,0:T(8,128)S(1)}, u32[]{:S(2)}, u32[]{:S(2)}) collective-permute-start(f32[40,128]{1,0:T(8,128)S(1)} %get-tuple-element.79), channel_id=1, source_target_pairs={{0,32},{32,64},{64,96},{96,128},{128,160},{160,192},{192,224},{224... | collective-permute-start | bytes 61448 | tf_op jit(solution)/shard_map/ppermute | solution.py:55
  145.2 2.4 %collective-permute-start.26 = (f32[40,128]{1,0:T(8,128)S(1)}, f32[40,128]{1,0:T(8,128)S(1)}, u32[]{:S(2)}, u32[]{:S(2)}) collective-permute-start(f32[40,128]{1,0:T(8,128)S(1)} %get-tuple-element.80), channel_id=1, source_target_pairs={{0,64},{32,96},{64,128},{96,160},{128,192},{160,224},{192,0},{224,... | collective-permute-start | bytes 61448 | tf_op jit(solution)/shard_map/ppermute | solution.py:55
  147.5 2.7 %collective-permute-start.27 = (f32[40,128]{1,0:T(8,128)S(1)}, f32[40,128]{1,0:T(8,128)S(1)}, u32[]{:S(2)}, u32[]{:S(2)}) collective-permute-start(f32[40,128]{1,0:T(8,128)S(1)} %get-tuple-element.81), channel_id=1, source_target_pairs={{0,96},{32,128},{64,160},{96,192},{128,224},{160,0},{192,32},{224,... | collective-permute-start | bytes 61448 | tf_op jit(solution)/shard_map/ppermute | solution.py:55
  150.2 2.4 %collective-permute-start.28 = (f32[40,128]{1,0:T(8,128)S(1)}, f32[40,128]{1,0:T(8,128)S(1)}, u32[]{:S(2)}, u32[]{:S(2)}) collective-permute-start(f32[40,128]{1,0:T(8,128)S(1)} %get-tuple-element.82), channel_id=1, source_target_pairs={{0,128},{32,160},{64,192},{96,224},{128,0},{160,32},{192,64},{224,... | collective-permute-start | bytes 61448 | tf_op jit(solution)/shard_map/ppermute | solution.py:55
  152.6 2.7 %collective-permute-start.29 = (f32[40,128]{1,0:T(8,128)S(1)}, f32[40,128]{1,0:T(8,128)S(1)}, u32[]{:S(2)}, u32[]{:S(2)}) collective-permute-start(f32[40,128]{1,0:T(8,128)S(1)} %get-tuple-element.83), channel_id=1, source_target_pairs={{0,160},{32,192},{64,224},{96,0},{128,32},{160,64},{192,96},{224,1... | collective-permute-start | bytes 61448 | tf_op jit(solution)/shard_map/ppermute | solution.py:55
  155.3 3.6 %collective-permute-start.30 = (f32[40,128]{1,0:T(8,128)S(1)}, f32[40,128]{1,0:T(8,128)S(1)}, u32[]{:S(2)}, u32[]{:S(2)}) collective-permute-start(f32[40,128]{1,0:T(8,128)S(1)} %get-tuple-element.84), channel_id=1, source_target_pairs={{0,192},{32,224},{64,0},{96,32},{128,64},{160,96},{192,128},{224,1... | collective-permute-start | bytes 61448 | tf_op jit(solution)/shard_map/ppermute | solution.py:55
  158.8 1.5 collective-permute-start.31
  160.4 2.3 %collective-permute-done.31.refs_7_ = f32[40,128]{1,0:T(8,128)S(1)} collective-permute-done((f32[40,128]{1,0:T(8,128)S(1)}, f32[40,128]{1,0:T(8,128)S(1)}, u32[]{:S(2)}, u32[]{:S(2)}) %collective-permute-start.31) | collective-permute-done | bytes 20512 | tf_op jit(solution)/shard_map/ppermute | solution.py:55
  163.2 1.9 collective-permute-start.32
  165.2 5.8 %collective-permute-start.33 = (f32[8,144,128]{2,1,0:T(8,128)S(1)}, f32[8,144,128]{2,1,0:T(8,128)S(1)}, u32[]{:S(2)}, u32[]{:S(2)}) collective-permute-start(f32[8,144,128]{2,1,0:T(8,128)S(1)} %pad_maximum_fusion.1), channel_id=1, source_target_pairs={{1,0},{2,1},{3,2},{4,3},{5,4},{6,5},{7,6},{8,7},{9,8},{10,9},{11,1... | collective-permute-start | bytes 1769480 | tf_op jit(solution)/shard_map/ppermute | solution.py:83
  172.5 3.2 %observe.1.seen_ref = f32[16,16,1024]{2,1,0:T(8,128)S(1)} custom-call(f32[40,128]{1,0:T(8,128)} %copy-done.9, f32[40,128]{1,0:T(8,128)} %copy-done.17, f32[40,128]{1,0:T(8,128)} %copy-done.18, f32[40,128]{1,0:T(8,128)} %copy-done.19, f32[40,128]{1,0:T(8,128)} %copy-done.20, f32[40,128]{1,0:T(8,128)} %copy-done.21, f32[40,128]{1,0:T(8,128)} %copy-done.22, ...), custom_call_target="tpu_custom_call" | custom-call | flops 1000000000 | bytes 1769472 | tf_op jit(solution)/shard_map/observe/pallas_call | solution.py:30
  176.5 1.8 collective-permute-done.33.below_ref
  178.3 2.7 %backward.1 = (f32[8,1024]{1,0:T(8,128)S(1)}, f32[10,16,1024]{2,1,0:T(8,128)S(1)}, f32[8,16,1024]{2,1,0:T(8,128)S(1)}, f32[10,16,1024]{2,1,0:T(8,128)S(1)}) custom-call(f32[16]{0:T(128)S(1)} %and_convert_fusion.inside_ref, f32[8,24,16,128]{3,2,1,0:T(8,128)S(1)} %all-to-all-done.2.back_ref, f32[8,144,128]{2,1,0:T(8,128)S(1)} %collective-permute-done.32.above_ref, ...), custom_call_target="tpu_custom_call" | custom-call | flops 100000000 | bytes 7831616 | tf_op jit(solution)/shard_map/backward/pallas_call | solution.py:30
  181.8 3.9 %all-to-all-start.4 = ((f32[8,8,1024]{2,1,0:T(8,128)}), f32[8,8,1024]{2,1,0:T(8,128)S(1)}, u32[]{:S(2)}, u32[]{:S(2)}) async-start(f32[8,8,1024]{2,1,0:T(8,128)} %broadcast_in_dim.8), calls=%async_computation.4 | async-start | bytes 524288 | tf_op jit(solution)/shard_map/all_to_all | solution.py:50
  185.8 1.5 finish.1
  187.2 9.0 %all-to-all-done.4 = f32[8,8,1024]{2,1,0:T(8,128)S(1)} async-done(((f32[8,8,1024]{2,1,0:T(8,128)}), f32[8,8,1024]{2,1,0:T(8,128)S(1)}, u32[]{:S(2)}, u32[]{:S(2)}) %all-to-all-start.4) | async-done | bytes 262176 | tf_op jit(solution)/shard_map/all_to_all | solution.py:50
  (121 shorter events, 26.4 us)
Async XLA Ops:
  2.8 17.2 %all-to-all-start = ((f32[8,24,128]{2,1,0:T(8,128)}), f32[8,24,128]{2,1,0:T(8,128)S(1)}, u32[]{:S(2)}, u32[]{:S(2)}) async-start(f32[8,24,128]{2,1,0:T(8,128)} %broadcast_in_dim.7), calls=%async_computation | async-start | bytes 196608 | tf_op jit(solution)/shard_map/all_to_all | solution.py:50
  20.0 20.5 %copy-start = (f32[3,8,16,1024]{3,2,1,0:T(8,128)S(1)}, f32[3,8,16,1024]{3,2,1,0:T(8,128)}, u32[]{:S(2)}) copy-start(f32[3,8,16,1024]{3,2,1,0:T(8,128)} %state_ref.3) | copy-start | bytes 4718596
  20.0 20.5 %copy-start.7 = (f32[8,1024]{1,0:T(8,128)S(1)}, f32[8,1024]{1,0:T(8,128)}, u32[]{:S(2)}) copy-start(f32[8,1024]{1,0:T(8,128)} %depth_ref.3) | copy-start | bytes 98308
  20.0 49.7 %all-to-all-start.1 = ((f32[8,384,128]{2,1,0:T(8,128)}), f32[8,384,128]{2,1,0:T(8,128)S(1)}, u32[]{:S(2)}, u32[]{:S(2)}) async-start(f32[8,384,128]{2,1,0:T(8,128)} %get-tuple-element.69), calls=%async_computation.1 | async-start | bytes 3145728 | tf_op jit(solution)/shard_map/all_to_all | solution.py:44
  23.7 15.0 %collective-permute-start = (f32[11,16,1024]{2,1,0:T(8,128)}, f32[11,16,1024]{2,1,0:T(8,128)}, u32[]{:S(2)}, u32[]{:S(2)}) collective-permute-start(f32[11,16,1024]{2,1,0:T(8,128)} %get-tuple-element.55), channel_id=1, source_target_pairs={{0,1},{1,2},{2,3},{3,4},{4,5},{5,6},{6,7},{7,8},{8,9},{9,10},{10,1... | collective-permute-start | bytes 2162696 | tf_op jit(solution)/shard_map/ppermute | solution.py:78
  25.7 14.9 %collective-permute-start.1 = (f32[11,16,1024]{2,1,0:T(8,128)}, f32[11,16,1024]{2,1,0:T(8,128)}, u32[]{:S(2)}, u32[]{:S(2)}) collective-permute-start(f32[11,16,1024]{2,1,0:T(8,128)} %get-tuple-element.56), channel_id=1, source_target_pairs={{1,0},{2,1},{3,2},{4,3},{5,4},{6,5},{7,6},{8,7},{9,8},{10,9},{11,1... | collective-permute-start | bytes 2162696 | tf_op jit(solution)/shard_map/ppermute | solution.py:83
  45.8 23.9 %copy-start.8 = (f32[4,16,128]{2,1,0:T(8,128)}, f32[4,16,128]{2,1,0:T(8,128)S(1)}, u32[]{:S(2)}) copy-start(f32[4,16,128]{2,1,0:T(8,128)S(1)} %get-tuple-element.59.refs_0_) | copy-start | bytes 98308
  45.8 16.6 %collective-permute-start.8 = (f32[4,16,128]{2,1,0:T(8,128)S(1)}, f32[4,16,128]{2,1,0:T(8,128)S(1)}, u32[]{:S(2)}, u32[]{:S(2)}) collective-permute-start(f32[4,16,128]{2,1,0:T(8,128)S(1)} %get-tuple-element.59.refs_0_), channel_id=1, source_target_pairs={{0,224},{32,0},{64,32},{96,64},{128,96},{160,128},{192,160},{224,1... | collective-permute-start | bytes 98312 | tf_op jit(solution)/shard_map/ppermute | solution.py:55
  49.1 13.4 %collective-permute-start.7 = (f32[4,16,128]{2,1,0:T(8,128)S(1)}, f32[4,16,128]{2,1,0:T(8,128)S(1)}, u32[]{:S(2)}, u32[]{:S(2)}) collective-permute-start(f32[4,16,128]{2,1,0:T(8,128)S(1)} %get-tuple-element.59.refs_0_), channel_id=1, source_target_pairs={{0,192},{32,224},{64,0},{96,32},{128,64},{160,96},{192,128},{224,1... | collective-permute-start | bytes 98312 | tf_op jit(solution)/shard_map/ppermute | solution.py:55
  51.4 15.0 %collective-permute-start.6 = (f32[4,16,128]{2,1,0:T(8,128)S(1)}, f32[4,16,128]{2,1,0:T(8,128)S(1)}, u32[]{:S(2)}, u32[]{:S(2)}) collective-permute-start(f32[4,16,128]{2,1,0:T(8,128)S(1)} %get-tuple-element.59.refs_0_), channel_id=1, source_target_pairs={{0,160},{32,192},{64,224},{96,0},{128,32},{160,64},{192,96},{224,1... | collective-permute-start | bytes 98312 | tf_op jit(solution)/shard_map/ppermute | solution.py:55
  52.8 13.6 %collective-permute-start.5 = (f32[4,16,128]{2,1,0:T(8,128)S(1)}, f32[4,16,128]{2,1,0:T(8,128)S(1)}, u32[]{:S(2)}, u32[]{:S(2)}) collective-permute-start(f32[4,16,128]{2,1,0:T(8,128)S(1)} %get-tuple-element.59.refs_0_), channel_id=1, source_target_pairs={{0,128},{32,160},{64,192},{96,224},{128,0},{160,32},{192,64},{224,... | collective-permute-start | bytes 98312 | tf_op jit(solution)/shard_map/ppermute | solution.py:55
  56.4 10.0 %collective-permute-start.4 = (f32[4,16,128]{2,1,0:T(8,128)S(1)}, f32[4,16,128]{2,1,0:T(8,128)S(1)}, u32[]{:S(2)}, u32[]{:S(2)}) collective-permute-start(f32[4,16,128]{2,1,0:T(8,128)S(1)} %get-tuple-element.59.refs_0_), channel_id=1, source_target_pairs={{0,96},{32,128},{64,160},{96,192},{128,224},{160,0},{192,32},{224,... | collective-permute-start | bytes 98312 | tf_op jit(solution)/shard_map/ppermute | solution.py:55
  62.5 6.0 %copy-start.10 = (f32[4,16,128]{2,1,0:T(8,128)}, f32[4,16,128]{2,1,0:T(8,128)S(1)}, u32[]{:S(2)}) copy-start(f32[4,16,128]{2,1,0:T(8,128)S(1)} %collective-permute-done.8.refs_7_) | copy-start | bytes 98308
  62.5 6.0 %collective-permute-start.3 = (f32[4,16,128]{2,1,0:T(8,128)S(1)}, f32[4,16,128]{2,1,0:T(8,128)S(1)}, u32[]{:S(2)}, u32[]{:S(2)}) collective-permute-start(f32[4,16,128]{2,1,0:T(8,128)S(1)} %get-tuple-element.59.refs_0_), channel_id=1, source_target_pairs={{0,64},{32,96},{64,128},{96,160},{128,192},{160,224},{192,0},{224,... | collective-permute-start | bytes 98312 | tf_op jit(solution)/shard_map/ppermute | solution.py:55
  62.5 6.0 %copy-start.11 = (f32[4,16,128]{2,1,0:T(8,128)}, f32[4,16,128]{2,1,0:T(8,128)S(1)}, u32[]{:S(2)}) copy-start(f32[4,16,128]{2,1,0:T(8,128)S(1)} %collective-permute-done.7.refs_6_) | copy-start | bytes 98308
  62.5 6.0 %collective-permute-start.2 = (f32[4,16,128]{2,1,0:T(8,128)S(1)}, f32[4,16,128]{2,1,0:T(8,128)S(1)}, u32[]{:S(2)}, u32[]{:S(2)}) collective-permute-start(f32[4,16,128]{2,1,0:T(8,128)S(1)} %get-tuple-element.59.refs_0_), channel_id=1, source_target_pairs={{0,32},{32,64},{64,96},{96,128},{128,160},{160,192},{192,224},{224... | collective-permute-start | bytes 98312 | tf_op jit(solution)/shard_map/ppermute | solution.py:55
  69.7 41.1 %all-to-all-start.3 = ((f32[8,24,16,128]{3,2,1,0:T(8,128)}), f32[8,24,16,128]{3,2,1,0:T(8,128)S(1)}, u32[]{:S(2)}, u32[]{:S(2)}) async-start(f32[8,24,16,128]{3,2,1,0:T(8,128)} %get-tuple-element.70), calls=%async_computation.3 | async-start | bytes 3145728 | tf_op jit(solution)/shard_map/all_to_all | solution.py:44
  77.8 1.3 collective-permute-start.9
  79.1 6.3 %collective-permute-start.12 = (f32[136,128]{1,0:T(8,128)S(1)}, f32[136,128]{1,0:T(8,128)S(1)}, u32[]{:S(2)}, u32[]{:S(2)}) collective-permute-start(f32[136,128]{1,0:T(8,128)S(1)} %add.53), channel_id=1, source_target_pairs={{0,6},{1,7},{2,4},{3,5},{4,2},{5,3},{6,0},{7,1},{8,14},{9,15},{10,... | collective-permute-start | bytes 208904 | tf_op jit(solution)/shard_map/ppermute | solution.py:62
  82.2 6.2 %collective-permute-start.11 = (f32[136,128]{1,0:T(8,128)S(1)}, f32[136,128]{1,0:T(8,128)S(1)}, u32[]{:S(2)}, u32[]{:S(2)}) collective-permute-start(f32[136,128]{1,0:T(8,128)S(1)} %add.53), channel_id=1, source_target_pairs={{0,4},{1,5},{2,6},{3,7},{4,0},{5,1},{6,2},{7,3},{8,12},{9,13},{10,... | collective-permute-start | bytes 208904 | tf_op jit(solution)/shard_map/ppermute | solution.py:62
  82.9 5.5 %collective-permute-start.10 = (f32[136,128]{1,0:T(8,128)S(1)}, f32[136,128]{1,0:T(8,128)S(1)}, u32[]{:S(2)}, u32[]{:S(2)}) collective-permute-start(f32[136,128]{1,0:T(8,128)S(1)} %add.53), channel_id=1, source_target_pairs={{0,2},{1,3},{2,0},{3,1},{4,6},{5,7},{6,4},{7,5},{8,10},{9,11},{10,... | collective-permute-start | bytes 208904 | tf_op jit(solution)/shard_map/ppermute | solution.py:62
  88.4 5.8 %collective-permute-start.15 = (f32[136,128]{1,0:T(8,128)S(1)}, f32[136,128]{1,0:T(8,128)S(1)}, u32[]{:S(2)}, u32[]{:S(2)}) collective-permute-start(f32[136,128]{1,0:T(8,128)S(1)} %add_add_fusion.1), channel_id=1, source_target_pairs={{0,24},{1,25},{2,26},{3,27},{4,28},{5,29},{6,30},{7,31},{8,16},{9,... | collective-permute-start | bytes 208904 | tf_op jit(solution)/shard_map/ppermute | solution.py:62
  89.2 5.8 %collective-permute-start.14 = (f32[136,128]{1,0:T(8,128)S(1)}, f32[136,128]{1,0:T(8,128)S(1)}, u32[]{:S(2)}, u32[]{:S(2)}) collective-permute-start(f32[136,128]{1,0:T(8,128)S(1)} %add_add_fusion.1), channel_id=1, source_target_pairs={{0,16},{1,17},{2,18},{3,19},{4,20},{5,21},{6,22},{7,23},{8,24},{9,... | collective-permute-start | bytes 208904 | tf_op jit(solution)/shard_map/ppermute | solution.py:62
  91.6 4.3 %collective-permute-start.13 = (f32[136,128]{1,0:T(8,128)S(1)}, f32[136,128]{1,0:T(8,128)S(1)}, u32[]{:S(2)}, u32[]{:S(2)}) collective-permute-start(f32[136,128]{1,0:T(8,128)S(1)} %add_add_fusion.1), channel_id=1, source_target_pairs={{0,8},{1,9},{2,10},{3,11},{4,12},{5,13},{6,14},{7,15},{8,0},{9,1},... | collective-permute-start | bytes 208904 | tf_op jit(solution)/shard_map/ppermute | solution.py:62
  112.0 50.6 %all-to-all-start.2 = ((f32[8,24,16,128]{3,2,1,0:T(8,128)}), f32[8,24,16,128]{3,2,1,0:T(8,128)S(1)}, u32[]{:S(2)}, u32[]{:S(2)}) async-start(f32[8,24,16,128]{3,2,1,0:T(8,128)} %mix.1), calls=%async_computation.2 | async-start | bytes 3145728 | tf_op jit(solution)/shard_map/all_to_all | solution.py:44
  120.8 1.3 collective-permute-start.16
  122.1 12.0 %collective-permute-start.19 = (f32[128,128]{1,0:T(8,128)S(1)}, f32[128,128]{1,0:T(8,128)S(1)}, u32[]{:S(2)}, u32[]{:S(2)}) collective-permute-start(f32[128,128]{1,0:T(8,128)S(1)} %add.60), channel_id=1, source_target_pairs={{0,6},{1,7},{2,4},{3,5},{4,2},{5,3},{6,0},{7,1},{8,14},{9,15},{10,... | collective-permute-start | bytes 196616 | tf_op jit(solution)/shard_map/ppermute | solution.py:62
  123.5 10.6 %collective-permute-start.18 = (f32[128,128]{1,0:T(8,128)S(1)}, f32[128,128]{1,0:T(8,128)S(1)}, u32[]{:S(2)}, u32[]{:S(2)}) collective-permute-start(f32[128,128]{1,0:T(8,128)S(1)} %add.60), channel_id=1, source_target_pairs={{0,4},{1,5},{2,6},{3,7},{4,0},{5,1},{6,2},{7,3},{8,12},{9,13},{10,... | collective-permute-start | bytes 196616 | tf_op jit(solution)/shard_map/ppermute | solution.py:62
  124.7 9.5 %collective-permute-start.17 = (f32[128,128]{1,0:T(8,128)S(1)}, f32[128,128]{1,0:T(8,128)S(1)}, u32[]{:S(2)}, u32[]{:S(2)}) collective-permute-start(f32[128,128]{1,0:T(8,128)S(1)} %add.60), channel_id=1, source_target_pairs={{0,2},{1,3},{2,0},{3,1},{4,6},{5,7},{6,4},{7,5},{8,10},{9,11},{10,... | collective-permute-start | bytes 196616 | tf_op jit(solution)/shard_map/ppermute | solution.py:62
  126.5 11.9 %collective-permute-start.23 = (f32[4,136,64]{2,1,0:T(8,128)S(1)}, f32[4,136,64]{2,1,0:T(8,128)S(1)}, u32[]{:S(2)}, u32[]{:S(2)}) collective-permute-start(f32[4,136,64]{2,1,0:T(8,128)S(1)} %get-tuple-element.110), channel_id=1, source_target_pairs={{0,1},{1,2},{2,3},{3,4},{4,5},{5,6},{6,7},{7,8},{8,9},{9,10},{10,1... | collective-permute-start | bytes 417800 | tf_op jit(solution)/shard_map/ppermute | solution.py:78
  128.4 10.0 %collective-permute-start.24 = (f32[4,136,64]{2,1,0:T(8,128)S(1)}, f32[4,136,64]{2,1,0:T(8,128)S(1)}, u32[]{:S(2)}, u32[]{:S(2)}) collective-permute-start(f32[4,136,64]{2,1,0:T(8,128)S(1)} %get-tuple-element.111), channel_id=1, source_target_pairs={{1,0},{2,1},{3,2},{4,3},{5,4},{6,5},{7,6},{8,7},{9,8},{10,9},{11,1... | collective-permute-start | bytes 417800 | tf_op jit(solution)/shard_map/ppermute | solution.py:83
  134.2 5.6 %collective-permute-start.22 = (f32[128,128]{1,0:T(8,128)S(1)}, f32[128,128]{1,0:T(8,128)S(1)}, u32[]{:S(2)}, u32[]{:S(2)}) collective-permute-start(f32[128,128]{1,0:T(8,128)S(1)} %add_add_fusion.3), channel_id=1, source_target_pairs={{0,24},{1,25},{2,26},{3,27},{4,28},{5,29},{6,30},{7,31},{8,16},{9,... | collective-permute-start | bytes 196616 | tf_op jit(solution)/shard_map/ppermute | solution.py:62
  134.3 7.4 %collective-permute-start.21 = (f32[128,128]{1,0:T(8,128)S(1)}, f32[128,128]{1,0:T(8,128)S(1)}, u32[]{:S(2)}, u32[]{:S(2)}) collective-permute-start(f32[128,128]{1,0:T(8,128)S(1)} %add_add_fusion.3), channel_id=1, source_target_pairs={{0,16},{1,17},{2,18},{3,19},{4,20},{5,21},{6,22},{7,23},{8,24},{9,... | collective-permute-start | bytes 196616 | tf_op jit(solution)/shard_map/ppermute | solution.py:62
  137.5 4.3 %collective-permute-start.20 = (f32[128,128]{1,0:T(8,128)S(1)}, f32[128,128]{1,0:T(8,128)S(1)}, u32[]{:S(2)}, u32[]{:S(2)}) collective-permute-start(f32[128,128]{1,0:T(8,128)S(1)} %add_add_fusion.3), channel_id=1, source_target_pairs={{0,8},{1,9},{2,10},{3,11},{4,12},{5,13},{6,14},{7,15},{8,0},{9,1},... | collective-permute-start | bytes 196616 | tf_op jit(solution)/shard_map/ppermute | solution.py:62
  143.1 19.7 %copy-start.9 = (f32[40,128]{1,0:T(8,128)}, f32[40,128]{1,0:T(8,128)S(1)}, u32[]{:S(2)}) copy-start(f32[40,128]{1,0:T(8,128)S(1)} %get-tuple-element.87.refs_0_) | copy-start | bytes 61444
  143.1 12.2 %collective-permute-start.25 = (f32[40,128]{1,0:T(8,128)S(1)}, f32[40,128]{1,0:T(8,128)S(1)}, u32[]{:S(2)}, u32[]{:S(2)}) collective-permute-start(f32[40,128]{1,0:T(8,128)S(1)} %get-tuple-element.79), channel_id=1, source_target_pairs={{0,32},{32,64},{64,96},{96,128},{128,160},{160,192},{192,224},{224... | collective-permute-start | bytes 61448 | tf_op jit(solution)/shard_map/ppermute | solution.py:55
  145.2 13.7 %collective-permute-start.26 = (f32[40,128]{1,0:T(8,128)S(1)}, f32[40,128]{1,0:T(8,128)S(1)}, u32[]{:S(2)}, u32[]{:S(2)}) collective-permute-start(f32[40,128]{1,0:T(8,128)S(1)} %get-tuple-element.80), channel_id=1, source_target_pairs={{0,64},{32,96},{64,128},{96,160},{128,192},{160,224},{192,0},{224,... | collective-permute-start | bytes 61448 | tf_op jit(solution)/shard_map/ppermute | solution.py:55
  147.5 12.8 %collective-permute-start.27 = (f32[40,128]{1,0:T(8,128)S(1)}, f32[40,128]{1,0:T(8,128)S(1)}, u32[]{:S(2)}, u32[]{:S(2)}) collective-permute-start(f32[40,128]{1,0:T(8,128)S(1)} %get-tuple-element.81), channel_id=1, source_target_pairs={{0,96},{32,128},{64,160},{96,192},{128,224},{160,0},{192,32},{224,... | collective-permute-start | bytes 61448 | tf_op jit(solution)/shard_map/ppermute | solution.py:55
  150.2 10.1 %collective-permute-start.28 = (f32[40,128]{1,0:T(8,128)S(1)}, f32[40,128]{1,0:T(8,128)S(1)}, u32[]{:S(2)}, u32[]{:S(2)}) collective-permute-start(f32[40,128]{1,0:T(8,128)S(1)} %get-tuple-element.82), channel_id=1, source_target_pairs={{0,128},{32,160},{64,192},{96,224},{128,0},{160,32},{192,64},{224,... | collective-permute-start | bytes 61448 | tf_op jit(solution)/shard_map/ppermute | solution.py:55
  152.6 7.7 %collective-permute-start.29 = (f32[40,128]{1,0:T(8,128)S(1)}, f32[40,128]{1,0:T(8,128)S(1)}, u32[]{:S(2)}, u32[]{:S(2)}) collective-permute-start(f32[40,128]{1,0:T(8,128)S(1)} %get-tuple-element.83), channel_id=1, source_target_pairs={{0,160},{32,192},{64,224},{96,0},{128,32},{160,64},{192,96},{224,1... | collective-permute-start | bytes 61448 | tf_op jit(solution)/shard_map/ppermute | solution.py:55
  155.3 7.5 %copy-start.17 = (f32[40,128]{1,0:T(8,128)}, f32[40,128]{1,0:T(8,128)S(1)}, u32[]{:S(2)}) copy-start(f32[40,128]{1,0:T(8,128)S(1)} %collective-permute-done.25.refs_1_) | copy-start | bytes 61444
  155.3 5.1 %collective-permute-start.30 = (f32[40,128]{1,0:T(8,128)S(1)}, f32[40,128]{1,0:T(8,128)S(1)}, u32[]{:S(2)}, u32[]{:S(2)}) collective-permute-start(f32[40,128]{1,0:T(8,128)S(1)} %get-tuple-element.84), channel_id=1, source_target_pairs={{0,192},{32,224},{64,0},{96,32},{128,64},{160,96},{192,128},{224,1... | collective-permute-start | bytes 61448 | tf_op jit(solution)/shard_map/ppermute | solution.py:55
  158.8 3.8 %collective-permute-start.31 = (f32[40,128]{1,0:T(8,128)S(1)}, f32[40,128]{1,0:T(8,128)S(1)}, u32[]{:S(2)}, u32[]{:S(2)}) collective-permute-start(f32[40,128]{1,0:T(8,128)S(1)} %get-tuple-element.85), channel_id=1, source_target_pairs={{0,224},{32,0},{64,32},{96,64},{128,96},{160,128},{192,160},{224,1... | collective-permute-start | bytes 61448 | tf_op jit(solution)/shard_map/ppermute | solution.py:55
  163.2 13.3 %collective-permute-start.32 = (f32[8,144,128]{2,1,0:T(8,128)S(1)}, f32[8,144,128]{2,1,0:T(8,128)S(1)}, u32[]{:S(2)}, u32[]{:S(2)}) collective-permute-start(f32[8,144,128]{2,1,0:T(8,128)S(1)} %pad_maximum_fusion), channel_id=1, source_target_pairs={{0,1},{1,2},{2,3},{3,4},{4,5},{5,6},{6,7},{7,8},{8,9},{9,10},{10,1... | collective-permute-start | bytes 1769480 | tf_op jit(solution)/shard_map/ppermute | solution.py:78
  165.2 13.1 %collective-permute-start.33 = (f32[8,144,128]{2,1,0:T(8,128)S(1)}, f32[8,144,128]{2,1,0:T(8,128)S(1)}, u32[]{:S(2)}, u32[]{:S(2)}) collective-permute-start(f32[8,144,128]{2,1,0:T(8,128)S(1)} %pad_maximum_fusion.1), channel_id=1, source_target_pairs={{1,0},{2,1},{3,2},{4,3},{5,4},{6,5},{7,6},{8,7},{9,8},{10,9},{11,1... | collective-permute-start | bytes 1769480 | tf_op jit(solution)/shard_map/ppermute | solution.py:83
  172.5 5.8 %copy-start.3 = (f32[8,16,1024]{2,1,0:T(8,128)S(1)}, f32[8,16,1024]{2,1,0:T(8,128)}, u32[]{:S(2)}) copy-start(f32[8,16,1024]{2,1,0:T(8,128)} %get-tuple-element.96.east1_ref) | copy-start | bytes 1572868
  172.5 5.8 %copy-start.4 = (f32[8,16,1024]{2,1,0:T(8,128)S(1)}, f32[8,16,1024]{2,1,0:T(8,128)}, u32[]{:S(2)}) copy-start(f32[8,16,1024]{2,1,0:T(8,128)} %get-tuple-element.97.north1_ref) | copy-start | bytes 1572868
  181.8 14.4 %all-to-all-start.4 = ((f32[8,8,1024]{2,1,0:T(8,128)}), f32[8,8,1024]{2,1,0:T(8,128)S(1)}, u32[]{:S(2)}, u32[]{:S(2)}) async-start(f32[8,8,1024]{2,1,0:T(8,128)} %broadcast_in_dim.8), calls=%async_computation.4 | async-start | bytes 524288 | tf_op jit(solution)/shard_map/all_to_all | solution.py:50
  (15 other events, 36.2 us)

commit v3 on v2

--- a/solution.py
+++ b/solution.py
@@ -53,6 +53,11 @@
 def turned(block, distance):
     count = lax.axis_size("ens")
     return lax.ppermute(block, "ens", [(i, (i + distance) % count) for i in range(count)])
+
+
+def crossed(block, distance):
+    count = lax.axis_size("ens")
+    return lax.ppermute(block, "ens", [(i, i ^ distance) for i in range(count)])
 
 
 def summed(block):
@@ -372,7 +377,8 @@
 def pullback_kernel(place_ref, cross_ref, inverse_ref, mean_ref, *refs):
     *parts, grad, column = refs
     members = inverse_ref.shape[0]
-    groups = len(parts)
+    near = len(parts)
+    groups = 2 * near
     size = members // groups
     inverse = inverse_ref[...]
     cross = cross_ref[...]
@@ -392,28 +398,23 @@
     gram_grad = -(inner_grad + outer + outer.T)
     grad[...] = gram_grad - jnp.mean(gram_grad, axis=0, keepdims=True)
     column[...] = every - jnp.mean(every, axis=0, keepdims=True)
-    for d, part in enumerate(parts):
-        there = lax.rem(place_ref[0] + d, groups)
-        rows_there = pl.ds(pl.multiple_of(there * size, size), size)
-        part[:size] = grad[rows_there]
-        part[size : 2 * size] = column[rows_there]
-        part[2 * size :] = proj_grad
+    for j, part in enumerate(parts):
+        for h in range(2):
+            there = place_ref[0] ^ (j + h * near)
+            rows_there = pl.ds(pl.multiple_of(there * size, size), size)
+            part[h, :size] = grad[rows_there]
+            part[h, size : 2 * size] = column[rows_there]
+            part[h, 2 * size :] = proj_grad
 
 
 def observe_kernel(*refs):
-    *part_refs, obs_ref, seen_ref, parts, sems = refs
+    near_ref, far_ref, obs_ref, seen_ref = refs
     tall, size, width = seen_ref.shape
     pairs, high, lanes = obs_ref.shape
     members = high - 8
     part = lanes
     groups = width // part
-    copies = []
-    for d, ref in enumerate(part_refs):
-        copies.append(pltpu.make_async_copy(ref, parts.at[d], sems.at[d]))
-        copies[-1].start()
-    for copy in copies:
-        copy.wait()
-    whole = parts[...].sum(0)
+    whole = near_ref[...] + far_ref[...]
     own_grad, own_proj, proj_grad = whole[:size], whole[size : 2 * size], whole[2 * size :]
     lane = lax.broadcasted_iota(jnp.int32, (size, lanes), 1)
     sub = lax.broadcasted_iota(jnp.int32, (part, lanes), 0)
@@ -436,15 +437,24 @@
                 seen_ref[t + h * pairs, :, j * part : (j + 1) * part] = put[at : at + size]
 
 
-def cross_kernel(state_ref, cot_ref, out_ref):
-    groups, sites, size, part = state_ref.shape
+def cross_kernel(state_ref, cot_ref, out_ref, state, sems):
+    groups, sites, size, part = state.shape
     members = groups * size
+    pieces = sems.shape[0]
+    piece = sites // pieces
+    copies = []
+    for i in range(pieces):
+        now = pl.ds(i * piece, piece)
+        copies.append(pltpu.make_async_copy(state_ref.at[:, now], state.at[:, now], sems.at[i]))
+        copies[-1].start()
     total = jnp.zeros((members, members), jnp.float32)
     for at in range(0, sites, 2):
+        if at % piece == 0:
+            copies[at // piece].wait()
         pick = lambda ref: jnp.concatenate(
             [ref[:, at + i].reshape(members, part) for i in range(2)], axis=1
         )
-        total += dot(pick(state_ref), pick(cot_ref), ((1,), (1,)))
+        total += dot(pick(state), pick(cot_ref), ((1,), (1,)))
     out_ref[...] = total
 
 
@@ -556,7 +566,14 @@
     )
 
     (own_cross,) = kernel_call(
-        cross_kernel, [(members, members)], [forecast, cot], flops=10**10, name="cross"
+        cross_kernel,
+        [(members, members)],
+        [forecast, cot],
+        [cot.shape],
+        copies=fields,
+        far_ins=(0,),
+        flops=10**10,
+        name="cross",
     )
     (mixed,) = kernel_call(
         mix_kernel,
@@ -571,26 +588,18 @@
     back = exchanged(mixed)
     cross, obs_tall = lax.optimization_barrier((summed(own_cross), obs_tall))
 
+    near = groups // 2
     parts = kernel_call(
         pullback_kernel,
-        [(2 * own_members + 8, members)] * groups,
+        [(2, 2 * own_members + 8, members)] * near,
         [place, cross, inverse, mean_weights],
         [(members, members)] * 2,
         flops=10**9,
         name="pullback",
     )
-    parts = [parts[0]] + [turned(parts[d], d) for d in range(1, groups)]
+    parts = [parts[0]] + [crossed(parts[j], j) for j in range(1, near)]
     back, parts = lax.optimization_barrier((back, parts))
-    (seen,) = kernel_call(
-        observe_kernel,
-        [padded],
-        parts + [obs_tall],
-        [(groups,) + parts[0].shape],
-        copies=groups,
-        far_ins=tuple(range(groups)),
-        flops=10**9,
-        name="observe",
-    )
+    whole = sum(parts[1:], parts[0])
 
     by_field = back.reshape(groups, fields, own_rows, own_members, block_cols)
 
@@ -600,8 +609,17 @@
         ]
         return jnp.concatenate(parts, axis=1)
 
-    adjoint_above = from_above(adjoint_edge(lambda n: slice(own_rows - n, own_rows)))
-    adjoint_below = from_below(adjoint_edge(lambda n: slice(0, n)))
+    adjoint_tail = adjoint_edge(lambda n: slice(own_rows - n, own_rows))
+    adjoint_head = adjoint_edge(lambda n: slice(0, n))
+    adjoint_above, adjoint_below = from_above(adjoint_tail), from_below(adjoint_head)
+    whole, _, _ = lax.optimization_barrier((whole, adjoint_tail, adjoint_head))
+    (seen,) = kernel_call(
+        observe_kernel,
+        [padded],
+        [whole[0], crossed(whole[1], near), obs_tall],
+        flops=10**9,
+        name="observe",
+    )
     depth_tall = jnp.concatenate([above[-1, half:own_rows], depth_field, below[-1, :half]])
     wider = (own_rows + 2, own_members, width)
     depth_grad, *remaining = kernel_call(

time: 198 us -> 193 us (0.975)
  starting transfers between devices: 99.9 us -> 90.3 us
  waiting for transfers between devices: 51.1 us -> 58.2 us
  local copies, waits for them, and re-layouts: 7.89 us -> 4.32 us
    ppermute x14 -> x7, starting transfers between devices: 32 us -> 14.8 us  [turned(): lax.ppermute(block, 'ens', [(i, (i + distance) % count) for i in range(co...]
    ppermute x0 -> x4, waiting for transfers between devices: none -> 11.1 us  [crossed(): return lax.ppermute(block, 'ens', [(i, i ^ distance) for i in range(count)])]
    ppermute x0 -> x4, starting transfers between devices: none -> 7.72 us  [crossed(): return lax.ppermute(block, 'ens', [(i, i ^ distance) for i in range(count)])]
    unnamed x50 -> x30, local copies, waits for them, and re-layouts: 4.29 us -> 0.69 us
    ppermute x14 -> x7, waiting for transfers between devices: 10.1 us -> 7.78 us  [turned(): lax.ppermute(block, 'ens', [(i, (i + distance) % count) for i in range(co...]
  transfers between devices with their start and end apart: 39 -> 36, of which waited for: 20 -> 22; matrix products, arithmetic and copies ran while one was open for 1% -> 1% of each run, Pallas kernels for 16% -> 17%
where the time goes in v3:
time: 193 us; the launch traced here: 192 us
  starting transfers between devices  90.3 us (47%)
  waiting for transfers between devices  58.2 us (30%)
  Pallas kernels  35.2 us (18%)
  local copies, waits for them, and re-layouts  4.32 us (2%)
  other arithmetic  2.51 us (1%)
    pallas_call x10, Pallas kernels, kernel_call(): pl.pallas_call(body, out_shape=[made(i, o) for i, o in enumerate(outs)],...  35.2 us
    ppermute x3, starting transfers between devices, from_below(): lax.ppermute(rows_sent, 'space', [(i + 1, i) for i in range(count - 1)])  17.3 us
    ppermute x14, starting transfers between devices, other(): lax.ppermute(block, 'space', [(i, i ^ distance) for i in range(count)])  17.1 us
    ppermute x7, starting transfers between devices, turned(): lax.ppermute(block, 'ens', [(i, (i + distance) % count) for i in range(co...  14.8 us
    all_to_all x3, starting transfers between devices, exchanged(): return lax.all_to_all(blocks, 'ens', 0, 0, tiled=False)  14.6 us
    all_to_all x2, waiting for transfers between devices, gathered(): return lax.all_to_all(copies, axis, 0, 0, tiled=False)  14.4 us
    ppermute x14, waiting for transfers between devices, other(): lax.ppermute(block, 'space', [(i, i ^ distance) for i in range(count)])  13.4 us
    all_to_all x2, starting transfers between devices, gathered(): return lax.all_to_all(copies, axis, 0, 0, tiled=False)  13.1 us
  transfers between devices with their start and end apart: 36, of which 22 were waited for; matrix products, arithmetic and copies ran while one was open for 1% of the time, Pallas kernels for 17%

profile of v3, /device:TPU:6, one launch (start us, length us, event | category | flops | bytes accessed | tf_op | source)
XLA Modules:
  0.0 191.6 jit_solution(14422543773606059423)
XLA Ops:
  2.8 8.5 %all-to-all-start = ((f32[8,24,128]{2,1,0:T(8,128)}), f32[8,24,128]{2,1,0:T(8,128)S(1)}, u32[]{:S(2)}, u32[]{:S(2)}) async-start(f32[8,24,128]{2,1,0:T(8,128)} %broadcast_in_dim.7), calls=%async_computation | async-start | bytes 196608 | tf_op jit(solution)/shard_map/all_to_all | solution.py:50
  11.3 3.3 %prepare.1 = (f32[11,16,1024]{2,1,0:T(8,128)}, f32[11,16,1024]{2,1,0:T(8,128)}, f32[8,384,128]{2,1,0:T(8,128)}) custom-call(f32[3,8,16,1024]{3,2,1,0:T(8,128)} %state_ref.3, f32[8,1024]{1,0:T(8,128)} %depth_ref.3, f32[384,1024]{1,0:T(8,128)} %bitcast.47), custom_call_target="tpu_custom_call" | custom-call | bytes 6193152 | tf_op jit(solution)/shard_map/prepare/pallas_call | solution.py:30
  14.6 5.4 %all-to-all-done = f32[8,24,128]{2,1,0:T(8,128)S(1)} async-done(((f32[8,24,128]{2,1,0:T(8,128)}), f32[8,24,128]{2,1,0:T(8,128)S(1)}, u32[]{:S(2)}, u32[]{:S(2)}) %all-to-all-start) | async-done | bytes 98336 | tf_op jit(solution)/shard_map/all_to_all | solution.py:50
  20.0 3.7 %all-to-all-start.1 = ((f32[8,384,128]{2,1,0:T(8,128)}), f32[8,384,128]{2,1,0:T(8,128)S(1)}, u32[]{:S(2)}, u32[]{:S(2)}) async-start(f32[8,384,128]{2,1,0:T(8,128)} %get-tuple-element.62), calls=%async_computation.1 | async-start | bytes 3145728 | tf_op jit(solution)/shard_map/all_to_all | solution.py:44
  23.7 1.9 %collective-permute-start = (f32[11,16,1024]{2,1,0:T(8,128)}, f32[11,16,1024]{2,1,0:T(8,128)}, u32[]{:S(2)}, u32[]{:S(2)}) collective-permute-start(f32[11,16,1024]{2,1,0:T(8,128)} %get-tuple-element.48), channel_id=1, source_target_pairs={{0,1},{1,2},{2,3},{3,4},{4,5},{5,6},{6,7},{7,8},{8,9},{9,10},{10,1... | collective-permute-start | bytes 2162696 | tf_op jit(solution)/shard_map/ppermute | solution.py:83
  25.7 5.8 %collective-permute-start.1 = (f32[11,16,1024]{2,1,0:T(8,128)}, f32[11,16,1024]{2,1,0:T(8,128)}, u32[]{:S(2)}, u32[]{:S(2)}) collective-permute-start(f32[11,16,1024]{2,1,0:T(8,128)} %get-tuple-element.49), channel_id=1, source_target_pairs={{1,0},{2,1},{3,2},{4,3},{5,4},{6,5},{7,6},{8,7},{9,8},{10,9},{11,1... | collective-permute-start | bytes 2162696 | tf_op jit(solution)/shard_map/ppermute | solution.py:88
  31.8 7.0 %collective-permute-done.above_ref = f32[11,16,1024]{2,1,0:T(8,128)} collective-permute-done((f32[11,16,1024]{2,1,0:T(8,128)}, f32[11,16,1024]{2,1,0:T(8,128)}, u32[]{:S(2)}, u32[]{:S(2)}) %collective-permute-start) | collective-permute-done | bytes 720928 | tf_op jit(solution)/shard_map/ppermute | solution.py:83
  38.8 1.8 collective-permute-done.1.below_ref
  40.5 5.3 %forward.1 = (f32[8,24,16,128]{3,2,1,0:T(8,128)}, f32[4,16,128]{2,1,0:T(8,128)S(1)}, f32[8,16,1024]{2,1,0:T(8,128)}, f32[8,16,1024]{2,1,0:T(8,128)}, f32[8,16,1024]{2,1,0:T(8,128)}, /*index=5*/f32[8,16,1024]{2,1,0:T(8,128)}) custom-call(f32[16]{0:T(128)S(1)} %and_convert_fusion.inside_ref, f32[3,8,16,1024]{3,2,1,0:T(8,128)S(1)} %copy-done, ...), custom_call_target="tpu_custom_call" | custom-call | flops 100000000 | bytes 6752320 | tf_op jit(solution)/shard_map/forward/pallas_call | solution.py:30
  45.9 3.2 %collective-permute-start.8 = (f32[4,16,128]{2,1,0:T(8,128)S(1)}, f32[4,16,128]{2,1,0:T(8,128)S(1)}, u32[]{:S(2)}, u32[]{:S(2)}) collective-permute-start(f32[4,16,128]{2,1,0:T(8,128)S(1)} %get-tuple-element.52.refs_0_), channel_id=1, source_target_pairs={{0,224},{32,0},{64,32},{96,64},{128,96},{160,128},{192,160},{224,1... | collective-permute-start | bytes 98312 | tf_op jit(solution)/shard_map/ppermute | solution.py:55
  49.1 2.3 %collective-permute-start.7 = (f32[4,16,128]{2,1,0:T(8,128)S(1)}, f32[4,16,128]{2,1,0:T(8,128)S(1)}, u32[]{:S(2)}, u32[]{:S(2)}) collective-permute-start(f32[4,16,128]{2,1,0:T(8,128)S(1)} %get-tuple-element.52.refs_0_), channel_id=1, source_target_pairs={{0,192},{32,224},{64,0},{96,32},{128,64},{160,96},{192,128},{224,1... | collective-permute-start | bytes 98312 | tf_op jit(solution)/shard_map/ppermute | solution.py:55
  51.4 1.4 collective-permute-start.6
  52.9 3.6 %collective-permute-start.5 = (f32[4,16,128]{2,1,0:T(8,128)S(1)}, f32[4,16,128]{2,1,0:T(8,128)S(1)}, u32[]{:S(2)}, u32[]{:S(2)}) collective-permute-start(f32[4,16,128]{2,1,0:T(8,128)S(1)} %get-tuple-element.52.refs_0_), channel_id=1, source_target_pairs={{0,128},{32,160},{64,192},{96,224},{128,0},{160,32},{192,64},{224,... | collective-permute-start | bytes 98312 | tf_op jit(solution)/shard_map/ppermute | solution.py:55
  56.7 5.8 %collective-permute-done.8.refs_7_ = f32[4,16,128]{2,1,0:T(8,128)S(1)} collective-permute-done((f32[4,16,128]{2,1,0:T(8,128)S(1)}, f32[4,16,128]{2,1,0:T(8,128)S(1)}, u32[]{:S(2)}, u32[]{:S(2)}) %collective-permute-start.8) | collective-permute-done | bytes 32800 | tf_op jit(solution)/shard_map/ppermute | solution.py:55
  62.5 4.0 %collective-permute-start.2 = (f32[4,16,128]{2,1,0:T(8,128)S(1)}, f32[4,16,128]{2,1,0:T(8,128)S(1)}, u32[]{:S(2)}, u32[]{:S(2)}) collective-permute-start(f32[4,16,128]{2,1,0:T(8,128)S(1)} %get-tuple-element.52.refs_0_), channel_id=1, source_target_pairs={{0,32},{32,64},{64,96},{96,128},{128,160},{160,192},{192,224},{224... | collective-permute-start | bytes 98312 | tf_op jit(solution)/shard_map/ppermute | solution.py:55
  66.5 2.0 %collective-permute-done.3.refs_2_ = f32[4,16,128]{2,1,0:T(8,128)S(1)} collective-permute-done((f32[4,16,128]{2,1,0:T(8,128)S(1)}, f32[4,16,128]{2,1,0:T(8,128)S(1)}, u32[]{:S(2)}, u32[]{:S(2)}) %collective-permute-start.3) | collective-permute-done | bytes 32800 | tf_op jit(solution)/shard_map/ppermute | solution.py:55
  69.1 5.9 %all-to-all-start.3 = ((f32[8,24,16,128]{3,2,1,0:T(8,128)}), f32[8,24,16,128]{3,2,1,0:T(8,128)}, u32[]{:S(2)}, u32[]{:S(2)}) async-start(f32[8,24,16,128]{3,2,1,0:T(8,128)} %get-tuple-element.63), calls=%async_computation.3 | async-start | bytes 3145728 | tf_op jit(solution)/shard_map/all_to_all | solution.py:44
  75.2 2.0 %gram.1 = (f32[4,128,128]{2,1,0:T(8,128)S(1)}, f32[4,8,128]{2,1,0:T(8,128)S(1)}, f32[136,128]{1,0:T(8,128)S(1)}) custom-call(s32[1]{0:T(128)} %bitcast.place_ref, f32[3,4,128]{2,1,0:T(4,128)S(1)} %reshape.25.params_ref, f32[4,16,128]{2,1,0:T(8,128)} %copy-done.6, f32[4,16,128]{2,1,0:T(8,128)} %copy-done.13, f32[4,16,128]{2,1,0:T(8,128)} %copy-done.12, ...), custom_call_target="tpu_custom_call" | custom-call | flops 100663296 | bytes 616452 | tf_op jit(solution)/shard_map/gram/pallas_call | solution.py:30
  78.5 3.0 %collective-permute-start.12 = (f32[136,128]{1,0:T(8,128)S(1)}, f32[136,128]{1,0:T(8,128)S(1)}, u32[]{:S(2)}, u32[]{:S(2)}) collective-permute-start(f32[136,128]{1,0:T(8,128)S(1)} %add.62), channel_id=1, source_target_pairs={{0,6},{1,7},{2,4},{3,5},{4,2},{5,3},{6,0},{7,1},{8,14},{9,15},{10,... | collective-permute-start | bytes 208904 | tf_op jit(solution)/shard_map/ppermute | solution.py:67
  82.7 2.1 %collective-permute-done.12 = f32[136,128]{1,0:T(8,128)S(1)} collective-permute-done((f32[136,128]{1,0:T(8,128)S(1)}, f32[136,128]{1,0:T(8,128)S(1)}, u32[]{:S(2)}, u32[]{:S(2)}) %collective-permute-start.12) | collective-permute-done | bytes 69664 | tf_op jit(solution)/shard_map/ppermute | solution.py:67
  84.9 2.9 %collective-permute-done.11 = f32[136,128]{1,0:T(8,128)S(1)} collective-permute-done((f32[136,128]{1,0:T(8,128)S(1)}, f32[136,128]{1,0:T(8,128)S(1)}, u32[]{:S(2)}, u32[]{:S(2)}) %collective-permute-start.11) | collective-permute-done | bytes 69664 | tf_op jit(solution)/shard_map/ppermute | solution.py:67
  88.6 2.4 %collective-permute-start.14 = (f32[136,128]{1,0:T(8,128)S(1)}, f32[136,128]{1,0:T(8,128)S(1)}, u32[]{:S(2)}, u32[]{:S(2)}) collective-permute-start(f32[136,128]{1,0:T(8,128)S(1)} %add_add_fusion.1), channel_id=1, source_target_pairs={{0,16},{1,17},{2,18},{3,19},{4,20},{5,21},{6,22},{7,23},{8,24},{9,... | collective-permute-start | bytes 208904 | tf_op jit(solution)/shard_map/ppermute | solution.py:67
  92.2 1.4 collective-permute-done.15
  95.4 11.2 %factor.1 = (f32[128,128]{1,0:T(8,128)S(1)}, f32[128,128]{1,0:T(8,128)S(1)}, f32[8,128]{1,0:T(8,128)S(1)}) custom-call(f32[136,128]{1,0:T(8,128)S(1)} %add_add_fusion.gram_ref), custom_call_target="tpu_custom_call" | custom-call | flops 1000000000 | bytes 204800 | tf_op jit(solution)/shard_map/factor/pallas_call | solution.py:30
  106.6 2.2 %mix.1 = f32[8,24,16,128]{3,2,1,0:T(8,128)} custom-call(f32[128,128]{1,0:T(8,128)S(1)} %get-tuple-element.61.mixing_ref, f32[8,24,16,128]{3,2,1,0:T(8,128)S(1)} %bitcast.45), custom_call_target="tpu_custom_call" | custom-call | flops 10000000000 | bytes 3211264 | tf_op jit(solution)/shard_map/mix/pallas_call | solution.py:30
  108.8 2.3 %all-to-all-done.3.state_ref = f32[8,24,16,128]{3,2,1,0:T(8,128)} async-done(((f32[8,24,16,128]{3,2,1,0:T(8,128)}), f32[8,24,16,128]{3,2,1,0:T(8,128)}, u32[]{:S(2)}, u32[]{:S(2)}) %all-to-all-start.3) | async-done | bytes 1572896 | tf_op jit(solution)/shard_map/all_to_all | solution.py:44
  111.1 4.9 %all-to-all-start.2 = ((f32[8,24,16,128]{3,2,1,0:T(8,128)}), f32[8,24,16,128]{3,2,1,0:T(8,128)S(1)}, u32[]{:S(2)}, u32[]{:S(2)}) async-start(f32[8,24,16,128]{3,2,1,0:T(8,128)} %mix.1), calls=%async_computation.2 | async-start | bytes 3145728 | tf_op jit(solution)/shard_map/all_to_all | solution.py:44
  116.8 3.5 %cross.1 = f32[128,128]{1,0:T(8,128)S(1)} custom-call(f32[8,24,16,128]{3,2,1,0:T(8,128)} %all-to-all-done.3.state_ref, f32[8,24,16,128]{3,2,1,0:T(8,128)S(1)} %bitcast.46), custom_call_target="tpu_custom_call" | custom-call | flops 10000000000 | bytes 3211264 | tf_op jit(solution)/shard_map/cross/pallas_call | solution.py:30
  121.7 1.4 collective-permute-start.19
  123.0 1.7 collective-permute-start.18
  126.0 1.9 %collective-permute-start.23 = (f32[4,136,64]{2,1,0:T(8,128)S(1)}, f32[4,136,64]{2,1,0:T(8,128)S(1)}, u32[]{:S(2)}, u32[]{:S(2)}) collective-permute-start(f32[4,136,64]{2,1,0:T(8,128)S(1)} %get-tuple-element.96), channel_id=1, source_target_pairs={{0,1},{1,2},{2,3},{3,4},{4,5},{5,6},{6,7},{7,8},{8,9},{9,10},{10,1... | collective-permute-start | bytes 417800 | tf_op jit(solution)/shard_map/ppermute | solution.py:83
  127.9 5.8 %collective-permute-start.24 = (f32[4,136,64]{2,1,0:T(8,128)S(1)}, f32[4,136,64]{2,1,0:T(8,128)S(1)}, u32[]{:S(2)}, u32[]{:S(2)}) collective-permute-start(f32[4,136,64]{2,1,0:T(8,128)S(1)} %get-tuple-element.97), channel_id=1, source_target_pairs={{1,0},{2,1},{3,2},{4,3},{5,4},{6,5},{7,6},{8,7},{9,8},{10,9},{11,1... | collective-permute-start | bytes 417800 | tf_op jit(solution)/shard_map/ppermute | solution.py:88
  133.8 3.2 %collective-permute-start.21 = (f32[128,128]{1,0:T(8,128)S(1)}, f32[128,128]{1,0:T(8,128)S(1)}, u32[]{:S(2)}, u32[]{:S(2)}) collective-permute-start(f32[128,128]{1,0:T(8,128)S(1)} %add_add_fusion.3), channel_id=1, source_target_pairs={{0,16},{1,17},{2,18},{3,19},{4,20},{5,21},{6,22},{7,23},{8,24},{9,... | collective-permute-start | bytes 196616 | tf_op jit(solution)/shard_map/ppermute | solution.py:67
  139.3 1.9 collective-permute-done.21
  141.3 1.3 pullback.1
  142.6 2.1 %collective-permute-start.25 = (f32[2,40,128]{2,1,0:T(8,128)S(1)}, f32[2,40,128]{2,1,0:T(8,128)S(1)}, u32[]{:S(2)}, u32[]{:S(2)}) collective-permute-start(f32[2,40,128]{2,1,0:T(8,128)S(1)} %get-tuple-element.72), channel_id=1, source_target_pairs={{0,32},{32,0},{64,96},{96,64},{128,160},{160,128},{192,224},{224,1... | collective-permute-start | bytes 122888 | tf_op jit(solution)/shard_map/ppermute | solution.py:60
  144.7 2.4 %collective-permute-start.26 = (f32[2,40,128]{2,1,0:T(8,128)S(1)}, f32[2,40,128]{2,1,0:T(8,128)S(1)}, u32[]{:S(2)}, u32[]{:S(2)}) collective-permute-start(f32[2,40,128]{2,1,0:T(8,128)S(1)} %get-tuple-element.73), channel_id=1, source_target_pairs={{0,64},{32,96},{64,0},{96,32},{128,192},{160,224},{192,128},{224,1... | collective-permute-start | bytes 122888 | tf_op jit(solution)/shard_map/ppermute | solution.py:60
  147.9 3.6 %collective-permute-done.25 = f32[2,40,128]{2,1,0:T(8,128)S(1)} collective-permute-done((f32[2,40,128]{2,1,0:T(8,128)S(1)}, f32[2,40,128]{2,1,0:T(8,128)S(1)}, u32[]{:S(2)}, u32[]{:S(2)}) %collective-permute-start.25) | collective-permute-done | bytes 40992 | tf_op jit(solution)/shard_map/ppermute | solution.py:60
  151.5 1.8 collective-permute-done.26
  154.5 1.9 %collective-permute-start.28 = (f32[8,144,128]{2,1,0:T(8,128)S(1)}, f32[8,144,128]{2,1,0:T(8,128)S(1)}, u32[]{:S(2)}, u32[]{:S(2)}) collective-permute-start(f32[8,144,128]{2,1,0:T(8,128)S(1)} %pad_maximum_fusion), channel_id=1, source_target_pairs={{0,1},{1,2},{2,3},{3,4},{4,5},{5,6},{6,7},{7,8},{8,9},{9,10},{10,1... | collective-permute-start | bytes 1769480 | tf_op jit(solution)/shard_map/ppermute | solution.py:83
  156.5 5.8 %collective-permute-start.29 = (f32[8,144,128]{2,1,0:T(8,128)S(1)}, f32[8,144,128]{2,1,0:T(8,128)S(1)}, u32[]{:S(2)}, u32[]{:S(2)}) collective-permute-start(f32[8,144,128]{2,1,0:T(8,128)S(1)} %pad_maximum_fusion.1), channel_id=1, source_target_pairs={{1,0},{2,1},{3,2},{4,3},{5,4},{6,5},{7,6},{8,7},{9,8},{10,9},{11,1... | collective-permute-start | bytes 1769480 | tf_op jit(solution)/shard_map/ppermute | solution.py:88
  162.3 3.1 %collective-permute-start.30 = (f32[40,128]{1,0:T(8,128)S(1)}, f32[40,128]{1,0:T(8,128)S(1)}, u32[]{:S(2)}, u32[]{:S(2)}) collective-permute-start(f32[40,128]{1,0:T(8,128)S(1)} %get-tuple-element.98), channel_id=1, source_target_pairs={{0,128},{32,160},{64,192},{96,224},{128,0},{160,32},{192,64},{224,... | collective-permute-start | bytes 61448 | tf_op jit(solution)/shard_map/ppermute | solution.py:60
  165.5 4.6 %collective-permute-done.30.refs_1_ = f32[40,128]{1,0:T(8,128)S(1)} collective-permute-done((f32[40,128]{1,0:T(8,128)S(1)}, f32[40,128]{1,0:T(8,128)S(1)}, u32[]{:S(2)}, u32[]{:S(2)}) %collective-permute-start.30) | collective-permute-done | bytes 20512 | tf_op jit(solution)/shard_map/ppermute | solution.py:60
  170.1 2.2 %observe.1.seen_ref = f32[16,16,1024]{2,1,0:T(8,128)S(1)} custom-call(f32[40,128]{1,0:T(8,128)S(1)} %get-tuple-element.99.refs_0_, f32[40,128]{1,0:T(8,128)S(1)} %collective-permute-done.30.refs_1_, f32[8,136,128]{2,1,0:T(8,128)S(1)} %maximum_maximum_fusion.refs_2_), custom_call_target="tpu_custom_call" | custom-call | flops 1000000000 | bytes 1646592 | tf_op jit(solution)/shard_map/observe/pallas_call | solution.py:30
  172.4 2.7 %backward.1 = (f32[8,1024]{1,0:T(8,128)S(1)}, f32[10,16,1024]{2,1,0:T(8,128)S(1)}, f32[8,16,1024]{2,1,0:T(8,128)S(1)}, f32[10,16,1024]{2,1,0:T(8,128)S(1)}) custom-call(f32[16]{0:T(128)S(1)} %and_convert_fusion.inside_ref, f32[8,24,16,128]{3,2,1,0:T(8,128)S(1)} %all-to-all-done.2.back_ref, f32[8,144,128]{2,1,0:T(8,128)S(1)} %collective-permute-done.28.above_ref, ...), custom_call_target="tpu_custom_call" | custom-call | flops 100000000 | bytes 7831616 | tf_op jit(solution)/shard_map/backward/pallas_call | solution.py:30
  175.9 4.6 %all-to-all-start.4 = ((f32[8,8,1024]{2,1,0:T(8,128)}), f32[8,8,1024]{2,1,0:T(8,128)S(1)}, u32[]{:S(2)}, u32[]{:S(2)}) async-start(f32[8,8,1024]{2,1,0:T(8,128)} %broadcast_in_dim.8), calls=%async_computation.4 | async-start | bytes 524288 | tf_op jit(solution)/shard_map/all_to_all | solution.py:50
  180.5 1.5 finish.1
  181.9 9.0 %all-to-all-done.4 = f32[8,8,1024]{2,1,0:T(8,128)S(1)} async-done(((f32[8,8,1024]{2,1,0:T(8,128)}), f32[8,8,1024]{2,1,0:T(8,128)S(1)}, u32[]{:S(2)}, u32[]{:S(2)}) %all-to-all-start.4) | async-done | bytes 262176 | tf_op jit(solution)/shard_map/all_to_all | solution.py:50
  (97 shorter events, 19.1 us)
Async XLA Ops:
  2.8 17.2 %all-to-all-start = ((f32[8,24,128]{2,1,0:T(8,128)}), f32[8,24,128]{2,1,0:T(8,128)S(1)}, u32[]{:S(2)}, u32[]{:S(2)}) async-start(f32[8,24,128]{2,1,0:T(8,128)} %broadcast_in_dim.7), calls=%async_computation | async-start | bytes 196608 | tf_op jit(solution)/shard_map/all_to_all | solution.py:50
  20.0 20.5 %copy-start = (f32[3,8,16,1024]{3,2,1,0:T(8,128)S(1)}, f32[3,8,16,1024]{3,2,1,0:T(8,128)}, u32[]{:S(2)}) copy-start(f32[3,8,16,1024]{3,2,1,0:T(8,128)} %state_ref.3) | copy-start | bytes 4718596
  20.0 20.5 %copy-start.5 = (f32[8,1024]{1,0:T(8,128)S(1)}, f32[8,1024]{1,0:T(8,128)}, u32[]{:S(2)}) copy-start(f32[8,1024]{1,0:T(8,128)} %depth_ref.3) | copy-start | bytes 98308
  20.0 48.5 %all-to-all-start.1 = ((f32[8,384,128]{2,1,0:T(8,128)}), f32[8,384,128]{2,1,0:T(8,128)S(1)}, u32[]{:S(2)}, u32[]{:S(2)}) async-start(f32[8,384,128]{2,1,0:T(8,128)} %get-tuple-element.62), calls=%async_computation.1 | async-start | bytes 3145728 | tf_op jit(solution)/shard_map/all_to_all | solution.py:44
  23.7 15.0 %collective-permute-start = (f32[11,16,1024]{2,1,0:T(8,128)}, f32[11,16,1024]{2,1,0:T(8,128)}, u32[]{:S(2)}, u32[]{:S(2)}) collective-permute-start(f32[11,16,1024]{2,1,0:T(8,128)} %get-tuple-element.48), channel_id=1, source_target_pairs={{0,1},{1,2},{2,3},{3,4},{4,5},{5,6},{6,7},{7,8},{8,9},{9,10},{10,1... | collective-permute-start | bytes 2162696 | tf_op jit(solution)/shard_map/ppermute | solution.py:83
  25.7 14.9 %collective-permute-start.1 = (f32[11,16,1024]{2,1,0:T(8,128)}, f32[11,16,1024]{2,1,0:T(8,128)}, u32[]{:S(2)}, u32[]{:S(2)}) collective-permute-start(f32[11,16,1024]{2,1,0:T(8,128)} %get-tuple-element.49), channel_id=1, source_target_pairs={{1,0},{2,1},{3,2},{4,3},{5,4},{6,5},{7,6},{8,7},{9,8},{10,9},{11,1... | collective-permute-start | bytes 2162696 | tf_op jit(solution)/shard_map/ppermute | solution.py:88
  45.8 22.7 %copy-start.6 = (f32[4,16,128]{2,1,0:T(8,128)}, f32[4,16,128]{2,1,0:T(8,128)S(1)}, u32[]{:S(2)}) copy-start(f32[4,16,128]{2,1,0:T(8,128)S(1)} %get-tuple-element.52.refs_0_) | copy-start | bytes 98308
  45.9 16.6 %collective-permute-start.8 = (f32[4,16,128]{2,1,0:T(8,128)S(1)}, f32[4,16,128]{2,1,0:T(8,128)S(1)}, u32[]{:S(2)}, u32[]{:S(2)}) collective-permute-start(f32[4,16,128]{2,1,0:T(8,128)S(1)} %get-tuple-element.52.refs_0_), channel_id=1, source_target_pairs={{0,224},{32,0},{64,32},{96,64},{128,96},{160,128},{192,160},{224,1... | collective-permute-start | bytes 98312 | tf_op jit(solution)/shard_map/ppermute | solution.py:55
  49.1 13.4 %collective-permute-start.7 = (f32[4,16,128]{2,1,0:T(8,128)S(1)}, f32[4,16,128]{2,1,0:T(8,128)S(1)}, u32[]{:S(2)}, u32[]{:S(2)}) collective-permute-start(f32[4,16,128]{2,1,0:T(8,128)S(1)} %get-tuple-element.52.refs_0_), channel_id=1, source_target_pairs={{0,192},{32,224},{64,0},{96,32},{128,64},{160,96},{192,128},{224,1... | collective-permute-start | bytes 98312 | tf_op jit(solution)/shard_map/ppermute | solution.py:55
  51.4 15.0 %collective-permute-start.6 = (f32[4,16,128]{2,1,0:T(8,128)S(1)}, f32[4,16,128]{2,1,0:T(8,128)S(1)}, u32[]{:S(2)}, u32[]{:S(2)}) collective-permute-start(f32[4,16,128]{2,1,0:T(8,128)S(1)} %get-tuple-element.52.refs_0_), channel_id=1, source_target_pairs={{0,160},{32,192},{64,224},{96,0},{128,32},{160,64},{192,96},{224,1... | collective-permute-start | bytes 98312 | tf_op jit(solution)/shard_map/ppermute | solution.py:55
  52.9 13.6 %collective-permute-start.5 = (f32[4,16,128]{2,1,0:T(8,128)S(1)}, f32[4,16,128]{2,1,0:T(8,128)S(1)}, u32[]{:S(2)}, u32[]{:S(2)}) collective-permute-start(f32[4,16,128]{2,1,0:T(8,128)S(1)} %get-tuple-element.52.refs_0_), channel_id=1, source_target_pairs={{0,128},{32,160},{64,192},{96,224},{128,0},{160,32},{192,64},{224,... | collective-permute-start | bytes 98312 | tf_op jit(solution)/shard_map/ppermute | solution.py:55
  56.5 10.0 %collective-permute-start.4 = (f32[4,16,128]{2,1,0:T(8,128)S(1)}, f32[4,16,128]{2,1,0:T(8,128)S(1)}, u32[]{:S(2)}, u32[]{:S(2)}) collective-permute-start(f32[4,16,128]{2,1,0:T(8,128)S(1)} %get-tuple-element.52.refs_0_), channel_id=1, source_target_pairs={{0,96},{32,128},{64,160},{96,192},{128,224},{160,0},{192,32},{224,... | collective-permute-start | bytes 98312 | tf_op jit(solution)/shard_map/ppermute | solution.py:55
  62.5 6.1 %copy-start.7 = (f32[4,16,128]{2,1,0:T(8,128)}, f32[4,16,128]{2,1,0:T(8,128)S(1)}, u32[]{:S(2)}) copy-start(f32[4,16,128]{2,1,0:T(8,128)S(1)} %collective-permute-done.8.refs_7_) | copy-start | bytes 98308
  62.5 6.0 %collective-permute-start.3 = (f32[4,16,128]{2,1,0:T(8,128)S(1)}, f32[4,16,128]{2,1,0:T(8,128)S(1)}, u32[]{:S(2)}, u32[]{:S(2)}) collective-permute-start(f32[4,16,128]{2,1,0:T(8,128)S(1)} %get-tuple-element.52.refs_0_), channel_id=1, source_target_pairs={{0,64},{32,96},{64,128},{96,160},{128,192},{160,224},{192,0},{224,... | collective-permute-start | bytes 98312 | tf_op jit(solution)/shard_map/ppermute | solution.py:55
  62.5 6.1 %copy-start.8 = (f32[4,16,128]{2,1,0:T(8,128)}, f32[4,16,128]{2,1,0:T(8,128)S(1)}, u32[]{:S(2)}) copy-start(f32[4,16,128]{2,1,0:T(8,128)S(1)} %collective-permute-done.7.refs_6_) | copy-start | bytes 98308
  62.5 6.0 %collective-permute-start.2 = (f32[4,16,128]{2,1,0:T(8,128)S(1)}, f32[4,16,128]{2,1,0:T(8,128)S(1)}, u32[]{:S(2)}, u32[]{:S(2)}) collective-permute-start(f32[4,16,128]{2,1,0:T(8,128)S(1)} %get-tuple-element.52.refs_0_), channel_id=1, source_target_pairs={{0,32},{32,64},{64,96},{96,128},{128,160},{160,192},{192,224},{224... | collective-permute-start | bytes 98312 | tf_op jit(solution)/shard_map/ppermute | solution.py:55
  66.4 2.1 %copy-start.9 = (f32[4,16,128]{2,1,0:T(8,128)}, f32[4,16,128]{2,1,0:T(8,128)S(1)}, u32[]{:S(2)}) copy-start(f32[4,16,128]{2,1,0:T(8,128)S(1)} %collective-permute-done.6.refs_5_) | copy-start | bytes 98308
  66.4 2.1 %copy-start.10 = (f32[4,16,128]{2,1,0:T(8,128)}, f32[4,16,128]{2,1,0:T(8,128)S(1)}, u32[]{:S(2)}) copy-start(f32[4,16,128]{2,1,0:T(8,128)S(1)} %collective-permute-done.5.refs_4_) | copy-start | bytes 98308
  66.5 2.1 %copy-start.11 = (f32[4,16,128]{2,1,0:T(8,128)}, f32[4,16,128]{2,1,0:T(8,128)S(1)}, u32[]{:S(2)}) copy-start(f32[4,16,128]{2,1,0:T(8,128)S(1)} %collective-permute-done.4.refs_3_) | copy-start | bytes 98308
  69.1 42.0 %all-to-all-start.3 = ((f32[8,24,16,128]{3,2,1,0:T(8,128)}), f32[8,24,16,128]{3,2,1,0:T(8,128)}, u32[]{:S(2)}, u32[]{:S(2)}) async-start(f32[8,24,16,128]{3,2,1,0:T(8,128)} %get-tuple-element.63), calls=%async_computation.3 | async-start | bytes 3145728 | tf_op jit(solution)/shard_map/all_to_all | solution.py:44
  77.2 1.3 collective-permute-start.9
  78.5 6.3 %collective-permute-start.12 = (f32[136,128]{1,0:T(8,128)S(1)}, f32[136,128]{1,0:T(8,128)S(1)}, u32[]{:S(2)}, u32[]{:S(2)}) collective-permute-start(f32[136,128]{1,0:T(8,128)S(1)} %add.62), channel_id=1, source_target_pairs={{0,6},{1,7},{2,4},{3,5},{4,2},{5,3},{6,0},{7,1},{8,14},{9,15},{10,... | collective-permute-start | bytes 208904 | tf_op jit(solution)/shard_map/ppermute | solution.py:67
  81.6 6.2 %collective-permute-start.11 = (f32[136,128]{1,0:T(8,128)S(1)}, f32[136,128]{1,0:T(8,128)S(1)}, u32[]{:S(2)}, u32[]{:S(2)}) collective-permute-start(f32[136,128]{1,0:T(8,128)S(1)} %add.62), channel_id=1, source_target_pairs={{0,4},{1,5},{2,6},{3,7},{4,0},{5,1},{6,2},{7,3},{8,12},{9,13},{10,... | collective-permute-start | bytes 208904 | tf_op jit(solution)/shard_map/ppermute | solution.py:67
  82.3 5.5 %collective-permute-start.10 = (f32[136,128]{1,0:T(8,128)S(1)}, f32[136,128]{1,0:T(8,128)S(1)}, u32[]{:S(2)}, u32[]{:S(2)}) collective-permute-start(f32[136,128]{1,0:T(8,128)S(1)} %add.62), channel_id=1, source_target_pairs={{0,2},{1,3},{2,0},{3,1},{4,6},{5,7},{6,4},{7,5},{8,10},{9,11},{10,... | collective-permute-start | bytes 208904 | tf_op jit(solution)/shard_map/ppermute | solution.py:67
  87.8 5.8 %collective-permute-start.15 = (f32[136,128]{1,0:T(8,128)S(1)}, f32[136,128]{1,0:T(8,128)S(1)}, u32[]{:S(2)}, u32[]{:S(2)}) collective-permute-start(f32[136,128]{1,0:T(8,128)S(1)} %add_add_fusion.1), channel_id=1, source_target_pairs={{0,24},{1,25},{2,26},{3,27},{4,28},{5,29},{6,30},{7,31},{8,16},{9,... | collective-permute-start | bytes 208904 | tf_op jit(solution)/shard_map/ppermute | solution.py:67
  88.6 5.8 %collective-permute-start.14 = (f32[136,128]{1,0:T(8,128)S(1)}, f32[136,128]{1,0:T(8,128)S(1)}, u32[]{:S(2)}, u32[]{:S(2)}) collective-permute-start(f32[136,128]{1,0:T(8,128)S(1)} %add_add_fusion.1), channel_id=1, source_target_pairs={{0,16},{1,17},{2,18},{3,19},{4,20},{5,21},{6,22},{7,23},{8,24},{9,... | collective-permute-start | bytes 208904 | tf_op jit(solution)/shard_map/ppermute | solution.py:67
  91.0 4.3 %collective-permute-start.13 = (f32[136,128]{1,0:T(8,128)S(1)}, f32[136,128]{1,0:T(8,128)S(1)}, u32[]{:S(2)}, u32[]{:S(2)}) collective-permute-start(f32[136,128]{1,0:T(8,128)S(1)} %add_add_fusion.1), channel_id=1, source_target_pairs={{0,8},{1,9},{2,10},{3,11},{4,12},{5,13},{6,14},{7,15},{8,0},{9,1},... | collective-permute-start | bytes 208904 | tf_op jit(solution)/shard_map/ppermute | solution.py:67
  111.1 43.3 %all-to-all-start.2 = ((f32[8,24,16,128]{3,2,1,0:T(8,128)}), f32[8,24,16,128]{3,2,1,0:T(8,128)S(1)}, u32[]{:S(2)}, u32[]{:S(2)}) async-start(f32[8,24,16,128]{3,2,1,0:T(8,128)} %mix.1), calls=%async_computation.2 | async-start | bytes 3145728 | tf_op jit(solution)/shard_map/all_to_all | solution.py:44
  120.3 1.3 collective-permute-start.16
  121.7 12.0 %collective-permute-start.19 = (f32[128,128]{1,0:T(8,128)S(1)}, f32[128,128]{1,0:T(8,128)S(1)}, u32[]{:S(2)}, u32[]{:S(2)}) collective-permute-start(f32[128,128]{1,0:T(8,128)S(1)} %add.69), channel_id=1, source_target_pairs={{0,6},{1,7},{2,4},{3,5},{4,2},{5,3},{6,0},{7,1},{8,14},{9,15},{10,... | collective-permute-start | bytes 196616 | tf_op jit(solution)/shard_map/ppermute | solution.py:67
  123.0 10.6 %collective-permute-start.18 = (f32[128,128]{1,0:T(8,128)S(1)}, f32[128,128]{1,0:T(8,128)S(1)}, u32[]{:S(2)}, u32[]{:S(2)}) collective-permute-start(f32[128,128]{1,0:T(8,128)S(1)} %add.69), channel_id=1, source_target_pairs={{0,4},{1,5},{2,6},{3,7},{4,0},{5,1},{6,2},{7,3},{8,12},{9,13},{10,... | collective-permute-start | bytes 196616 | tf_op jit(solution)/shard_map/ppermute | solution.py:67
  124.7 8.9 %collective-permute-start.17 = (f32[128,128]{1,0:T(8,128)S(1)}, f32[128,128]{1,0:T(8,128)S(1)}, u32[]{:S(2)}, u32[]{:S(2)}) collective-permute-start(f32[128,128]{1,0:T(8,128)S(1)} %add.69), channel_id=1, source_target_pairs={{0,2},{1,3},{2,0},{3,1},{4,6},{5,7},{6,4},{7,5},{8,10},{9,11},{10,... | collective-permute-start | bytes 196616 | tf_op jit(solution)/shard_map/ppermute | solution.py:67
  126.0 11.9 %collective-permute-start.23 = (f32[4,136,64]{2,1,0:T(8,128)S(1)}, f32[4,136,64]{2,1,0:T(8,128)S(1)}, u32[]{:S(2)}, u32[]{:S(2)}) collective-permute-start(f32[4,136,64]{2,1,0:T(8,128)S(1)} %get-tuple-element.96), channel_id=1, source_target_pairs={{0,1},{1,2},{2,3},{3,4},{4,5},{5,6},{6,7},{7,8},{8,9},{9,10},{10,1... | collective-permute-start | bytes 417800 | tf_op jit(solution)/shard_map/ppermute | solution.py:83
  127.9 10.4 %collective-permute-start.24 = (f32[4,136,64]{2,1,0:T(8,128)S(1)}, f32[4,136,64]{2,1,0:T(8,128)S(1)}, u32[]{:S(2)}, u32[]{:S(2)}) collective-permute-start(f32[4,136,64]{2,1,0:T(8,128)S(1)} %get-tuple-element.97), channel_id=1, source_target_pairs={{1,0},{2,1},{3,2},{4,3},{5,4},{6,5},{7,6},{8,7},{9,8},{10,9},{11,1... | collective-permute-start | bytes 417800 | tf_op jit(solution)/shard_map/ppermute | solution.py:88
  133.7 5.6 %collective-permute-start.22 = (f32[128,128]{1,0:T(8,128)S(1)}, f32[128,128]{1,0:T(8,128)S(1)}, u32[]{:S(2)}, u32[]{:S(2)}) collective-permute-start(f32[128,128]{1,0:T(8,128)S(1)} %add_add_fusion.3), channel_id=1, source_target_pairs={{0,24},{1,25},{2,26},{3,27},{4,28},{5,29},{6,30},{7,31},{8,16},{9,... | collective-permute-start | bytes 196616 | tf_op jit(solution)/shard_map/ppermute | solution.py:67
  133.8 7.4 %collective-permute-start.21 = (f32[128,128]{1,0:T(8,128)S(1)}, f32[128,128]{1,0:T(8,128)S(1)}, u32[]{:S(2)}, u32[]{:S(2)}) collective-permute-start(f32[128,128]{1,0:T(8,128)S(1)} %add_add_fusion.3), channel_id=1, source_target_pairs={{0,16},{1,17},{2,18},{3,19},{4,20},{5,21},{6,22},{7,23},{8,24},{9,... | collective-permute-start | bytes 196616 | tf_op jit(solution)/shard_map/ppermute | solution.py:67
  137.0 4.3 %collective-permute-start.20 = (f32[128,128]{1,0:T(8,128)S(1)}, f32[128,128]{1,0:T(8,128)S(1)}, u32[]{:S(2)}, u32[]{:S(2)}) collective-permute-start(f32[128,128]{1,0:T(8,128)S(1)} %add_add_fusion.3), channel_id=1, source_target_pairs={{0,8},{1,9},{2,10},{3,11},{4,12},{5,13},{6,14},{7,15},{8,0},{9,1},... | collective-permute-start | bytes 196616 | tf_op jit(solution)/shard_map/ppermute | solution.py:67
  142.6 8.9 %collective-permute-start.25 = (f32[2,40,128]{2,1,0:T(8,128)S(1)}, f32[2,40,128]{2,1,0:T(8,128)S(1)}, u32[]{:S(2)}, u32[]{:S(2)}) collective-permute-start(f32[2,40,128]{2,1,0:T(8,128)S(1)} %get-tuple-element.72), channel_id=1, source_target_pairs={{0,32},{32,0},{64,96},{96,64},{128,160},{160,128},{192,224},{224,1... | collective-permute-start | bytes 122888 | tf_op jit(solution)/shard_map/ppermute | solution.py:60
  144.7 8.6 %collective-permute-start.26 = (f32[2,40,128]{2,1,0:T(8,128)S(1)}, f32[2,40,128]{2,1,0:T(8,128)S(1)}, u32[]{:S(2)}, u32[]{:S(2)}) collective-permute-start(f32[2,40,128]{2,1,0:T(8,128)S(1)} %get-tuple-element.73), channel_id=1, source_target_pairs={{0,64},{32,96},{64,0},{96,32},{128,192},{160,224},{192,128},{224,1... | collective-permute-start | bytes 122888 | tf_op jit(solution)/shard_map/ppermute | solution.py:60
  147.1 7.3 %collective-permute-start.27 = (f32[2,40,128]{2,1,0:T(8,128)S(1)}, f32[2,40,128]{2,1,0:T(8,128)S(1)}, u32[]{:S(2)}, u32[]{:S(2)}) collective-permute-start(f32[2,40,128]{2,1,0:T(8,128)S(1)} %get-tuple-element.74), channel_id=1, source_target_pairs={{0,96},{32,64},{64,32},{96,0},{128,224},{160,192},{192,160},{224,1... | collective-permute-start | bytes 122888 | tf_op jit(solution)/shard_map/ppermute | solution.py:60
  154.5 17.8 %collective-permute-start.28 = (f32[8,144,128]{2,1,0:T(8,128)S(1)}, f32[8,144,128]{2,1,0:T(8,128)S(1)}, u32[]{:S(2)}, u32[]{:S(2)}) collective-permute-start(f32[8,144,128]{2,1,0:T(8,128)S(1)} %pad_maximum_fusion), channel_id=1, source_target_pairs={{0,1},{1,2},{2,3},{3,4},{4,5},{5,6},{6,7},{7,8},{8,9},{9,10},{10,1... | collective-permute-start | bytes 1769480 | tf_op jit(solution)/shard_map/ppermute | solution.py:83
  156.5 15.8 %collective-permute-start.29 = (f32[8,144,128]{2,1,0:T(8,128)S(1)}, f32[8,144,128]{2,1,0:T(8,128)S(1)}, u32[]{:S(2)}, u32[]{:S(2)}) collective-permute-start(f32[8,144,128]{2,1,0:T(8,128)S(1)} %pad_maximum_fusion.1), channel_id=1, source_target_pairs={{1,0},{2,1},{3,2},{4,3},{5,4},{6,5},{7,6},{8,7},{9,8},{10,9},{11,1... | collective-permute-start | bytes 1769480 | tf_op jit(solution)/shard_map/ppermute | solution.py:88
  162.3 7.8 %collective-permute-start.30 = (f32[40,128]{1,0:T(8,128)S(1)}, f32[40,128]{1,0:T(8,128)S(1)}, u32[]{:S(2)}, u32[]{:S(2)}) collective-permute-start(f32[40,128]{1,0:T(8,128)S(1)} %get-tuple-element.98), channel_id=1, source_target_pairs={{0,128},{32,160},{64,192},{96,224},{128,0},{160,32},{192,64},{224,... | collective-permute-start | bytes 61448 | tf_op jit(solution)/shard_map/ppermute | solution.py:60
  170.1 2.3 %copy-start.1 = (f32[8,16,1024]{2,1,0:T(8,128)S(1)}, f32[8,16,1024]{2,1,0:T(8,128)}, u32[]{:S(2)}) copy-start(f32[8,16,1024]{2,1,0:T(8,128)} %get-tuple-element.82.east1_ref) | copy-start | bytes 1572868
  170.1 2.3 %copy-start.2 = (f32[8,16,1024]{2,1,0:T(8,128)S(1)}, f32[8,16,1024]{2,1,0:T(8,128)}, u32[]{:S(2)}) copy-start(f32[8,16,1024]{2,1,0:T(8,128)} %get-tuple-element.83.north1_ref) | copy-start | bytes 1572868
  170.1 2.3 %copy-start.3 = (f32[8,16,1024]{2,1,0:T(8,128)S(1)}, f32[8,16,1024]{2,1,0:T(8,128)}, u32[]{:S(2)}) copy-start(f32[8,16,1024]{2,1,0:T(8,128)} %get-tuple-element.84.east2_ref) | copy-start | bytes 1572868
  170.1 2.3 %copy-start.4 = (f32[8,16,1024]{2,1,0:T(8,128)S(1)}, f32[8,16,1024]{2,1,0:T(8,128)}, u32[]{:S(2)}) copy-start(f32[8,16,1024]{2,1,0:T(8,128)} %get-tuple-element.85.north2_ref) | copy-start | bytes 1572868
  175.9 15.1 %all-to-all-start.4 = ((f32[8,8,1024]{2,1,0:T(8,128)}), f32[8,8,1024]{2,1,0:T(8,128)S(1)}, u32[]{:S(2)}, u32[]{:S(2)}) async-start(f32[8,8,1024]{2,1,0:T(8,128)} %broadcast_in_dim.8), calls=%async_computation.4 | async-start | bytes 524288 | tf_op jit(solution)/shard_map/all_to_all | solution.py:50
  (2 other events, 1.2 us)

commit v4 on v3

--- a/solution.py
+++ b/solution.py
@@ -598,7 +598,7 @@
         name="pullback",
     )
     parts = [parts[0]] + [crossed(parts[j], j) for j in range(1, near)]
-    back, parts = lax.optimization_barrier((back, parts))
+    back, parts[1] = lax.optimization_barrier((back, parts[1]))
     whole = sum(parts[1:], parts[0])
 
     by_field = back.reshape(groups, fields, own_rows, own_members, block_cols)

time: 193 us -> 192 us (level)
    ppermute x4, waiting for transfers between devices: 11.1 us -> 8.33 us  [crossed(): return lax.ppermute(block, 'ens', [(i, i ^ distance) for i in range(count)])]
  transfers between devices with their start and end apart: 36 -> 36, of which waited for: 22 -> 21; matrix products, arithmetic and copies ran while one was open for 1% -> 1% of each run, Pallas kernels for 17% -> 17%
where the time goes in v4:
time: 192 us; the launch traced here: 190 us
  starting transfers between devices  90.2 us (47%)
  waiting for transfers between devices  56.6 us (29%)
  Pallas kernels  35.2 us (18%)
  local copies, waits for them, and re-layouts  4.32 us (2%)
  other arithmetic  2.51 us (1%)
    pallas_call x10, Pallas kernels, kernel_call(): pl.pallas_call(body, out_shape=[made(i, o) for i, o in enumerate(outs)],...  35.2 us
    ppermute x3, starting transfers between devices, from_below(): lax.ppermute(rows_sent, 'space', [(i + 1, i) for i in range(count - 1)])  17.3 us
    ppermute x14, starting transfers between devices, other(): lax.ppermute(block, 'space', [(i, i ^ distance) for i in range(count)])  17.1 us
    ppermute x7, starting transfers between devices, turned(): lax.ppermute(block, 'ens', [(i, (i + distance) % count) for i in range(co...  14.8 us
    all_to_all x3, starting transfers between devices, exchanged(): return lax.all_to_all(blocks, 'ens', 0, 0, tiled=False)  14.6 us
    all_to_all x2, waiting for transfers between devices, gathered(): return lax.all_to_all(copies, axis, 0, 0, tiled=False)  14.4 us
    ppermute x14, waiting for transfers between devices, other(): lax.ppermute(block, 'space', [(i, i ^ distance) for i in range(count)])  13.4 us
    all_to_all x2, starting transfers between devices, gathered(): return lax.all_to_all(copies, axis, 0, 0, tiled=False)  13 us
  transfers between devices with their start and end apart: 36, of which 21 were waited for; matrix products, arithmetic and copies ran while one was open for 1% of the time, Pallas kernels for 17%

profile of v4, /device:TPU:6, one launch (start us, length us, event | category | flops | bytes accessed | tf_op | source)
XLA Modules:
  0.0 190.0 jit_solution(13933129893086793544)
XLA Ops:
  2.8 8.5 %all-to-all-start = ((f32[8,24,128]{2,1,0:T(8,128)}), f32[8,24,128]{2,1,0:T(8,128)S(1)}, u32[]{:S(2)}, u32[]{:S(2)}) async-start(f32[8,24,128]{2,1,0:T(8,128)} %broadcast_in_dim.7), calls=%async_computation | async-start | bytes 196608 | tf_op jit(solution)/shard_map/all_to_all | solution.py:50
  11.3 3.3 %prepare.1 = (f32[11,16,1024]{2,1,0:T(8,128)}, f32[11,16,1024]{2,1,0:T(8,128)}, f32[8,384,128]{2,1,0:T(8,128)}) custom-call(f32[3,8,16,1024]{3,2,1,0:T(8,128)} %state_ref.3, f32[8,1024]{1,0:T(8,128)} %depth_ref.3, f32[384,1024]{1,0:T(8,128)} %bitcast.47), custom_call_target="tpu_custom_call" | custom-call | bytes 6193152 | tf_op jit(solution)/shard_map/prepare/pallas_call | solution.py:30
  14.6 5.4 %all-to-all-done = f32[8,24,128]{2,1,0:T(8,128)S(1)} async-done(((f32[8,24,128]{2,1,0:T(8,128)}), f32[8,24,128]{2,1,0:T(8,128)S(1)}, u32[]{:S(2)}, u32[]{:S(2)}) %all-to-all-start) | async-done | bytes 98336 | tf_op jit(solution)/shard_map/all_to_all | solution.py:50
  20.0 3.7 %all-to-all-start.1 = ((f32[8,384,128]{2,1,0:T(8,128)}), f32[8,384,128]{2,1,0:T(8,128)S(1)}, u32[]{:S(2)}, u32[]{:S(2)}) async-start(f32[8,384,128]{2,1,0:T(8,128)} %get-tuple-element.59), calls=%async_computation.1 | async-start | bytes 3145728 | tf_op jit(solution)/shard_map/all_to_all | solution.py:44
  23.7 1.9 %collective-permute-start = (f32[11,16,1024]{2,1,0:T(8,128)}, f32[11,16,1024]{2,1,0:T(8,128)}, u32[]{:S(2)}, u32[]{:S(2)}) collective-permute-start(f32[11,16,1024]{2,1,0:T(8,128)} %get-tuple-element.45), channel_id=1, source_target_pairs={{0,1},{1,2},{2,3},{3,4},{4,5},{5,6},{6,7},{7,8},{8,9},{9,10},{10,1... | collective-permute-start | bytes 2162696 | tf_op jit(solution)/shard_map/ppermute | solution.py:83
  25.7 5.8 %collective-permute-start.1 = (f32[11,16,1024]{2,1,0:T(8,128)}, f32[11,16,1024]{2,1,0:T(8,128)}, u32[]{:S(2)}, u32[]{:S(2)}) collective-permute-start(f32[11,16,1024]{2,1,0:T(8,128)} %get-tuple-element.46), channel_id=1, source_target_pairs={{1,0},{2,1},{3,2},{4,3},{5,4},{6,5},{7,6},{8,7},{9,8},{10,9},{11,1... | collective-permute-start | bytes 2162696 | tf_op jit(solution)/shard_map/ppermute | solution.py:88
  31.8 7.0 %collective-permute-done.above_ref = f32[11,16,1024]{2,1,0:T(8,128)} collective-permute-done((f32[11,16,1024]{2,1,0:T(8,128)}, f32[11,16,1024]{2,1,0:T(8,128)}, u32[]{:S(2)}, u32[]{:S(2)}) %collective-permute-start) | collective-permute-done | bytes 720928 | tf_op jit(solution)/shard_map/ppermute | solution.py:83
  38.8 1.8 collective-permute-done.1.below_ref
  40.5 5.3 %forward.1 = (f32[8,24,16,128]{3,2,1,0:T(8,128)}, f32[4,16,128]{2,1,0:T(8,128)S(1)}, f32[8,16,1024]{2,1,0:T(8,128)}, f32[8,16,1024]{2,1,0:T(8,128)}, f32[8,16,1024]{2,1,0:T(8,128)}, /*index=5*/f32[8,16,1024]{2,1,0:T(8,128)}) custom-call(f32[16]{0:T(128)S(1)} %and_convert_fusion.inside_ref, f32[3,8,16,1024]{3,2,1,0:T(8,128)S(1)} %copy-done, ...), custom_call_target="tpu_custom_call" | custom-call | flops 100000000 | bytes 6752320 | tf_op jit(solution)/shard_map/forward/pallas_call | solution.py:30
  45.9 3.2 %collective-permute-start.8 = (f32[4,16,128]{2,1,0:T(8,128)S(1)}, f32[4,16,128]{2,1,0:T(8,128)S(1)}, u32[]{:S(2)}, u32[]{:S(2)}) collective-permute-start(f32[4,16,128]{2,1,0:T(8,128)S(1)} %get-tuple-element.49.refs_0_), channel_id=1, source_target_pairs={{0,224},{32,0},{64,32},{96,64},{128,96},{160,128},{192,160},{224,1... | collective-permute-start | bytes 98312 | tf_op jit(solution)/shard_map/ppermute | solution.py:55
  49.1 2.3 %collective-permute-start.7 = (f32[4,16,128]{2,1,0:T(8,128)S(1)}, f32[4,16,128]{2,1,0:T(8,128)S(1)}, u32[]{:S(2)}, u32[]{:S(2)}) collective-permute-start(f32[4,16,128]{2,1,0:T(8,128)S(1)} %get-tuple-element.49.refs_0_), channel_id=1, source_target_pairs={{0,192},{32,224},{64,0},{96,32},{128,64},{160,96},{192,128},{224,1... | collective-permute-start | bytes 98312 | tf_op jit(solution)/shard_map/ppermute | solution.py:55
  51.4 1.4 collective-permute-start.6
  52.9 3.6 %collective-permute-start.5 = (f32[4,16,128]{2,1,0:T(8,128)S(1)}, f32[4,16,128]{2,1,0:T(8,128)S(1)}, u32[]{:S(2)}, u32[]{:S(2)}) collective-permute-start(f32[4,16,128]{2,1,0:T(8,128)S(1)} %get-tuple-element.49.refs_0_), channel_id=1, source_target_pairs={{0,128},{32,160},{64,192},{96,224},{128,0},{160,32},{192,64},{224,... | collective-permute-start | bytes 98312 | tf_op jit(solution)/shard_map/ppermute | solution.py:55
  56.7 5.8 %collective-permute-done.8.refs_7_ = f32[4,16,128]{2,1,0:T(8,128)S(1)} collective-permute-done((f32[4,16,128]{2,1,0:T(8,128)S(1)}, f32[4,16,128]{2,1,0:T(8,128)S(1)}, u32[]{:S(2)}, u32[]{:S(2)}) %collective-permute-start.8) | collective-permute-done | bytes 32800 | tf_op jit(solution)/shard_map/ppermute | solution.py:55
  62.5 4.0 %collective-permute-start.2 = (f32[4,16,128]{2,1,0:T(8,128)S(1)}, f32[4,16,128]{2,1,0:T(8,128)S(1)}, u32[]{:S(2)}, u32[]{:S(2)}) collective-permute-start(f32[4,16,128]{2,1,0:T(8,128)S(1)} %get-tuple-element.49.refs_0_), channel_id=1, source_target_pairs={{0,32},{32,64},{64,96},{96,128},{128,160},{160,192},{192,224},{224... | collective-permute-start | bytes 98312 | tf_op jit(solution)/shard_map/ppermute | solution.py:55
  66.5 2.0 %collective-permute-done.3.refs_2_ = f32[4,16,128]{2,1,0:T(8,128)S(1)} collective-permute-done((f32[4,16,128]{2,1,0:T(8,128)S(1)}, f32[4,16,128]{2,1,0:T(8,128)S(1)}, u32[]{:S(2)}, u32[]{:S(2)}) %collective-permute-start.3) | collective-permute-done | bytes 32800 | tf_op jit(solution)/shard_map/ppermute | solution.py:55
  69.1 5.9 %all-to-all-start.3 = ((f32[8,24,16,128]{3,2,1,0:T(8,128)}), f32[8,24,16,128]{3,2,1,0:T(8,128)}, u32[]{:S(2)}, u32[]{:S(2)}) async-start(f32[8,24,16,128]{3,2,1,0:T(8,128)} %get-tuple-element.60), calls=%async_computation.3 | async-start | bytes 3145728 | tf_op jit(solution)/shard_map/all_to_all | solution.py:44
  75.2 2.0 %gram.1 = (f32[4,128,128]{2,1,0:T(8,128)S(1)}, f32[4,8,128]{2,1,0:T(8,128)S(1)}, f32[136,128]{1,0:T(8,128)S(1)}) custom-call(s32[1]{0:T(128)} %bitcast.place_ref, f32[3,4,128]{2,1,0:T(4,128)S(1)} %reshape.25.params_ref, f32[4,16,128]{2,1,0:T(8,128)} %copy-done.6, f32[4,16,128]{2,1,0:T(8,128)} %copy-done.13, f32[4,16,128]{2,1,0:T(8,128)} %copy-done.12, ...), custom_call_target="tpu_custom_call" | custom-call | flops 100663296 | bytes 616452 | tf_op jit(solution)/shard_map/gram/pallas_call | solution.py:30
  77.3 1.2 collective-permute-done.9
  78.5 3.0 %collective-permute-start.12 = (f32[136,128]{1,0:T(8,128)S(1)}, f32[136,128]{1,0:T(8,128)S(1)}, u32[]{:S(2)}, u32[]{:S(2)}) collective-permute-start(f32[136,128]{1,0:T(8,128)S(1)} %add.62), channel_id=1, source_target_pairs={{0,6},{1,7},{2,4},{3,5},{4,2},{5,3},{6,0},{7,1},{8,14},{9,15},{10,... | collective-permute-start | bytes 208904 | tf_op jit(solution)/shard_map/ppermute | solution.py:67
  82.7 2.1 %collective-permute-done.12 = f32[136,128]{1,0:T(8,128)S(1)} collective-permute-done((f32[136,128]{1,0:T(8,128)S(1)}, f32[136,128]{1,0:T(8,128)S(1)}, u32[]{:S(2)}, u32[]{:S(2)}) %collective-permute-start.12) | collective-permute-done | bytes 69664 | tf_op jit(solution)/shard_map/ppermute | solution.py:67
  84.9 2.9 %collective-permute-done.11 = f32[136,128]{1,0:T(8,128)S(1)} collective-permute-done((f32[136,128]{1,0:T(8,128)S(1)}, f32[136,128]{1,0:T(8,128)S(1)}, u32[]{:S(2)}, u32[]{:S(2)}) %collective-permute-start.11) | collective-permute-done | bytes 69664 | tf_op jit(solution)/shard_map/ppermute | solution.py:67
  88.6 2.4 %collective-permute-start.14 = (f32[136,128]{1,0:T(8,128)S(1)}, f32[136,128]{1,0:T(8,128)S(1)}, u32[]{:S(2)}, u32[]{:S(2)}) collective-permute-start(f32[136,128]{1,0:T(8,128)S(1)} %add_add_fusion.1), channel_id=1, source_target_pairs={{0,16},{1,17},{2,18},{3,19},{4,20},{5,21},{6,22},{7,23},{8,24},{9,... | collective-permute-start | bytes 208904 | tf_op jit(solution)/shard_map/ppermute | solution.py:67
  92.2 1.4 collective-permute-done.15
  95.4 11.2 %factor.1 = (f32[128,128]{1,0:T(8,128)S(1)}, f32[128,128]{1,0:T(8,128)S(1)}, f32[8,128]{1,0:T(8,128)S(1)}) custom-call(f32[136,128]{1,0:T(8,128)S(1)} %add_add_fusion.gram_ref), custom_call_target="tpu_custom_call" | custom-call | flops 1000000000 | bytes 204800 | tf_op jit(solution)/shard_map/factor/pallas_call | solution.py:30
  106.6 2.2 %mix.1 = f32[8,24,16,128]{3,2,1,0:T(8,128)} custom-call(f32[128,128]{1,0:T(8,128)S(1)} %get-tuple-element.58.mixing_ref, f32[8,24,16,128]{3,2,1,0:T(8,128)S(1)} %bitcast.45), custom_call_target="tpu_custom_call" | custom-call | flops 10000000000 | bytes 3211264 | tf_op jit(solution)/shard_map/mix/pallas_call | solution.py:30
  108.8 2.3 %all-to-all-done.3.state_ref = f32[8,24,16,128]{3,2,1,0:T(8,128)} async-done(((f32[8,24,16,128]{3,2,1,0:T(8,128)}), f32[8,24,16,128]{3,2,1,0:T(8,128)}, u32[]{:S(2)}, u32[]{:S(2)}) %all-to-all-start.3) | async-done | bytes 1572896 | tf_op jit(solution)/shard_map/all_to_all | solution.py:44
  111.1 4.9 %all-to-all-start.2 = ((f32[8,24,16,128]{3,2,1,0:T(8,128)}), f32[8,24,16,128]{3,2,1,0:T(8,128)S(1)}, u32[]{:S(2)}, u32[]{:S(2)}) async-start(f32[8,24,16,128]{3,2,1,0:T(8,128)} %mix.1), calls=%async_computation.2 | async-start | bytes 3145728 | tf_op jit(solution)/shard_map/all_to_all | solution.py:44
  116.8 3.5 %cross.1 = f32[128,128]{1,0:T(8,128)S(1)} custom-call(f32[8,24,16,128]{3,2,1,0:T(8,128)} %all-to-all-done.3.state_ref, f32[8,24,16,128]{3,2,1,0:T(8,128)S(1)} %bitcast.46), custom_call_target="tpu_custom_call" | custom-call | flops 10000000000 | bytes 3211264 | tf_op jit(solution)/shard_map/cross/pallas_call | solution.py:30
  121.7 1.4 collective-permute-start.19
  123.0 1.7 collective-permute-start.18
  126.0 1.9 %collective-permute-start.23 = (f32[4,136,64]{2,1,0:T(8,128)S(1)}, f32[4,136,64]{2,1,0:T(8,128)S(1)}, u32[]{:S(2)}, u32[]{:S(2)}) collective-permute-start(f32[4,136,64]{2,1,0:T(8,128)S(1)} %get-tuple-element.90), channel_id=1, source_target_pairs={{0,1},{1,2},{2,3},{3,4},{4,5},{5,6},{6,7},{7,8},{8,9},{9,10},{10,1... | collective-permute-start | bytes 417800 | tf_op jit(solution)/shard_map/ppermute | solution.py:83
  127.9 5.8 %collective-permute-start.24 = (f32[4,136,64]{2,1,0:T(8,128)S(1)}, f32[4,136,64]{2,1,0:T(8,128)S(1)}, u32[]{:S(2)}, u32[]{:S(2)}) collective-permute-start(f32[4,136,64]{2,1,0:T(8,128)S(1)} %get-tuple-element.91), channel_id=1, source_target_pairs={{1,0},{2,1},{3,2},{4,3},{5,4},{6,5},{7,6},{8,7},{9,8},{10,9},{11,1... | collective-permute-start | bytes 417800 | tf_op jit(solution)/shard_map/ppermute | solution.py:88
  133.8 3.2 %collective-permute-start.21 = (f32[128,128]{1,0:T(8,128)S(1)}, f32[128,128]{1,0:T(8,128)S(1)}, u32[]{:S(2)}, u32[]{:S(2)}) collective-permute-start(f32[128,128]{1,0:T(8,128)S(1)} %add_add_fusion.3), channel_id=1, source_target_pairs={{0,16},{1,17},{2,18},{3,19},{4,20},{5,21},{6,22},{7,23},{8,24},{9,... | collective-permute-start | bytes 196616 | tf_op jit(solution)/shard_map/ppermute | solution.py:67
  139.3 1.9 %collective-permute-done.21 = f32[128,128]{1,0:T(8,128)S(1)} collective-permute-done((f32[128,128]{1,0:T(8,128)S(1)}, f32[128,128]{1,0:T(8,128)S(1)}, u32[]{:S(2)}, u32[]{:S(2)}) %collective-permute-start.21) | collective-permute-done | bytes 65568 | tf_op jit(solution)/shard_map/ppermute | solution.py:67
  141.3 1.3 pullback.1
  142.6 2.1 %collective-permute-start.25 = (f32[2,40,128]{2,1,0:T(8,128)S(1)}, f32[2,40,128]{2,1,0:T(8,128)S(1)}, u32[]{:S(2)}, u32[]{:S(2)}) collective-permute-start(f32[2,40,128]{2,1,0:T(8,128)S(1)} %get-tuple-element.68), channel_id=1, source_target_pairs={{0,32},{32,0},{64,96},{96,64},{128,160},{160,128},{192,224},{224,1... | collective-permute-start | bytes 122888 | tf_op jit(solution)/shard_map/ppermute | solution.py:60
  145.5 2.4 %collective-permute-start.28 = (f32[2,40,128]{2,1,0:T(8,128)S(1)}, f32[2,40,128]{2,1,0:T(8,128)S(1)}, u32[]{:S(2)}, u32[]{:S(2)}) collective-permute-start(f32[2,40,128]{2,1,0:T(8,128)S(1)} %get-tuple-element.72), channel_id=1, source_target_pairs={{0,64},{32,96},{64,0},{96,32},{128,192},{160,224},{192,128},{224,1... | collective-permute-start | bytes 122888 | tf_op jit(solution)/shard_map/ppermute | solution.py:60
  147.8 3.9 %collective-permute-done.25 = f32[2,40,128]{2,1,0:T(8,128)S(1)} collective-permute-done((f32[2,40,128]{2,1,0:T(8,128)S(1)}, f32[2,40,128]{2,1,0:T(8,128)S(1)}, u32[]{:S(2)}, u32[]{:S(2)}) %collective-permute-start.25) | collective-permute-done | bytes 40992 | tf_op jit(solution)/shard_map/ppermute | solution.py:60
  153.0 1.9 %collective-permute-start.26 = (f32[8,144,128]{2,1,0:T(8,128)S(1)}, f32[8,144,128]{2,1,0:T(8,128)S(1)}, u32[]{:S(2)}, u32[]{:S(2)}) collective-permute-start(f32[8,144,128]{2,1,0:T(8,128)S(1)} %pad_maximum_fusion), channel_id=1, source_target_pairs={{0,1},{1,2},{2,3},{3,4},{4,5},{5,6},{6,7},{7,8},{8,9},{9,10},{10,1... | collective-permute-start | bytes 1769480 | tf_op jit(solution)/shard_map/ppermute | solution.py:83
  155.0 5.8 %collective-permute-start.27 = (f32[8,144,128]{2,1,0:T(8,128)S(1)}, f32[8,144,128]{2,1,0:T(8,128)S(1)}, u32[]{:S(2)}, u32[]{:S(2)}) collective-permute-start(f32[8,144,128]{2,1,0:T(8,128)S(1)} %pad_maximum_fusion.1), channel_id=1, source_target_pairs={{1,0},{2,1},{3,2},{4,3},{5,4},{6,5},{7,6},{8,7},{9,8},{10,9},{11,1... | collective-permute-start | bytes 1769480 | tf_op jit(solution)/shard_map/ppermute | solution.py:88
  160.8 3.3 %collective-permute-start.30 = (f32[40,128]{1,0:T(8,128)S(1)}, f32[40,128]{1,0:T(8,128)S(1)}, u32[]{:S(2)}, u32[]{:S(2)}) collective-permute-start(f32[40,128]{1,0:T(8,128)S(1)} %get-tuple-element.92), channel_id=1, source_target_pairs={{0,128},{32,160},{64,192},{96,224},{128,0},{160,32},{192,64},{224,... | collective-permute-start | bytes 61448 | tf_op jit(solution)/shard_map/ppermute | solution.py:60
  164.1 4.5 %collective-permute-done.30.refs_1_ = f32[40,128]{1,0:T(8,128)S(1)} collective-permute-done((f32[40,128]{1,0:T(8,128)S(1)}, f32[40,128]{1,0:T(8,128)S(1)}, u32[]{:S(2)}, u32[]{:S(2)}) %collective-permute-start.30) | collective-permute-done | bytes 20512 | tf_op jit(solution)/shard_map/ppermute | solution.py:60
  168.6 2.2 %observe.1.seen_ref = f32[16,16,1024]{2,1,0:T(8,128)S(1)} custom-call(f32[40,128]{1,0:T(8,128)S(1)} %get-tuple-element.93.refs_0_, f32[40,128]{1,0:T(8,128)S(1)} %collective-permute-done.30.refs_1_, f32[8,136,128]{2,1,0:T(8,128)S(1)} %maximum_maximum_fusion.refs_2_), custom_call_target="tpu_custom_call" | custom-call | flops 1000000000 | bytes 1646592 | tf_op jit(solution)/shard_map/observe/pallas_call | solution.py:30
  170.9 2.7 %backward.1 = (f32[8,1024]{1,0:T(8,128)S(1)}, f32[10,16,1024]{2,1,0:T(8,128)S(1)}, f32[8,16,1024]{2,1,0:T(8,128)S(1)}, f32[10,16,1024]{2,1,0:T(8,128)S(1)}) custom-call(f32[16]{0:T(128)S(1)} %and_convert_fusion.inside_ref, f32[8,24,16,128]{3,2,1,0:T(8,128)S(1)} %all-to-all-done.2.back_ref, f32[8,144,128]{2,1,0:T(8,128)S(1)} %collective-permute-done.26.above_ref, ...), custom_call_target="tpu_custom_call" | custom-call | flops 100000000 | bytes 7831616 | tf_op jit(solution)/shard_map/backward/pallas_call | solution.py:30
  174.4 4.5 %all-to-all-start.4 = ((f32[8,8,1024]{2,1,0:T(8,128)}), f32[8,8,1024]{2,1,0:T(8,128)S(1)}, u32[]{:S(2)}, u32[]{:S(2)}) async-start(f32[8,8,1024]{2,1,0:T(8,128)} %broadcast_in_dim.8), calls=%async_computation.4 | async-start | bytes 524288 | tf_op jit(solution)/shard_map/all_to_all | solution.py:50
  178.9 1.5 finish.1
  180.3 9.0 %all-to-all-done.4 = f32[8,8,1024]{2,1,0:T(8,128)S(1)} async-done(((f32[8,8,1024]{2,1,0:T(8,128)}), f32[8,8,1024]{2,1,0:T(8,128)S(1)}, u32[]{:S(2)}, u32[]{:S(2)}) %all-to-all-start.4) | async-done | bytes 262176 | tf_op jit(solution)/shard_map/all_to_all | solution.py:50
  (97 shorter events, 17.8 us)
Async XLA Ops:
  2.8 17.2 %all-to-all-start = ((f32[8,24,128]{2,1,0:T(8,128)}), f32[8,24,128]{2,1,0:T(8,128)S(1)}, u32[]{:S(2)}, u32[]{:S(2)}) async-start(f32[8,24,128]{2,1,0:T(8,128)} %broadcast_in_dim.7), calls=%async_computation | async-start | bytes 196608 | tf_op jit(solution)/shard_map/all_to_all | solution.py:50
  20.0 20.5 %copy-start = (f32[3,8,16,1024]{3,2,1,0:T(8,128)S(1)}, f32[3,8,16,1024]{3,2,1,0:T(8,128)}, u32[]{:S(2)}) copy-start(f32[3,8,16,1024]{3,2,1,0:T(8,128)} %state_ref.3) | copy-start | bytes 4718596
  20.0 20.5 %copy-start.5 = (f32[8,1024]{1,0:T(8,128)S(1)}, f32[8,1024]{1,0:T(8,128)}, u32[]{:S(2)}) copy-start(f32[8,1024]{1,0:T(8,128)} %depth_ref.3) | copy-start | bytes 98308
  20.0 48.5 %all-to-all-start.1 = ((f32[8,384,128]{2,1,0:T(8,128)}), f32[8,384,128]{2,1,0:T(8,128)S(1)}, u32[]{:S(2)}, u32[]{:S(2)}) async-start(f32[8,384,128]{2,1,0:T(8,128)} %get-tuple-element.59), calls=%async_computation.1 | async-start | bytes 3145728 | tf_op jit(solution)/shard_map/all_to_all | solution.py:44
  23.7 15.0 %collective-permute-start = (f32[11,16,1024]{2,1,0:T(8,128)}, f32[11,16,1024]{2,1,0:T(8,128)}, u32[]{:S(2)}, u32[]{:S(2)}) collective-permute-start(f32[11,16,1024]{2,1,0:T(8,128)} %get-tuple-element.45), channel_id=1, source_target_pairs={{0,1},{1,2},{2,3},{3,4},{4,5},{5,6},{6,7},{7,8},{8,9},{9,10},{10,1... | collective-permute-start | bytes 2162696 | tf_op jit(solution)/shard_map/ppermute | solution.py:83
  25.7 14.9 %collective-permute-start.1 = (f32[11,16,1024]{2,1,0:T(8,128)}, f32[11,16,1024]{2,1,0:T(8,128)}, u32[]{:S(2)}, u32[]{:S(2)}) collective-permute-start(f32[11,16,1024]{2,1,0:T(8,128)} %get-tuple-element.46), channel_id=1, source_target_pairs={{1,0},{2,1},{3,2},{4,3},{5,4},{6,5},{7,6},{8,7},{9,8},{10,9},{11,1... | collective-permute-start | bytes 2162696 | tf_op jit(solution)/shard_map/ppermute | solution.py:88
  45.8 22.7 %copy-start.6 = (f32[4,16,128]{2,1,0:T(8,128)}, f32[4,16,128]{2,1,0:T(8,128)S(1)}, u32[]{:S(2)}) copy-start(f32[4,16,128]{2,1,0:T(8,128)S(1)} %get-tuple-element.49.refs_0_) | copy-start | bytes 98308
  45.9 16.6 %collective-permute-start.8 = (f32[4,16,128]{2,1,0:T(8,128)S(1)}, f32[4,16,128]{2,1,0:T(8,128)S(1)}, u32[]{:S(2)}, u32[]{:S(2)}) collective-permute-start(f32[4,16,128]{2,1,0:T(8,128)S(1)} %get-tuple-element.49.refs_0_), channel_id=1, source_target_pairs={{0,224},{32,0},{64,32},{96,64},{128,96},{160,128},{192,160},{224,1... | collective-permute-start | bytes 98312 | tf_op jit(solution)/shard_map/ppermute | solution.py:55
  49.1 13.4 %collective-permute-start.7 = (f32[4,16,128]{2,1,0:T(8,128)S(1)}, f32[4,16,128]{2,1,0:T(8,128)S(1)}, u32[]{:S(2)}, u32[]{:S(2)}) collective-permute-start(f32[4,16,128]{2,1,0:T(8,128)S(1)} %get-tuple-element.49.refs_0_), channel_id=1, source_target_pairs={{0,192},{32,224},{64,0},{96,32},{128,64},{160,96},{192,128},{224,1... | collective-permute-start | bytes 98312 | tf_op jit(solution)/shard_map/ppermute | solution.py:55
  51.4 15.0 %collective-permute-start.6 = (f32[4,16,128]{2,1,0:T(8,128)S(1)}, f32[4,16,128]{2,1,0:T(8,128)S(1)}, u32[]{:S(2)}, u32[]{:S(2)}) collective-permute-start(f32[4,16,128]{2,1,0:T(8,128)S(1)} %get-tuple-element.49.refs_0_), channel_id=1, source_target_pairs={{0,160},{32,192},{64,224},{96,0},{128,32},{160,64},{192,96},{224,1... | collective-permute-start | bytes 98312 | tf_op jit(solution)/shard_map/ppermute | solution.py:55
  52.9 13.6 %collective-permute-start.5 = (f32[4,16,128]{2,1,0:T(8,128)S(1)}, f32[4,16,128]{2,1,0:T(8,128)S(1)}, u32[]{:S(2)}, u32[]{:S(2)}) collective-permute-start(f32[4,16,128]{2,1,0:T(8,128)S(1)} %get-tuple-element.49.refs_0_), channel_id=1, source_target_pairs={{0,128},{32,160},{64,192},{96,224},{128,0},{160,32},{192,64},{224,... | collective-permute-start | bytes 98312 | tf_op jit(solution)/shard_map/ppermute | solution.py:55
  56.5 10.0 %collective-permute-start.4 = (f32[4,16,128]{2,1,0:T(8,128)S(1)}, f32[4,16,128]{2,1,0:T(8,128)S(1)}, u32[]{:S(2)}, u32[]{:S(2)}) collective-permute-start(f32[4,16,128]{2,1,0:T(8,128)S(1)} %get-tuple-element.49.refs_0_), channel_id=1, source_target_pairs={{0,96},{32,128},{64,160},{96,192},{128,224},{160,0},{192,32},{224,... | collective-permute-start | bytes 98312 | tf_op jit(solution)/shard_map/ppermute | solution.py:55
  62.5 6.1 %copy-start.7 = (f32[4,16,128]{2,1,0:T(8,128)}, f32[4,16,128]{2,1,0:T(8,128)S(1)}, u32[]{:S(2)}) copy-start(f32[4,16,128]{2,1,0:T(8,128)S(1)} %collective-permute-done.8.refs_7_) | copy-start | bytes 98308
  62.5 6.0 %collective-permute-start.3 = (f32[4,16,128]{2,1,0:T(8,128)S(1)}, f32[4,16,128]{2,1,0:T(8,128)S(1)}, u32[]{:S(2)}, u32[]{:S(2)}) collective-permute-start(f32[4,16,128]{2,1,0:T(8,128)S(1)} %get-tuple-element.49.refs_0_), channel_id=1, source_target_pairs={{0,64},{32,96},{64,128},{96,160},{128,192},{160,224},{192,0},{224,... | collective-permute-start | bytes 98312 | tf_op jit(solution)/shard_map/ppermute | solution.py:55
  62.5 6.1 %copy-start.8 = (f32[4,16,128]{2,1,0:T(8,128)}, f32[4,16,128]{2,1,0:T(8,128)S(1)}, u32[]{:S(2)}) copy-start(f32[4,16,128]{2,1,0:T(8,128)S(1)} %collective-permute-done.7.refs_6_) | copy-start | bytes 98308
  62.5 6.0 %collective-permute-start.2 = (f32[4,16,128]{2,1,0:T(8,128)S(1)}, f32[4,16,128]{2,1,0:T(8,128)S(1)}, u32[]{:S(2)}, u32[]{:S(2)}) collective-permute-start(f32[4,16,128]{2,1,0:T(8,128)S(1)} %get-tuple-element.49.refs_0_), channel_id=1, source_target_pairs={{0,32},{32,64},{64,96},{96,128},{128,160},{160,192},{192,224},{224... | collective-permute-start | bytes 98312 | tf_op jit(solution)/shard_map/ppermute | solution.py:55
  66.4 2.1 %copy-start.9 = (f32[4,16,128]{2,1,0:T(8,128)}, f32[4,16,128]{2,1,0:T(8,128)S(1)}, u32[]{:S(2)}) copy-start(f32[4,16,128]{2,1,0:T(8,128)S(1)} %collective-permute-done.6.refs_5_) | copy-start | bytes 98308
  66.4 2.1 %copy-start.10 = (f32[4,16,128]{2,1,0:T(8,128)}, f32[4,16,128]{2,1,0:T(8,128)S(1)}, u32[]{:S(2)}) copy-start(f32[4,16,128]{2,1,0:T(8,128)S(1)} %collective-permute-done.5.refs_4_) | copy-start | bytes 98308
  66.5 2.1 %copy-start.11 = (f32[4,16,128]{2,1,0:T(8,128)}, f32[4,16,128]{2,1,0:T(8,128)S(1)}, u32[]{:S(2)}) copy-start(f32[4,16,128]{2,1,0:T(8,128)S(1)} %collective-permute-done.4.refs_3_) | copy-start | bytes 98308
  69.1 42.0 %all-to-all-start.3 = ((f32[8,24,16,128]{3,2,1,0:T(8,128)}), f32[8,24,16,128]{3,2,1,0:T(8,128)}, u32[]{:S(2)}, u32[]{:S(2)}) async-start(f32[8,24,16,128]{3,2,1,0:T(8,128)} %get-tuple-element.60), calls=%async_computation.3 | async-start | bytes 3145728 | tf_op jit(solution)/shard_map/all_to_all | solution.py:44
  77.2 1.3 collective-permute-start.9
  78.5 6.3 %collective-permute-start.12 = (f32[136,128]{1,0:T(8,128)S(1)}, f32[136,128]{1,0:T(8,128)S(1)}, u32[]{:S(2)}, u32[]{:S(2)}) collective-permute-start(f32[136,128]{1,0:T(8,128)S(1)} %add.62), channel_id=1, source_target_pairs={{0,6},{1,7},{2,4},{3,5},{4,2},{5,3},{6,0},{7,1},{8,14},{9,15},{10,... | collective-permute-start | bytes 208904 | tf_op jit(solution)/shard_map/ppermute | solution.py:67
  81.6 6.2 %collective-permute-start.11 = (f32[136,128]{1,0:T(8,128)S(1)}, f32[136,128]{1,0:T(8,128)S(1)}, u32[]{:S(2)}, u32[]{:S(2)}) collective-permute-start(f32[136,128]{1,0:T(8,128)S(1)} %add.62), channel_id=1, source_target_pairs={{0,4},{1,5},{2,6},{3,7},{4,0},{5,1},{6,2},{7,3},{8,12},{9,13},{10,... | collective-permute-start | bytes 208904 | tf_op jit(solution)/shard_map/ppermute | solution.py:67
  82.3 5.5 %collective-permute-start.10 = (f32[136,128]{1,0:T(8,128)S(1)}, f32[136,128]{1,0:T(8,128)S(1)}, u32[]{:S(2)}, u32[]{:S(2)}) collective-permute-start(f32[136,128]{1,0:T(8,128)S(1)} %add.62), channel_id=1, source_target_pairs={{0,2},{1,3},{2,0},{3,1},{4,6},{5,7},{6,4},{7,5},{8,10},{9,11},{10,... | collective-permute-start | bytes 208904 | tf_op jit(solution)/shard_map/ppermute | solution.py:67
  87.8 5.8 %collective-permute-start.15 = (f32[136,128]{1,0:T(8,128)S(1)}, f32[136,128]{1,0:T(8,128)S(1)}, u32[]{:S(2)}, u32[]{:S(2)}) collective-permute-start(f32[136,128]{1,0:T(8,128)S(1)} %add_add_fusion.1), channel_id=1, source_target_pairs={{0,24},{1,25},{2,26},{3,27},{4,28},{5,29},{6,30},{7,31},{8,16},{9,... | collective-permute-start | bytes 208904 | tf_op jit(solution)/shard_map/ppermute | solution.py:67
  88.6 5.8 %collective-permute-start.14 = (f32[136,128]{1,0:T(8,128)S(1)}, f32[136,128]{1,0:T(8,128)S(1)}, u32[]{:S(2)}, u32[]{:S(2)}) collective-permute-start(f32[136,128]{1,0:T(8,128)S(1)} %add_add_fusion.1), channel_id=1, source_target_pairs={{0,16},{1,17},{2,18},{3,19},{4,20},{5,21},{6,22},{7,23},{8,24},{9,... | collective-permute-start | bytes 208904 | tf_op jit(solution)/shard_map/ppermute | solution.py:67
  91.0 4.3 %collective-permute-start.13 = (f32[136,128]{1,0:T(8,128)S(1)}, f32[136,128]{1,0:T(8,128)S(1)}, u32[]{:S(2)}, u32[]{:S(2)}) collective-permute-start(f32[136,128]{1,0:T(8,128)S(1)} %add_add_fusion.1), channel_id=1, source_target_pairs={{0,8},{1,9},{2,10},{3,11},{4,12},{5,13},{6,14},{7,15},{8,0},{9,1},... | collective-permute-start | bytes 208904 | tf_op jit(solution)/shard_map/ppermute | solution.py:67
  111.1 41.8 %all-to-all-start.2 = ((f32[8,24,16,128]{3,2,1,0:T(8,128)}), f32[8,24,16,128]{3,2,1,0:T(8,128)S(1)}, u32[]{:S(2)}, u32[]{:S(2)}) async-start(f32[8,24,16,128]{3,2,1,0:T(8,128)} %mix.1), calls=%async_computation.2 | async-start | bytes 3145728 | tf_op jit(solution)/shard_map/all_to_all | solution.py:44
  120.3 1.3 collective-permute-start.16
  121.7 12.0 %collective-permute-start.19 = (f32[128,128]{1,0:T(8,128)S(1)}, f32[128,128]{1,0:T(8,128)S(1)}, u32[]{:S(2)}, u32[]{:S(2)}) collective-permute-start(f32[128,128]{1,0:T(8,128)S(1)} %add.69), channel_id=1, source_target_pairs={{0,6},{1,7},{2,4},{3,5},{4,2},{5,3},{6,0},{7,1},{8,14},{9,15},{10,... | collective-permute-start | bytes 196616 | tf_op jit(solution)/shard_map/ppermute | solution.py:67
  123.0 10.6 %collective-permute-start.18 = (f32[128,128]{1,0:T(8,128)S(1)}, f32[128,128]{1,0:T(8,128)S(1)}, u32[]{:S(2)}, u32[]{:S(2)}) collective-permute-start(f32[128,128]{1,0:T(8,128)S(1)} %add.69), channel_id=1, source_target_pairs={{0,4},{1,5},{2,6},{3,7},{4,0},{5,1},{6,2},{7,3},{8,12},{9,13},{10,... | collective-permute-start | bytes 196616 | tf_op jit(solution)/shard_map/ppermute | solution.py:67
  124.7 8.9 %collective-permute-start.17 = (f32[128,128]{1,0:T(8,128)S(1)}, f32[128,128]{1,0:T(8,128)S(1)}, u32[]{:S(2)}, u32[]{:S(2)}) collective-permute-start(f32[128,128]{1,0:T(8,128)S(1)} %add.69), channel_id=1, source_target_pairs={{0,2},{1,3},{2,0},{3,1},{4,6},{5,7},{6,4},{7,5},{8,10},{9,11},{10,... | collective-permute-start | bytes 196616 | tf_op jit(solution)/shard_map/ppermute | solution.py:67
  126.0 11.9 %collective-permute-start.23 = (f32[4,136,64]{2,1,0:T(8,128)S(1)}, f32[4,136,64]{2,1,0:T(8,128)S(1)}, u32[]{:S(2)}, u32[]{:S(2)}) collective-permute-start(f32[4,136,64]{2,1,0:T(8,128)S(1)} %get-tuple-element.90), channel_id=1, source_target_pairs={{0,1},{1,2},{2,3},{3,4},{4,5},{5,6},{6,7},{7,8},{8,9},{9,10},{10,1... | collective-permute-start | bytes 417800 | tf_op jit(solution)/shard_map/ppermute | solution.py:83
  127.9 10.4 %collective-permute-start.24 = (f32[4,136,64]{2,1,0:T(8,128)S(1)}, f32[4,136,64]{2,1,0:T(8,128)S(1)}, u32[]{:S(2)}, u32[]{:S(2)}) collective-permute-start(f32[4,136,64]{2,1,0:T(8,128)S(1)} %get-tuple-element.91), channel_id=1, source_target_pairs={{1,0},{2,1},{3,2},{4,3},{5,4},{6,5},{7,6},{8,7},{9,8},{10,9},{11,1... | collective-permute-start | bytes 417800 | tf_op jit(solution)/shard_map/ppermute | solution.py:88
  133.7 5.6 %collective-permute-start.22 = (f32[128,128]{1,0:T(8,128)S(1)}, f32[128,128]{1,0:T(8,128)S(1)}, u32[]{:S(2)}, u32[]{:S(2)}) collective-permute-start(f32[128,128]{1,0:T(8,128)S(1)} %add_add_fusion.3), channel_id=1, source_target_pairs={{0,24},{1,25},{2,26},{3,27},{4,28},{5,29},{6,30},{7,31},{8,16},{9,... | collective-permute-start | bytes 196616 | tf_op jit(solution)/shard_map/ppermute | solution.py:67
  133.8 7.4 %collective-permute-start.21 = (f32[128,128]{1,0:T(8,128)S(1)}, f32[128,128]{1,0:T(8,128)S(1)}, u32[]{:S(2)}, u32[]{:S(2)}) collective-permute-start(f32[128,128]{1,0:T(8,128)S(1)} %add_add_fusion.3), channel_id=1, source_target_pairs={{0,16},{1,17},{2,18},{3,19},{4,20},{5,21},{6,22},{7,23},{8,24},{9,... | collective-permute-start | bytes 196616 | tf_op jit(solution)/shard_map/ppermute | solution.py:67
  137.0 4.3 %collective-permute-start.20 = (f32[128,128]{1,0:T(8,128)S(1)}, f32[128,128]{1,0:T(8,128)S(1)}, u32[]{:S(2)}, u32[]{:S(2)}) collective-permute-start(f32[128,128]{1,0:T(8,128)S(1)} %add_add_fusion.3), channel_id=1, source_target_pairs={{0,8},{1,9},{2,10},{3,11},{4,12},{5,13},{6,14},{7,15},{8,0},{9,1},... | collective-permute-start | bytes 196616 | tf_op jit(solution)/shard_map/ppermute | solution.py:67
  142.6 9.1 %collective-permute-start.25 = (f32[2,40,128]{2,1,0:T(8,128)S(1)}, f32[2,40,128]{2,1,0:T(8,128)S(1)}, u32[]{:S(2)}, u32[]{:S(2)}) collective-permute-start(f32[2,40,128]{2,1,0:T(8,128)S(1)} %get-tuple-element.68), channel_id=1, source_target_pairs={{0,32},{32,0},{64,96},{96,64},{128,160},{160,128},{192,224},{224,1... | collective-permute-start | bytes 122888 | tf_op jit(solution)/shard_map/ppermute | solution.py:60
  145.5 15.3 %collective-permute-start.28 = (f32[2,40,128]{2,1,0:T(8,128)S(1)}, f32[2,40,128]{2,1,0:T(8,128)S(1)}, u32[]{:S(2)}, u32[]{:S(2)}) collective-permute-start(f32[2,40,128]{2,1,0:T(8,128)S(1)} %get-tuple-element.72), channel_id=1, source_target_pairs={{0,64},{32,96},{64,0},{96,32},{128,192},{160,224},{192,128},{224,1... | collective-permute-start | bytes 122888 | tf_op jit(solution)/shard_map/ppermute | solution.py:60
  147.8 12.9 %collective-permute-start.29 = (f32[2,40,128]{2,1,0:T(8,128)S(1)}, f32[2,40,128]{2,1,0:T(8,128)S(1)}, u32[]{:S(2)}, u32[]{:S(2)}) collective-permute-start(f32[2,40,128]{2,1,0:T(8,128)S(1)} %get-tuple-element.73), channel_id=1, source_target_pairs={{0,96},{32,64},{64,32},{96,0},{128,224},{160,192},{192,160},{224,1... | collective-permute-start | bytes 122888 | tf_op jit(solution)/shard_map/ppermute | solution.py:60
  153.0 17.8 %collective-permute-start.26 = (f32[8,144,128]{2,1,0:T(8,128)S(1)}, f32[8,144,128]{2,1,0:T(8,128)S(1)}, u32[]{:S(2)}, u32[]{:S(2)}) collective-permute-start(f32[8,144,128]{2,1,0:T(8,128)S(1)} %pad_maximum_fusion), channel_id=1, source_target_pairs={{0,1},{1,2},{2,3},{3,4},{4,5},{5,6},{6,7},{7,8},{8,9},{9,10},{10,1... | collective-permute-start | bytes 1769480 | tf_op jit(solution)/shard_map/ppermute | solution.py:83
  155.0 15.8 %collective-permute-start.27 = (f32[8,144,128]{2,1,0:T(8,128)S(1)}, f32[8,144,128]{2,1,0:T(8,128)S(1)}, u32[]{:S(2)}, u32[]{:S(2)}) collective-permute-start(f32[8,144,128]{2,1,0:T(8,128)S(1)} %pad_maximum_fusion.1), channel_id=1, source_target_pairs={{1,0},{2,1},{3,2},{4,3},{5,4},{6,5},{7,6},{8,7},{9,8},{10,9},{11,1... | collective-permute-start | bytes 1769480 | tf_op jit(solution)/shard_map/ppermute | solution.py:88
  160.8 7.8 %collective-permute-start.30 = (f32[40,128]{1,0:T(8,128)S(1)}, f32[40,128]{1,0:T(8,128)S(1)}, u32[]{:S(2)}, u32[]{:S(2)}) collective-permute-start(f32[40,128]{1,0:T(8,128)S(1)} %get-tuple-element.92), channel_id=1, source_target_pairs={{0,128},{32,160},{64,192},{96,224},{128,0},{160,32},{192,64},{224,... | collective-permute-start | bytes 61448 | tf_op jit(solution)/shard_map/ppermute | solution.py:60
  168.6 2.2 %copy-start.1 = (f32[8,16,1024]{2,1,0:T(8,128)S(1)}, f32[8,16,1024]{2,1,0:T(8,128)}, u32[]{:S(2)}) copy-start(f32[8,16,1024]{2,1,0:T(8,128)} %get-tuple-element.76.east1_ref) | copy-start | bytes 1572868
  168.6 2.3 %copy-start.2 = (f32[8,16,1024]{2,1,0:T(8,128)S(1)}, f32[8,16,1024]{2,1,0:T(8,128)}, u32[]{:S(2)}) copy-start(f32[8,16,1024]{2,1,0:T(8,128)} %get-tuple-element.77.north1_ref) | copy-start | bytes 1572868
  168.6 2.3 %copy-start.3 = (f32[8,16,1024]{2,1,0:T(8,128)S(1)}, f32[8,16,1024]{2,1,0:T(8,128)}, u32[]{:S(2)}) copy-start(f32[8,16,1024]{2,1,0:T(8,128)} %get-tuple-element.78.east2_ref) | copy-start | bytes 1572868
  168.6 2.3 %copy-start.4 = (f32[8,16,1024]{2,1,0:T(8,128)S(1)}, f32[8,16,1024]{2,1,0:T(8,128)}, u32[]{:S(2)}) copy-start(f32[8,16,1024]{2,1,0:T(8,128)} %get-tuple-element.79.north2_ref) | copy-start | bytes 1572868
  174.4 15.0 %all-to-all-start.4 = ((f32[8,8,1024]{2,1,0:T(8,128)}), f32[8,8,1024]{2,1,0:T(8,128)S(1)}, u32[]{:S(2)}, u32[]{:S(2)}) async-start(f32[8,8,1024]{2,1,0:T(8,128)} %broadcast_in_dim.8), calls=%async_computation.4 | async-start | bytes 524288 | tf_op jit(solution)/shard_map/all_to_all | solution.py:50
  (2 other events, 1.2 us)

commit v5 on v4

--- a/solution.py
+++ b/solution.py
@@ -13,7 +13,6 @@
 HALO = 4
 HIGHEST = lax.Precision.HIGHEST
 STATE_EDGE = ((0, 4), (1, 3), (2, 3))
-ADJOINT_EDGE = ((0, 4), (2, 3), (1, 2))
 VMEM = pl.BlockSpec(memory_space=pltpu.VMEM)
 HBM = pl.BlockSpec(memory_space=pltpu.HBM)
 SMEM = pl.BlockSpec(memory_space=pltpu.SMEM)
@@ -93,9 +92,9 @@
     return pltpu.roll(field, width - 1, 1) - pltpu.roll(field, 1, 1)
 
 
-def dot(a, b, dims=((1,), (0,))):
+def dot(a, b, dims=((1,), (0,)), precision=HIGHEST):
     return lax.dot_general(
-        a, b, (dims, ((), ())), precision=HIGHEST, preferred_element_type=jnp.float32
+        a, b, (dims, ((), ())), precision=precision, preferred_element_type=jnp.float32
     )
 
 
@@ -229,6 +228,40 @@
         copy.wait()
 
 
+def boundary(sign, h, e, n, d):
+    def north(i):
+        return n(i) + sign * WAVE_COEF * d(i) * (h(i - 1) - h(i + 1))
+
+    def east(i):
+        return e(i) + WAVE_COEF * d(i) * cols(h(i))
+
+    near = east(1)
+    later = h(1) + WAVE_COEF * (cols(near) - sign * north(2))
+    beyond = h(2) + WAVE_COEF * (cols(east(2)) - sign * north(3))
+    first = n(1) - sign * WAVE_COEF * d(1) * h(2)
+    second = SPIN_COEF * near - sign * WAVE_COEF * d(1) * beyond
+    return h(1), later, first, second
+
+
+def edges_kernel(back_ref, depth_ref, tail_ref, head_ref):
+    own = depth_ref.shape[0]
+    groups = back_ref.shape[0]
+
+    def field(f, at):
+        return lambda i: jnp.concatenate(
+            [back_ref[j, f * own + at(i)] for j in range(groups)], axis=1
+        )
+
+    for sign, out_ref, at in (
+        (1.0, tail_ref, lambda i: own - i),
+        (-1.0, head_ref, lambda i: i - 1),
+    ):
+        depth = lambda i: depth_ref[at(i) : at(i) + 1]
+        found = boundary(sign, field(0, at), field(1, at), field(2, at), depth)
+        for q, row in enumerate(found):
+            out_ref[q] = row
+
+
 def backward_kernel(
     inside_ref, back_ref, above_ref, below_ref, seen_ref, depth_ref,
     east1_ref, north1_ref, east2_ref, north2_ref,
@@ -238,40 +271,49 @@
     own, size, width = east1_ref.shape
     groups = back_ref.shape[0]
     low, high = HALO, HALO + own
-    wide = lambda ref, at: jnp.concatenate([ref[j, at] for j in range(groups)], axis=1)
-    row, _ = padded_rows(
-        ADJOINT_EDGE,
-        size,
-        lambda f, r: wide(back_ref, f * own + r),
-        lambda i: wide(above_ref, slice(i, i + size)),
-        lambda i: wide(below_ref, slice(i, i + size)),
-    )
-    row = functools.partial(row, own_rows=own)
+    none = jnp.zeros((size, width), jnp.float32)
+
+    def row(f, p):
+        at = f * own + p - low
+        return jnp.concatenate([back_ref[j, at] for j in range(groups)], axis=1)
 
     def d(p):
         return depth_ref[p : p + 1]
 
-    for p in range(0, high + HALO):
+    for p in range(low, high):
         h2[p] = row(0, p) + seen_ref[p]
-    for p in range(low - 3, high + 3):
+    sides = (
+        (1.0, above_ref, low, lambda i: low - i),
+        (-1.0, below_ref, high - 1, lambda i: high - 1 + i),
+    )
+    for sign, sent_ref, edge, at in sides:
+        seen = boundary(
+            sign, lambda i: seen_ref[at(i)], lambda i: none, lambda i: none, lambda i: d(at(i))
+        )
+        out = at(1)
+        h2[out] = sent_ref[0] + seen[0]
+        h1[out] = sent_ref[1] + seen[1]
+        nt[out] = sent_ref[2] + seen[2] + sign * WAVE_COEF * d(out) * h2[edge]
+        n1[out] = sent_ref[3] + seen[3] + nt[out] * (1.0 - WAVE_COEF * WAVE_COEF * d(out))
+    for p in range(low, high):
+        nt[p] = row(2, p) + d(p) * WAVE_COEF * (h2[p + 1] - h2[p - 1])
+    for p in range(low, high):
+        r = p - low
+        across = WAVE_COEF * cols(h2[p])
         along = WAVE_COEF * (h2[p + 1] - h2[p - 1])
-        nt[p] = row(2, p) + d(p) * along
-    for p in range(low - 2, high + 2):
-        across = WAVE_COEF * cols(h2[p])
         total = row(1, p) + d(p) * across
-        h1[p] = (h2[p] + WAVE_COEF * (cols(total) + (nt[p + 1] - nt[p - 1]))) * inside_ref[p]
-        if low - 1 <= p < high + 1:
-            n1[p] = nt[p] + SPIN_COEF * total
-        if low <= p < high:
-            r = p - low
-            e1[p] = total - SPIN_COEF * nt[p]
-            along = WAVE_COEF * (h2[p + 1] - h2[p - 1])
-            depth_grad_ref[r : r + 1] = jnp.sum(
-                east2_ref[r] * across + north2_ref[r] * along, axis=0, keepdims=True
-            )
-    for p in range(low - 1, high + 1):
-        along = WAVE_COEF * (h1[p + 1] - h1[p - 1])
-        nt[p] = n1[p] + d(p) * along
+        h1[p] = h2[p] + WAVE_COEF * (cols(total) + (nt[p + 1] - nt[p - 1]))
+        n1[p] = nt[p] + SPIN_COEF * total
+        e1[p] = total - SPIN_COEF * nt[p]
+        depth_grad_ref[r : r + 1] = jnp.sum(
+            east2_ref[r] * across + north2_ref[r] * along, axis=0, keepdims=True
+        )
+    for sign, _, edge, at in sides:
+        out = at(1)
+        h1[out] = (h1[out] + sign * WAVE_COEF * nt[edge]) * inside_ref[out]
+        nt[out] = n1[out] + sign * WAVE_COEF * d(out) * h1[edge]
+    for p in range(low, high):
+        nt[p] = n1[p] + d(p) * WAVE_COEF * (h1[p + 1] - h1[p - 1])
     height_ref[...] = h1[low - 1 : high + 1]
     for p in range(low, high):
         r = p - low
@@ -430,7 +472,7 @@
             [jnp.where(lane // block == i, obs_grad, 0.0) for i in range(2 * groups)], axis=0
         )
         hit = (sub == index.astype(jnp.int32)).astype(jnp.float32)
-        put = dot(apart, hit, ((1,), (1,)))
+        put = dot(apart, hit, ((1,), (1,)), lax.Precision.HIGH)
         for h in range(2):
             for j in range(groups):
                 at = (h * groups + j) * size
@@ -601,23 +643,20 @@
     back, parts[1] = lax.optimization_barrier((back, parts[1]))
     whole = sum(parts[1:], parts[0])
 
-    by_field = back.reshape(groups, fields, own_rows, own_members, block_cols)
-
-    def adjoint_edge(take):
-        parts = [
-            by_field[:, f, take(n)].reshape(groups, -1, block_cols) for f, n in ADJOINT_EDGE
-        ]
-        return jnp.concatenate(parts, axis=1)
-
-    adjoint_tail = adjoint_edge(lambda n: slice(own_rows - n, own_rows))
-    adjoint_head = adjoint_edge(lambda n: slice(0, n))
+    adjoint_tail, adjoint_head = kernel_call(
+        edges_kernel,
+        [(4, own_members, width)] * 2,
+        [back, depth_field],
+        flops=10**7,
+        name="edges",
+    )
     adjoint_above, adjoint_below = from_above(adjoint_tail), from_below(adjoint_head)
     whole, _, _ = lax.optimization_barrier((whole, adjoint_tail, adjoint_head))
     (seen,) = kernel_call(
         observe_kernel,
         [padded],
         [whole[0], crossed(whole[1], near), obs_tall],
-        flops=10**9,
+        flops=10**11,
         name="observe",
     )
     depth_tall = jnp.concatenate([above[-1, half:own_rows], depth_field, below[-1, :half]])

time: 192 us -> 191 us (level)
    ppermute x4, waiting for transfers between devices: 8.33 us -> 4.58 us  [crossed(): return lax.ppermute(block, 'ens', [(i, i ^ distance) for i in range(count)])]
    pallas_call x10 -> x11, Pallas kernels: 35.2 us -> 35.7 us  [kernel_call(): pl.pallas_call(body, out_shape=[made(i, o) for i, o in enumerate(outs)],...]
  transfers between devices with their start and end apart: 36 -> 36, of which waited for: 21 -> 22; matrix products, arithmetic and copies ran while one was open for 1% -> 1% of each run, Pallas kernels for 17% -> 17%
where the time goes in v5:
time: 191 us; the launch traced here: 189 us
  starting transfers between devices  89.9 us (47%)
  waiting for transfers between devices  55.3 us (29%)
  Pallas kernels  35.7 us (19%)
  local copies, waits for them, and re-layouts  4.22 us (2%)
  other arithmetic  2.43 us (1%)
    pallas_call x11, Pallas kernels, kernel_call(): pl.pallas_call(body, out_shape=[made(i, o) for i, o in enumerate(outs)],...  35.7 us
    ppermute x3, starting transfers between devices, from_below(): lax.ppermute(rows_sent, 'space', [(i + 1, i) for i in range(count - 1)])  17.3 us
    ppermute x14, starting transfers between devices, other(): lax.ppermute(block, 'space', [(i, i ^ distance) for i in range(count)])  17.1 us
    all_to_all x2, waiting for transfers between devices, gathered(): return lax.all_to_all(copies, axis, 0, 0, tiled=False)  15.1 us
    ppermute x7, starting transfers between devices, turned(): lax.ppermute(block, 'ens', [(i, (i + distance) % count) for i in range(co...  14.8 us
    all_to_all x3, starting transfers between devices, exchanged(): return lax.all_to_all(blocks, 'ens', 0, 0, tiled=False)  14.7 us
    ppermute x14, waiting for transfers between devices, other(): lax.ppermute(block, 'space', [(i, i ^ distance) for i in range(count)])  13.4 us
    all_to_all x2, starting transfers between devices, gathered(): return lax.all_to_all(copies, axis, 0, 0, tiled=False)  12.6 us
  transfers between devices with their start and end apart: 36, of which 22 were waited for; matrix products, arithmetic and copies ran while one was open for 1% of the time, Pallas kernels for 17%

profile of v5, /device:TPU:6, one launch (start us, length us, event | category | flops | bytes accessed | tf_op | source)
XLA Modules:
  0.0 188.6 jit_solution(14792250866411902349)
XLA Ops:
  2.8 8.5 %all-to-all-start = ((f32[8,24,128]{2,1,0:T(8,128)}), f32[8,24,128]{2,1,0:T(8,128)S(1)}, u32[]{:S(2)}, u32[]{:S(2)}) async-start(f32[8,24,128]{2,1,0:T(8,128)} %broadcast_in_dim.7), calls=%async_computation | async-start | bytes 196608 | tf_op jit(solution)/shard_map/all_to_all | solution.py:49
  11.3 3.3 %prepare.1 = (f32[11,16,1024]{2,1,0:T(8,128)}, f32[11,16,1024]{2,1,0:T(8,128)}, f32[8,384,128]{2,1,0:T(8,128)}) custom-call(f32[3,8,16,1024]{3,2,1,0:T(8,128)} %state_ref.3, f32[8,1024]{1,0:T(8,128)} %depth_ref.5, f32[384,1024]{1,0:T(8,128)} %bitcast.25), custom_call_target="tpu_custom_call" | custom-call | bytes 6193152 | tf_op jit(solution)/shard_map/prepare/pallas_call | solution.py:29
  14.6 5.4 %all-to-all-done = f32[8,24,128]{2,1,0:T(8,128)S(1)} async-done(((f32[8,24,128]{2,1,0:T(8,128)}), f32[8,24,128]{2,1,0:T(8,128)S(1)}, u32[]{:S(2)}, u32[]{:S(2)}) %all-to-all-start) | async-done | bytes 98336 | tf_op jit(solution)/shard_map/all_to_all | solution.py:49
  20.0 3.7 %all-to-all-start.1 = ((f32[8,384,128]{2,1,0:T(8,128)}), f32[8,384,128]{2,1,0:T(8,128)S(1)}, u32[]{:S(2)}, u32[]{:S(2)}) async-start(f32[8,384,128]{2,1,0:T(8,128)} %get-tuple-element.61), calls=%async_computation.1 | async-start | bytes 3145728 | tf_op jit(solution)/shard_map/all_to_all | solution.py:43
  23.7 1.9 %collective-permute-start = (f32[11,16,1024]{2,1,0:T(8,128)}, f32[11,16,1024]{2,1,0:T(8,128)}, u32[]{:S(2)}, u32[]{:S(2)}) collective-permute-start(f32[11,16,1024]{2,1,0:T(8,128)} %get-tuple-element.47), channel_id=1, source_target_pairs={{0,1},{1,2},{2,3},{3,4},{4,5},{5,6},{6,7},{7,8},{8,9},{9,10},{10,1... | collective-permute-start | bytes 2162696 | tf_op jit(solution)/shard_map/ppermute | solution.py:82
  25.7 5.8 %collective-permute-start.1 = (f32[11,16,1024]{2,1,0:T(8,128)}, f32[11,16,1024]{2,1,0:T(8,128)}, u32[]{:S(2)}, u32[]{:S(2)}) collective-permute-start(f32[11,16,1024]{2,1,0:T(8,128)} %get-tuple-element.48), channel_id=1, source_target_pairs={{1,0},{2,1},{3,2},{4,3},{5,4},{6,5},{7,6},{8,7},{9,8},{10,9},{11,1... | collective-permute-start | bytes 2162696 | tf_op jit(solution)/shard_map/ppermute | solution.py:87
  31.8 7.0 %collective-permute-done.above_ref = f32[11,16,1024]{2,1,0:T(8,128)} collective-permute-done((f32[11,16,1024]{2,1,0:T(8,128)}, f32[11,16,1024]{2,1,0:T(8,128)}, u32[]{:S(2)}, u32[]{:S(2)}) %collective-permute-start) | collective-permute-done | bytes 720928 | tf_op jit(solution)/shard_map/ppermute | solution.py:82
  38.8 1.8 collective-permute-done.1.below_ref
  40.5 5.2 %forward.1 = (f32[8,24,16,128]{3,2,1,0:T(8,128)}, f32[4,16,128]{2,1,0:T(8,128)S(1)}, f32[8,16,1024]{2,1,0:T(8,128)}, f32[8,16,1024]{2,1,0:T(8,128)}, f32[8,16,1024]{2,1,0:T(8,128)}, /*index=5*/f32[8,16,1024]{2,1,0:T(8,128)}) custom-call(f32[16]{0:T(128)S(1)} %and_convert_fusion.inside_ref, f32[3,8,16,1024]{3,2,1,0:T(8,128)S(1)} %copy-done, ...), custom_call_target="tpu_custom_call" | custom-call | flops 100000000 | bytes 6752320 | tf_op jit(solution)/shard_map/forward/pallas_call | solution.py:29
  45.8 3.2 %collective-permute-start.8 = (f32[4,16,128]{2,1,0:T(8,128)S(1)}, f32[4,16,128]{2,1,0:T(8,128)S(1)}, u32[]{:S(2)}, u32[]{:S(2)}) collective-permute-start(f32[4,16,128]{2,1,0:T(8,128)S(1)} %get-tuple-element.51.refs_0_), channel_id=1, source_target_pairs={{0,224},{32,0},{64,32},{96,64},{128,96},{160,128},{192,160},{224,1... | collective-permute-start | bytes 98312 | tf_op jit(solution)/shard_map/ppermute | solution.py:54
  49.0 2.3 %collective-permute-start.7 = (f32[4,16,128]{2,1,0:T(8,128)S(1)}, f32[4,16,128]{2,1,0:T(8,128)S(1)}, u32[]{:S(2)}, u32[]{:S(2)}) collective-permute-start(f32[4,16,128]{2,1,0:T(8,128)S(1)} %get-tuple-element.51.refs_0_), channel_id=1, source_target_pairs={{0,192},{32,224},{64,0},{96,32},{128,64},{160,96},{192,128},{224,1... | collective-permute-start | bytes 98312 | tf_op jit(solution)/shard_map/ppermute | solution.py:54
  51.4 1.4 collective-permute-start.6
  52.8 3.6 %collective-permute-start.5 = (f32[4,16,128]{2,1,0:T(8,128)S(1)}, f32[4,16,128]{2,1,0:T(8,128)S(1)}, u32[]{:S(2)}, u32[]{:S(2)}) collective-permute-start(f32[4,16,128]{2,1,0:T(8,128)S(1)} %get-tuple-element.51.refs_0_), channel_id=1, source_target_pairs={{0,128},{32,160},{64,192},{96,224},{128,0},{160,32},{192,64},{224,... | collective-permute-start | bytes 98312 | tf_op jit(solution)/shard_map/ppermute | solution.py:54
  56.7 5.8 %collective-permute-done.8.refs_7_ = f32[4,16,128]{2,1,0:T(8,128)S(1)} collective-permute-done((f32[4,16,128]{2,1,0:T(8,128)S(1)}, f32[4,16,128]{2,1,0:T(8,128)S(1)}, u32[]{:S(2)}, u32[]{:S(2)}) %collective-permute-start.8) | collective-permute-done | bytes 32800 | tf_op jit(solution)/shard_map/ppermute | solution.py:54
  62.5 4.0 %collective-permute-start.2 = (f32[4,16,128]{2,1,0:T(8,128)S(1)}, f32[4,16,128]{2,1,0:T(8,128)S(1)}, u32[]{:S(2)}, u32[]{:S(2)}) collective-permute-start(f32[4,16,128]{2,1,0:T(8,128)S(1)} %get-tuple-element.51.refs_0_), channel_id=1, source_target_pairs={{0,32},{32,64},{64,96},{96,128},{128,160},{160,192},{192,224},{224... | collective-permute-start | bytes 98312 | tf_op jit(solution)/shard_map/ppermute | solution.py:54
  66.5 2.0 %collective-permute-done.3.refs_2_ = f32[4,16,128]{2,1,0:T(8,128)S(1)} collective-permute-done((f32[4,16,128]{2,1,0:T(8,128)S(1)}, f32[4,16,128]{2,1,0:T(8,128)S(1)}, u32[]{:S(2)}, u32[]{:S(2)}) %collective-permute-start.3) | collective-permute-done | bytes 32800 | tf_op jit(solution)/shard_map/ppermute | solution.py:54
  69.1 5.9 %all-to-all-start.3 = ((f32[8,24,16,128]{3,2,1,0:T(8,128)}), f32[8,24,16,128]{3,2,1,0:T(8,128)}, u32[]{:S(2)}, u32[]{:S(2)}) async-start(f32[8,24,16,128]{3,2,1,0:T(8,128)} %get-tuple-element.62), calls=%async_computation.3 | async-start | bytes 3145728 | tf_op jit(solution)/shard_map/all_to_all | solution.py:43
  75.2 2.0 %gram.1 = (f32[4,128,128]{2,1,0:T(8,128)S(1)}, f32[4,8,128]{2,1,0:T(8,128)S(1)}, f32[136,128]{1,0:T(8,128)S(1)}) custom-call(s32[1]{0:T(128)} %bitcast.place_ref, f32[3,4,128]{2,1,0:T(4,128)S(1)} %reshape.22.params_ref, f32[4,16,128]{2,1,0:T(8,128)} %copy-done.6, f32[4,16,128]{2,1,0:T(8,128)} %copy-done.13, f32[4,16,128]{2,1,0:T(8,128)} %copy-done.12, ...), custom_call_target="tpu_custom_call" | custom-call | flops 100663296 | bytes 616452 | tf_op jit(solution)/shard_map/gram/pallas_call | solution.py:29
  78.5 3.0 %collective-permute-start.12 = (f32[136,128]{1,0:T(8,128)S(1)}, f32[136,128]{1,0:T(8,128)S(1)}, u32[]{:S(2)}, u32[]{:S(2)}) collective-permute-start(f32[136,128]{1,0:T(8,128)S(1)} %add.62), channel_id=1, source_target_pairs={{0,6},{1,7},{2,4},{3,5},{4,2},{5,3},{6,0},{7,1},{8,14},{9,15},{10,... | collective-permute-start | bytes 208904 | tf_op jit(solution)/shard_map/ppermute | solution.py:66
  82.7 2.2 %collective-permute-done.12 = f32[136,128]{1,0:T(8,128)S(1)} collective-permute-done((f32[136,128]{1,0:T(8,128)S(1)}, f32[136,128]{1,0:T(8,128)S(1)}, u32[]{:S(2)}, u32[]{:S(2)}) %collective-permute-start.12) | collective-permute-done | bytes 69664 | tf_op jit(solution)/shard_map/ppermute | solution.py:66
  84.9 2.9 %collective-permute-done.11 = f32[136,128]{1,0:T(8,128)S(1)} collective-permute-done((f32[136,128]{1,0:T(8,128)S(1)}, f32[136,128]{1,0:T(8,128)S(1)}, u32[]{:S(2)}, u32[]{:S(2)}) %collective-permute-start.11) | collective-permute-done | bytes 69664 | tf_op jit(solution)/shard_map/ppermute | solution.py:66
  88.6 2.4 %collective-permute-start.14 = (f32[136,128]{1,0:T(8,128)S(1)}, f32[136,128]{1,0:T(8,128)S(1)}, u32[]{:S(2)}, u32[]{:S(2)}) collective-permute-start(f32[136,128]{1,0:T(8,128)S(1)} %add_add_fusion.1), channel_id=1, source_target_pairs={{0,16},{1,17},{2,18},{3,19},{4,20},{5,21},{6,22},{7,23},{8,24},{9,... | collective-permute-start | bytes 208904 | tf_op jit(solution)/shard_map/ppermute | solution.py:66
  92.2 1.4 collective-permute-done.15
  95.3 11.2 %factor.1 = (f32[128,128]{1,0:T(8,128)S(1)}, f32[128,128]{1,0:T(8,128)S(1)}, f32[8,128]{1,0:T(8,128)S(1)}) custom-call(f32[136,128]{1,0:T(8,128)S(1)} %add_add_fusion.gram_ref), custom_call_target="tpu_custom_call" | custom-call | flops 1000000000 | bytes 204800 | tf_op jit(solution)/shard_map/factor/pallas_call | solution.py:29
  106.6 2.2 %mix.1 = f32[8,24,16,128]{3,2,1,0:T(8,128)} custom-call(f32[128,128]{1,0:T(8,128)S(1)} %get-tuple-element.60.mixing_ref, f32[8,24,16,128]{3,2,1,0:T(8,128)S(1)} %bitcast.23), custom_call_target="tpu_custom_call" | custom-call | flops 10000000000 | bytes 3211264 | tf_op jit(solution)/shard_map/mix/pallas_call | solution.py:29
  108.8 2.2 %all-to-all-done.3.state_ref = f32[8,24,16,128]{3,2,1,0:T(8,128)} async-done(((f32[8,24,16,128]{3,2,1,0:T(8,128)}), f32[8,24,16,128]{3,2,1,0:T(8,128)}, u32[]{:S(2)}, u32[]{:S(2)}) %all-to-all-start.3) | async-done | bytes 1572896 | tf_op jit(solution)/shard_map/all_to_all | solution.py:43
  111.0 5.0 %all-to-all-start.2 = ((f32[8,24,16,128]{3,2,1,0:T(8,128)}), f32[8,24,16,128]{3,2,1,0:T(8,128)S(1)}, u32[]{:S(2)}, u32[]{:S(2)}) async-start(f32[8,24,16,128]{3,2,1,0:T(8,128)} %mix.1), calls=%async_computation.2 | async-start | bytes 3145728 | tf_op jit(solution)/shard_map/all_to_all | solution.py:43
  116.8 3.4 %cross.1 = f32[128,128]{1,0:T(8,128)S(1)} custom-call(f32[8,24,16,128]{3,2,1,0:T(8,128)} %all-to-all-done.3.state_ref, f32[8,24,16,128]{3,2,1,0:T(8,128)S(1)} %bitcast.24), custom_call_target="tpu_custom_call" | custom-call | flops 10000000000 | bytes 3211264 | tf_op jit(solution)/shard_map/cross/pallas_call | solution.py:29
  121.6 1.4 collective-permute-start.19
  123.0 1.7 collective-permute-start.18
  125.9 1.9 %collective-permute-start.23 = (f32[4,136,64]{2,1,0:T(8,128)S(1)}, f32[4,136,64]{2,1,0:T(8,128)S(1)}, u32[]{:S(2)}, u32[]{:S(2)}) collective-permute-start(f32[4,136,64]{2,1,0:T(8,128)S(1)} %get-tuple-element.88), channel_id=1, source_target_pairs={{0,1},{1,2},{2,3},{3,4},{4,5},{5,6},{6,7},{7,8},{8,9},{9,10},{10,1... | collective-permute-start | bytes 417800 | tf_op jit(solution)/shard_map/ppermute | solution.py:82
  127.9 5.8 %collective-permute-start.24 = (f32[4,136,64]{2,1,0:T(8,128)S(1)}, f32[4,136,64]{2,1,0:T(8,128)S(1)}, u32[]{:S(2)}, u32[]{:S(2)}) collective-permute-start(f32[4,136,64]{2,1,0:T(8,128)S(1)} %get-tuple-element.89), channel_id=1, source_target_pairs={{1,0},{2,1},{3,2},{4,3},{5,4},{6,5},{7,6},{8,7},{9,8},{10,9},{11,1... | collective-permute-start | bytes 417800 | tf_op jit(solution)/shard_map/ppermute | solution.py:87
  133.8 3.2 %collective-permute-start.21 = (f32[128,128]{1,0:T(8,128)S(1)}, f32[128,128]{1,0:T(8,128)S(1)}, u32[]{:S(2)}, u32[]{:S(2)}) collective-permute-start(f32[128,128]{1,0:T(8,128)S(1)} %add_add_fusion.3), channel_id=1, source_target_pairs={{0,16},{1,17},{2,18},{3,19},{4,20},{5,21},{6,22},{7,23},{8,24},{9,... | collective-permute-start | bytes 196616 | tf_op jit(solution)/shard_map/ppermute | solution.py:66
  139.3 1.9 %collective-permute-done.21 = f32[128,128]{1,0:T(8,128)S(1)} collective-permute-done((f32[128,128]{1,0:T(8,128)S(1)}, f32[128,128]{1,0:T(8,128)S(1)}, u32[]{:S(2)}, u32[]{:S(2)}) %collective-permute-start.21) | collective-permute-done | bytes 65568 | tf_op jit(solution)/shard_map/ppermute | solution.py:66
  141.3 1.3 pullback.1
  142.6 2.1 %collective-permute-start.25 = (f32[2,40,128]{2,1,0:T(8,128)S(1)}, f32[2,40,128]{2,1,0:T(8,128)S(1)}, u32[]{:S(2)}, u32[]{:S(2)}) collective-permute-start(f32[2,40,128]{2,1,0:T(8,128)S(1)} %get-tuple-element.70), channel_id=1, source_target_pairs={{0,32},{32,0},{64,96},{96,64},{128,160},{160,128},{192,224},{224,1... | collective-permute-start | bytes 122888 | tf_op jit(solution)/shard_map/ppermute | solution.py:59
  144.7 2.4 %collective-permute-start.28 = (f32[2,40,128]{2,1,0:T(8,128)S(1)}, f32[2,40,128]{2,1,0:T(8,128)S(1)}, u32[]{:S(2)}, u32[]{:S(2)}) collective-permute-start(f32[2,40,128]{2,1,0:T(8,128)S(1)} %get-tuple-element.76), channel_id=1, source_target_pairs={{0,64},{32,96},{64,0},{96,32},{128,192},{160,224},{192,128},{224,1... | collective-permute-start | bytes 122888 | tf_op jit(solution)/shard_map/ppermute | solution.py:59
  147.9 3.6 %collective-permute-done.25 = f32[2,40,128]{2,1,0:T(8,128)S(1)} collective-permute-done((f32[2,40,128]{2,1,0:T(8,128)S(1)}, f32[2,40,128]{2,1,0:T(8,128)S(1)}, u32[]{:S(2)}, u32[]{:S(2)}) %collective-permute-start.25) | collective-permute-done | bytes 40992 | tf_op jit(solution)/shard_map/ppermute | solution.py:59
  151.5 1.3 all-to-all-done.2.back_ref
  154.4 3.1 %collective-permute-start.30 = (f32[40,128]{1,0:T(8,128)S(1)}, f32[40,128]{1,0:T(8,128)S(1)}, u32[]{:S(2)}, u32[]{:S(2)}) collective-permute-start(f32[40,128]{1,0:T(8,128)S(1)} %get-tuple-element.90), channel_id=1, source_target_pairs={{0,128},{32,160},{64,192},{96,224},{128,0},{160,32},{192,64},{224,... | collective-permute-start | bytes 61448 | tf_op jit(solution)/shard_map/ppermute | solution.py:59
  157.6 1.9 %collective-permute-start.26 = (f32[4,16,1024]{2,1,0:T(8,128)S(1)}, f32[4,16,1024]{2,1,0:T(8,128)S(1)}, u32[]{:S(2)}, u32[]{:S(2)}) collective-permute-start(f32[4,16,1024]{2,1,0:T(8,128)S(1)} %get-tuple-element.72), channel_id=1, source_target_pairs={{0,1},{1,2},{2,3},{3,4},{4,5},{5,6},{6,7},{7,8},{8,9},{9,10},{10,1... | collective-permute-start | bytes 786440 | tf_op jit(solution)/shard_map/ppermute | solution.py:82
  159.5 5.8 %collective-permute-start.27 = (f32[4,16,1024]{2,1,0:T(8,128)S(1)}, f32[4,16,1024]{2,1,0:T(8,128)S(1)}, u32[]{:S(2)}, u32[]{:S(2)}) collective-permute-start(f32[4,16,1024]{2,1,0:T(8,128)S(1)} %get-tuple-element.73), channel_id=1, source_target_pairs={{1,0},{2,1},{3,2},{4,3},{5,4},{6,5},{7,6},{8,7},{9,8},{10,9},{11,1... | collective-permute-start | bytes 786440 | tf_op jit(solution)/shard_map/ppermute | solution.py:87
  165.3 2.2 %observe.1.seen_ref = f32[16,16,1024]{2,1,0:T(8,128)S(1)} custom-call(f32[40,128]{1,0:T(8,128)S(1)} %get-tuple-element.91.refs_0_, f32[40,128]{1,0:T(8,128)S(1)} %collective-permute-done.30.refs_1_, f32[8,136,128]{2,1,0:T(8,128)S(1)} %maximum_maximum_fusion.refs_2_), custom_call_target="tpu_custom_call" | custom-call | flops 99999997952 | bytes 1646592 | tf_op jit(solution)/shard_map/observe/pallas_call | solution.py:29
  167.5 1.6 collective-permute-done.27.below_ref
  169.1 2.7 %backward.1 = (f32[8,1024]{1,0:T(8,128)S(1)}, f32[10,16,1024]{2,1,0:T(8,128)S(1)}, f32[8,16,1024]{2,1,0:T(8,128)S(1)}, f32[10,16,1024]{2,1,0:T(8,128)S(1)}) custom-call(f32[16]{0:T(128)S(1)} %and_convert_fusion.inside_ref, f32[8,24,16,128]{3,2,1,0:T(8,128)S(1)} %all-to-all-done.2.back_ref, f32[4,16,1024]{2,1,0:T(8,128)S(1)} %collective-permute-done.26.above_ref, ...), custom_call_target="tpu_custom_call" | custom-call | flops 100000000 | bytes 7176256 | tf_op jit(solution)/shard_map/backward/pallas_call | solution.py:29
  172.6 4.1 %all-to-all-start.4 = ((f32[8,8,1024]{2,1,0:T(8,128)}), f32[8,8,1024]{2,1,0:T(8,128)S(1)}, u32[]{:S(2)}, u32[]{:S(2)}) async-start(f32[8,8,1024]{2,1,0:T(8,128)} %broadcast_in_dim.8), calls=%async_computation.4 | async-start | bytes 524288 | tf_op jit(solution)/shard_map/all_to_all | solution.py:49
  176.7 1.5 finish.1
  178.2 9.7 %all-to-all-done.4 = f32[8,8,1024]{2,1,0:T(8,128)S(1)} async-done(((f32[8,8,1024]{2,1,0:T(8,128)}), f32[8,8,1024]{2,1,0:T(8,128)S(1)}, u32[]{:S(2)}, u32[]{:S(2)}) %all-to-all-start.4) | async-done | bytes 262176 | tf_op jit(solution)/shard_map/all_to_all | solution.py:49
  (93 shorter events, 19.4 us)
Async XLA Ops:
  2.8 17.2 %all-to-all-start = ((f32[8,24,128]{2,1,0:T(8,128)}), f32[8,24,128]{2,1,0:T(8,128)S(1)}, u32[]{:S(2)}, u32[]{:S(2)}) async-start(f32[8,24,128]{2,1,0:T(8,128)} %broadcast_in_dim.7), calls=%async_computation | async-start | bytes 196608 | tf_op jit(solution)/shard_map/all_to_all | solution.py:49
  20.0 20.5 %copy-start = (f32[3,8,16,1024]{3,2,1,0:T(8,128)S(1)}, f32[3,8,16,1024]{3,2,1,0:T(8,128)}, u32[]{:S(2)}) copy-start(f32[3,8,16,1024]{3,2,1,0:T(8,128)} %state_ref.3) | copy-start | bytes 4718596
  20.0 20.5 %copy-start.1 = (f32[8,1024]{1,0:T(8,128)S(1)}, f32[8,1024]{1,0:T(8,128)}, u32[]{:S(2)}) copy-start(f32[8,1024]{1,0:T(8,128)} %depth_ref.5) | copy-start | bytes 98308
  20.0 48.5 %all-to-all-start.1 = ((f32[8,384,128]{2,1,0:T(8,128)}), f32[8,384,128]{2,1,0:T(8,128)S(1)}, u32[]{:S(2)}, u32[]{:S(2)}) async-start(f32[8,384,128]{2,1,0:T(8,128)} %get-tuple-element.61), calls=%async_computation.1 | async-start | bytes 3145728 | tf_op jit(solution)/shard_map/all_to_all | solution.py:43
  23.7 15.0 %collective-permute-start = (f32[11,16,1024]{2,1,0:T(8,128)}, f32[11,16,1024]{2,1,0:T(8,128)}, u32[]{:S(2)}, u32[]{:S(2)}) collective-permute-start(f32[11,16,1024]{2,1,0:T(8,128)} %get-tuple-element.47), channel_id=1, source_target_pairs={{0,1},{1,2},{2,3},{3,4},{4,5},{5,6},{6,7},{7,8},{8,9},{9,10},{10,1... | collective-permute-start | bytes 2162696 | tf_op jit(solution)/shard_map/ppermute | solution.py:82
  25.7 14.9 %collective-permute-start.1 = (f32[11,16,1024]{2,1,0:T(8,128)}, f32[11,16,1024]{2,1,0:T(8,128)}, u32[]{:S(2)}, u32[]{:S(2)}) collective-permute-start(f32[11,16,1024]{2,1,0:T(8,128)} %get-tuple-element.48), channel_id=1, source_target_pairs={{1,0},{2,1},{3,2},{4,3},{5,4},{6,5},{7,6},{8,7},{9,8},{10,9},{11,1... | collective-permute-start | bytes 2162696 | tf_op jit(solution)/shard_map/ppermute | solution.py:87
  45.8 22.7 %copy-start.6 = (f32[4,16,128]{2,1,0:T(8,128)}, f32[4,16,128]{2,1,0:T(8,128)S(1)}, u32[]{:S(2)}) copy-start(f32[4,16,128]{2,1,0:T(8,128)S(1)} %get-tuple-element.51.refs_0_) | copy-start | bytes 98308
  45.8 16.6 %collective-permute-start.8 = (f32[4,16,128]{2,1,0:T(8,128)S(1)}, f32[4,16,128]{2,1,0:T(8,128)S(1)}, u32[]{:S(2)}, u32[]{:S(2)}) collective-permute-start(f32[4,16,128]{2,1,0:T(8,128)S(1)} %get-tuple-element.51.refs_0_), channel_id=1, source_target_pairs={{0,224},{32,0},{64,32},{96,64},{128,96},{160,128},{192,160},{224,1... | collective-permute-start | bytes 98312 | tf_op jit(solution)/shard_map/ppermute | solution.py:54
  49.0 13.4 %collective-permute-start.7 = (f32[4,16,128]{2,1,0:T(8,128)S(1)}, f32[4,16,128]{2,1,0:T(8,128)S(1)}, u32[]{:S(2)}, u32[]{:S(2)}) collective-permute-start(f32[4,16,128]{2,1,0:T(8,128)S(1)} %get-tuple-element.51.refs_0_), channel_id=1, source_target_pairs={{0,192},{32,224},{64,0},{96,32},{128,64},{160,96},{192,128},{224,1... | collective-permute-start | bytes 98312 | tf_op jit(solution)/shard_map/ppermute | solution.py:54
  51.4 15.0 %collective-permute-start.6 = (f32[4,16,128]{2,1,0:T(8,128)S(1)}, f32[4,16,128]{2,1,0:T(8,128)S(1)}, u32[]{:S(2)}, u32[]{:S(2)}) collective-permute-start(f32[4,16,128]{2,1,0:T(8,128)S(1)} %get-tuple-element.51.refs_0_), channel_id=1, source_target_pairs={{0,160},{32,192},{64,224},{96,0},{128,32},{160,64},{192,96},{224,1... | collective-permute-start | bytes 98312 | tf_op jit(solution)/shard_map/ppermute | solution.py:54
  52.8 13.6 %collective-permute-start.5 = (f32[4,16,128]{2,1,0:T(8,128)S(1)}, f32[4,16,128]{2,1,0:T(8,128)S(1)}, u32[]{:S(2)}, u32[]{:S(2)}) collective-permute-start(f32[4,16,128]{2,1,0:T(8,128)S(1)} %get-tuple-element.51.refs_0_), channel_id=1, source_target_pairs={{0,128},{32,160},{64,192},{96,224},{128,0},{160,32},{192,64},{224,... | collective-permute-start | bytes 98312 | tf_op jit(solution)/shard_map/ppermute | solution.py:54
  56.4 10.0 %collective-permute-start.4 = (f32[4,16,128]{2,1,0:T(8,128)S(1)}, f32[4,16,128]{2,1,0:T(8,128)S(1)}, u32[]{:S(2)}, u32[]{:S(2)}) collective-permute-start(f32[4,16,128]{2,1,0:T(8,128)S(1)} %get-tuple-element.51.refs_0_), channel_id=1, source_target_pairs={{0,96},{32,128},{64,160},{96,192},{128,224},{160,0},{192,32},{224,... | collective-permute-start | bytes 98312 | tf_op jit(solution)/shard_map/ppermute | solution.py:54
  62.5 6.1 %copy-start.7 = (f32[4,16,128]{2,1,0:T(8,128)}, f32[4,16,128]{2,1,0:T(8,128)S(1)}, u32[]{:S(2)}) copy-start(f32[4,16,128]{2,1,0:T(8,128)S(1)} %collective-permute-done.8.refs_7_) | copy-start | bytes 98308
  62.5 6.0 %collective-permute-start.3 = (f32[4,16,128]{2,1,0:T(8,128)S(1)}, f32[4,16,128]{2,1,0:T(8,128)S(1)}, u32[]{:S(2)}, u32[]{:S(2)}) collective-permute-start(f32[4,16,128]{2,1,0:T(8,128)S(1)} %get-tuple-element.51.refs_0_), channel_id=1, source_target_pairs={{0,64},{32,96},{64,128},{96,160},{128,192},{160,224},{192,0},{224,... | collective-permute-start | bytes 98312 | tf_op jit(solution)/shard_map/ppermute | solution.py:54
  62.5 6.1 %copy-start.8 = (f32[4,16,128]{2,1,0:T(8,128)}, f32[4,16,128]{2,1,0:T(8,128)S(1)}, u32[]{:S(2)}) copy-start(f32[4,16,128]{2,1,0:T(8,128)S(1)} %collective-permute-done.7.refs_6_) | copy-start | bytes 98308
  62.5 6.0 %collective-permute-start.2 = (f32[4,16,128]{2,1,0:T(8,128)S(1)}, f32[4,16,128]{2,1,0:T(8,128)S(1)}, u32[]{:S(2)}, u32[]{:S(2)}) collective-permute-start(f32[4,16,128]{2,1,0:T(8,128)S(1)} %get-tuple-element.51.refs_0_), channel_id=1, source_target_pairs={{0,32},{32,64},{64,96},{96,128},{128,160},{160,192},{192,224},{224... | collective-permute-start | bytes 98312 | tf_op jit(solution)/shard_map/ppermute | solution.py:54
  66.4 2.1 %copy-start.9 = (f32[4,16,128]{2,1,0:T(8,128)}, f32[4,16,128]{2,1,0:T(8,128)S(1)}, u32[]{:S(2)}) copy-start(f32[4,16,128]{2,1,0:T(8,128)S(1)} %collective-permute-done.6.refs_5_) | copy-start | bytes 98308
  66.4 2.1 %copy-start.10 = (f32[4,16,128]{2,1,0:T(8,128)}, f32[4,16,128]{2,1,0:T(8,128)S(1)}, u32[]{:S(2)}) copy-start(f32[4,16,128]{2,1,0:T(8,128)S(1)} %collective-permute-done.5.refs_4_) | copy-start | bytes 98308
  66.5 2.1 %copy-start.11 = (f32[4,16,128]{2,1,0:T(8,128)}, f32[4,16,128]{2,1,0:T(8,128)S(1)}, u32[]{:S(2)}) copy-start(f32[4,16,128]{2,1,0:T(8,128)S(1)} %collective-permute-done.4.refs_3_) | copy-start | bytes 98308
  69.1 41.9 %all-to-all-start.3 = ((f32[8,24,16,128]{3,2,1,0:T(8,128)}), f32[8,24,16,128]{3,2,1,0:T(8,128)}, u32[]{:S(2)}, u32[]{:S(2)}) async-start(f32[8,24,16,128]{3,2,1,0:T(8,128)} %get-tuple-element.62), calls=%async_computation.3 | async-start | bytes 3145728 | tf_op jit(solution)/shard_map/all_to_all | solution.py:43
  77.2 1.3 collective-permute-start.9
  78.5 6.3 %collective-permute-start.12 = (f32[136,128]{1,0:T(8,128)S(1)}, f32[136,128]{1,0:T(8,128)S(1)}, u32[]{:S(2)}, u32[]{:S(2)}) collective-permute-start(f32[136,128]{1,0:T(8,128)S(1)} %add.62), channel_id=1, source_target_pairs={{0,6},{1,7},{2,4},{3,5},{4,2},{5,3},{6,0},{7,1},{8,14},{9,15},{10,... | collective-permute-start | bytes 208904 | tf_op jit(solution)/shard_map/ppermute | solution.py:66
  81.6 6.2 %collective-permute-start.11 = (f32[136,128]{1,0:T(8,128)S(1)}, f32[136,128]{1,0:T(8,128)S(1)}, u32[]{:S(2)}, u32[]{:S(2)}) collective-permute-start(f32[136,128]{1,0:T(8,128)S(1)} %add.62), channel_id=1, source_target_pairs={{0,4},{1,5},{2,6},{3,7},{4,0},{5,1},{6,2},{7,3},{8,12},{9,13},{10,... | collective-permute-start | bytes 208904 | tf_op jit(solution)/shard_map/ppermute | solution.py:66
  82.3 5.5 %collective-permute-start.10 = (f32[136,128]{1,0:T(8,128)S(1)}, f32[136,128]{1,0:T(8,128)S(1)}, u32[]{:S(2)}, u32[]{:S(2)}) collective-permute-start(f32[136,128]{1,0:T(8,128)S(1)} %add.62), channel_id=1, source_target_pairs={{0,2},{1,3},{2,0},{3,1},{4,6},{5,7},{6,4},{7,5},{8,10},{9,11},{10,... | collective-permute-start | bytes 208904 | tf_op jit(solution)/shard_map/ppermute | solution.py:66
  87.8 5.8 %collective-permute-start.15 = (f32[136,128]{1,0:T(8,128)S(1)}, f32[136,128]{1,0:T(8,128)S(1)}, u32[]{:S(2)}, u32[]{:S(2)}) collective-permute-start(f32[136,128]{1,0:T(8,128)S(1)} %add_add_fusion.1), channel_id=1, source_target_pairs={{0,24},{1,25},{2,26},{3,27},{4,28},{5,29},{6,30},{7,31},{8,16},{9,... | collective-permute-start | bytes 208904 | tf_op jit(solution)/shard_map/ppermute | solution.py:66
  88.6 5.8 %collective-permute-start.14 = (f32[136,128]{1,0:T(8,128)S(1)}, f32[136,128]{1,0:T(8,128)S(1)}, u32[]{:S(2)}, u32[]{:S(2)}) collective-permute-start(f32[136,128]{1,0:T(8,128)S(1)} %add_add_fusion.1), channel_id=1, source_target_pairs={{0,16},{1,17},{2,18},{3,19},{4,20},{5,21},{6,22},{7,23},{8,24},{9,... | collective-permute-start | bytes 208904 | tf_op jit(solution)/shard_map/ppermute | solution.py:66
  91.0 4.3 %collective-permute-start.13 = (f32[136,128]{1,0:T(8,128)S(1)}, f32[136,128]{1,0:T(8,128)S(1)}, u32[]{:S(2)}, u32[]{:S(2)}) collective-permute-start(f32[136,128]{1,0:T(8,128)S(1)} %add_add_fusion.1), channel_id=1, source_target_pairs={{0,8},{1,9},{2,10},{3,11},{4,12},{5,13},{6,14},{7,15},{8,0},{9,1},... | collective-permute-start | bytes 208904 | tf_op jit(solution)/shard_map/ppermute | solution.py:66
  111.0 41.7 %all-to-all-start.2 = ((f32[8,24,16,128]{3,2,1,0:T(8,128)}), f32[8,24,16,128]{3,2,1,0:T(8,128)S(1)}, u32[]{:S(2)}, u32[]{:S(2)}) async-start(f32[8,24,16,128]{3,2,1,0:T(8,128)} %mix.1), calls=%async_computation.2 | async-start | bytes 3145728 | tf_op jit(solution)/shard_map/all_to_all | solution.py:43
  120.3 1.3 collective-permute-start.16
  121.6 12.0 %collective-permute-start.19 = (f32[128,128]{1,0:T(8,128)S(1)}, f32[128,128]{1,0:T(8,128)S(1)}, u32[]{:S(2)}, u32[]{:S(2)}) collective-permute-start(f32[128,128]{1,0:T(8,128)S(1)} %add.69), channel_id=1, source_target_pairs={{0,6},{1,7},{2,4},{3,5},{4,2},{5,3},{6,0},{7,1},{8,14},{9,15},{10,... | collective-permute-start | bytes 196616 | tf_op jit(solution)/shard_map/ppermute | solution.py:66
  123.0 10.6 %collective-permute-start.18 = (f32[128,128]{1,0:T(8,128)S(1)}, f32[128,128]{1,0:T(8,128)S(1)}, u32[]{:S(2)}, u32[]{:S(2)}) collective-permute-start(f32[128,128]{1,0:T(8,128)S(1)} %add.69), channel_id=1, source_target_pairs={{0,4},{1,5},{2,6},{3,7},{4,0},{5,1},{6,2},{7,3},{8,12},{9,13},{10,... | collective-permute-start | bytes 196616 | tf_op jit(solution)/shard_map/ppermute | solution.py:66
  124.7 8.9 %collective-permute-start.17 = (f32[128,128]{1,0:T(8,128)S(1)}, f32[128,128]{1,0:T(8,128)S(1)}, u32[]{:S(2)}, u32[]{:S(2)}) collective-permute-start(f32[128,128]{1,0:T(8,128)S(1)} %add.69), channel_id=1, source_target_pairs={{0,2},{1,3},{2,0},{3,1},{4,6},{5,7},{6,4},{7,5},{8,10},{9,11},{10,... | collective-permute-start | bytes 196616 | tf_op jit(solution)/shard_map/ppermute | solution.py:66
  125.9 11.9 %collective-permute-start.23 = (f32[4,136,64]{2,1,0:T(8,128)S(1)}, f32[4,136,64]{2,1,0:T(8,128)S(1)}, u32[]{:S(2)}, u32[]{:S(2)}) collective-permute-start(f32[4,136,64]{2,1,0:T(8,128)S(1)} %get-tuple-element.88), channel_id=1, source_target_pairs={{0,1},{1,2},{2,3},{3,4},{4,5},{5,6},{6,7},{7,8},{8,9},{9,10},{10,1... | collective-permute-start | bytes 417800 | tf_op jit(solution)/shard_map/ppermute | solution.py:82
  127.9 10.5 %collective-permute-start.24 = (f32[4,136,64]{2,1,0:T(8,128)S(1)}, f32[4,136,64]{2,1,0:T(8,128)S(1)}, u32[]{:S(2)}, u32[]{:S(2)}) collective-permute-start(f32[4,136,64]{2,1,0:T(8,128)S(1)} %get-tuple-element.89), channel_id=1, source_target_pairs={{1,0},{2,1},{3,2},{4,3},{5,4},{6,5},{7,6},{8,7},{9,8},{10,9},{11,1... | collective-permute-start | bytes 417800 | tf_op jit(solution)/shard_map/ppermute | solution.py:87
  133.7 5.6 %collective-permute-start.22 = (f32[128,128]{1,0:T(8,128)S(1)}, f32[128,128]{1,0:T(8,128)S(1)}, u32[]{:S(2)}, u32[]{:S(2)}) collective-permute-start(f32[128,128]{1,0:T(8,128)S(1)} %add_add_fusion.3), channel_id=1, source_target_pairs={{0,24},{1,25},{2,26},{3,27},{4,28},{5,29},{6,30},{7,31},{8,16},{9,... | collective-permute-start | bytes 196616 | tf_op jit(solution)/shard_map/ppermute | solution.py:66
  133.8 7.4 %collective-permute-start.21 = (f32[128,128]{1,0:T(8,128)S(1)}, f32[128,128]{1,0:T(8,128)S(1)}, u32[]{:S(2)}, u32[]{:S(2)}) collective-permute-start(f32[128,128]{1,0:T(8,128)S(1)} %add_add_fusion.3), channel_id=1, source_target_pairs={{0,16},{1,17},{2,18},{3,19},{4,20},{5,21},{6,22},{7,23},{8,24},{9,... | collective-permute-start | bytes 196616 | tf_op jit(solution)/shard_map/ppermute | solution.py:66
  137.0 4.3 %collective-permute-start.20 = (f32[128,128]{1,0:T(8,128)S(1)}, f32[128,128]{1,0:T(8,128)S(1)}, u32[]{:S(2)}, u32[]{:S(2)}) collective-permute-start(f32[128,128]{1,0:T(8,128)S(1)} %add_add_fusion.3), channel_id=1, source_target_pairs={{0,8},{1,9},{2,10},{3,11},{4,12},{5,13},{6,14},{7,15},{8,0},{9,1},... | collective-permute-start | bytes 196616 | tf_op jit(solution)/shard_map/ppermute | solution.py:66
  142.6 8.9 %collective-permute-start.25 = (f32[2,40,128]{2,1,0:T(8,128)S(1)}, f32[2,40,128]{2,1,0:T(8,128)S(1)}, u32[]{:S(2)}, u32[]{:S(2)}) collective-permute-start(f32[2,40,128]{2,1,0:T(8,128)S(1)} %get-tuple-element.70), channel_id=1, source_target_pairs={{0,32},{32,0},{64,96},{96,64},{128,160},{160,128},{192,224},{224,1... | collective-permute-start | bytes 122888 | tf_op jit(solution)/shard_map/ppermute | solution.py:59
  144.7 8.7 %collective-permute-start.28 = (f32[2,40,128]{2,1,0:T(8,128)S(1)}, f32[2,40,128]{2,1,0:T(8,128)S(1)}, u32[]{:S(2)}, u32[]{:S(2)}) collective-permute-start(f32[2,40,128]{2,1,0:T(8,128)S(1)} %get-tuple-element.76), channel_id=1, source_target_pairs={{0,64},{32,96},{64,0},{96,32},{128,192},{160,224},{192,128},{224,1... | collective-permute-start | bytes 122888 | tf_op jit(solution)/shard_map/ppermute | solution.py:59
  147.0 7.3 %collective-permute-start.29 = (f32[2,40,128]{2,1,0:T(8,128)S(1)}, f32[2,40,128]{2,1,0:T(8,128)S(1)}, u32[]{:S(2)}, u32[]{:S(2)}) collective-permute-start(f32[2,40,128]{2,1,0:T(8,128)S(1)} %get-tuple-element.77), channel_id=1, source_target_pairs={{0,96},{32,64},{64,32},{96,0},{128,224},{160,192},{192,160},{224,1... | collective-permute-start | bytes 122888 | tf_op jit(solution)/shard_map/ppermute | solution.py:59
  154.4 10.9 %collective-permute-start.30 = (f32[40,128]{1,0:T(8,128)S(1)}, f32[40,128]{1,0:T(8,128)S(1)}, u32[]{:S(2)}, u32[]{:S(2)}) collective-permute-start(f32[40,128]{1,0:T(8,128)S(1)} %get-tuple-element.90), channel_id=1, source_target_pairs={{0,128},{32,160},{64,192},{96,224},{128,0},{160,32},{192,64},{224,... | collective-permute-start | bytes 61448 | tf_op jit(solution)/shard_map/ppermute | solution.py:59
  157.6 9.9 %collective-permute-start.26 = (f32[4,16,1024]{2,1,0:T(8,128)S(1)}, f32[4,16,1024]{2,1,0:T(8,128)S(1)}, u32[]{:S(2)}, u32[]{:S(2)}) collective-permute-start(f32[4,16,1024]{2,1,0:T(8,128)S(1)} %get-tuple-element.72), channel_id=1, source_target_pairs={{0,1},{1,2},{2,3},{3,4},{4,5},{5,6},{6,7},{7,8},{8,9},{9,10},{10,1... | collective-permute-start | bytes 786440 | tf_op jit(solution)/shard_map/ppermute | solution.py:82
  159.5 9.6 %collective-permute-start.27 = (f32[4,16,1024]{2,1,0:T(8,128)S(1)}, f32[4,16,1024]{2,1,0:T(8,128)S(1)}, u32[]{:S(2)}, u32[]{:S(2)}) collective-permute-start(f32[4,16,1024]{2,1,0:T(8,128)S(1)} %get-tuple-element.73), channel_id=1, source_target_pairs={{1,0},{2,1},{3,2},{4,3},{5,4},{6,5},{7,6},{8,7},{9,8},{10,9},{11,1... | collective-permute-start | bytes 786440 | tf_op jit(solution)/shard_map/ppermute | solution.py:87
  165.3 3.9 %copy-start.2 = (f32[8,16,1024]{2,1,0:T(8,128)S(1)}, f32[8,16,1024]{2,1,0:T(8,128)}, u32[]{:S(2)}) copy-start(f32[8,16,1024]{2,1,0:T(8,128)} %get-tuple-element.80.east1_ref) | copy-start | bytes 1572868
  165.3 3.9 %copy-start.3 = (f32[8,16,1024]{2,1,0:T(8,128)S(1)}, f32[8,16,1024]{2,1,0:T(8,128)}, u32[]{:S(2)}) copy-start(f32[8,16,1024]{2,1,0:T(8,128)} %get-tuple-element.81.north1_ref) | copy-start | bytes 1572868
  165.3 3.8 %copy-start.4 = (f32[8,16,1024]{2,1,0:T(8,128)S(1)}, f32[8,16,1024]{2,1,0:T(8,128)}, u32[]{:S(2)}) copy-start(f32[8,16,1024]{2,1,0:T(8,128)} %get-tuple-element.82.east2_ref) | copy-start | bytes 1572868
  165.3 3.8 %copy-start.5 = (f32[8,16,1024]{2,1,0:T(8,128)S(1)}, f32[8,16,1024]{2,1,0:T(8,128)}, u32[]{:S(2)}) copy-start(f32[8,16,1024]{2,1,0:T(8,128)} %get-tuple-element.83.north2_ref) | copy-start | bytes 1572868
  172.6 15.3 %all-to-all-start.4 = ((f32[8,8,1024]{2,1,0:T(8,128)}), f32[8,8,1024]{2,1,0:T(8,128)S(1)}, u32[]{:S(2)}, u32[]{:S(2)}) async-start(f32[8,8,1024]{2,1,0:T(8,128)} %broadcast_in_dim.8), calls=%async_computation.4 | async-start | bytes 524288 | tf_op jit(solution)/shard_map/all_to_all | solution.py:49
  (2 other events, 1.2 us)

commit v6 on v5

--- a/solution.py
+++ b/solution.py
@@ -549,9 +549,13 @@
         far_ins=(0, 1, 2),
         name="prepare",
     )
-    packed = jnp.concatenate([obs_index.T.astype(jnp.float32), obs_value.T, obs_var.T])
-    packed = jnp.pad(packed, ((0, 0), (0, block_cols - packed.shape[1])))
-    params = gathered(packed, "ens")
+    packed = [
+        jnp.broadcast_to(a.T[None], (groups,) + a.T.shape)
+        for a in (obs_index.astype(jnp.float32), obs_value, obs_var)
+    ]
+    packed = jnp.concatenate(packed, axis=1)
+    packed = jnp.pad(packed, ((0, 0), (0, 0), (0, block_cols - packed.shape[2])))
+    params = exchanged(packed)
     above, below = from_above(tail), from_below(head)
     cot_out, params = lax.optimization_barrier((cot_out, params))
     cot = exchanged(cot_out).reshape(groups, sites, own_members, block_cols)

time: 191 us -> 192 us (level)
    all_to_all x3 -> x4, starting transfers between devices: 14.7 us -> 23.1 us  [exchanged(): return lax.all_to_all(blocks, 'ens', 0, 0, tiled=False)]
    all_to_all x2 -> x1, starting transfers between devices: 12.6 us -> 4.15 us  [gathered(): return lax.all_to_all(copies, axis, 0, 0, tiled=False)]
    all_to_all x2 -> x1, waiting for transfers between devices: 15.1 us -> 9.71 us  [gathered(): return lax.all_to_all(copies, axis, 0, 0, tiled=False)]
    all_to_all x3 -> x4, waiting for transfers between devices: 3.48 us -> 8.88 us  [exchanged(): return lax.all_to_all(blocks, 'ens', 0, 0, tiled=False)]
where the time goes in v6:
time: 192 us; the launch traced here: 189 us
  starting transfers between devices  89.9 us (47%)
  waiting for transfers between devices  55.2 us (29%)
  Pallas kernels  35.7 us (19%)
  local copies, waits for them, and re-layouts  5.61 us (3%)
    pallas_call x11, Pallas kernels, kernel_call(): pl.pallas_call(body, out_shape=[made(i, o) for i, o in enumerate(outs)],...  35.7 us
    all_to_all x4, starting transfers between devices, exchanged(): return lax.all_to_all(blocks, 'ens', 0, 0, tiled=False)  23.1 us
    ppermute x3, starting transfers between devices, from_below(): lax.ppermute(rows_sent, 'space', [(i + 1, i) for i in range(count - 1)])  17.3 us
    ppermute x14, starting transfers between devices, other(): lax.ppermute(block, 'space', [(i, i ^ distance) for i in range(count)])  17.1 us
    ppermute x7, starting transfers between devices, turned(): lax.ppermute(block, 'ens', [(i, (i + distance) % count) for i in range(co...  14.8 us
    ppermute x14, waiting for transfers between devices, other(): lax.ppermute(block, 'space', [(i, i ^ distance) for i in range(count)])  13.4 us
    all_to_all x1, waiting for transfers between devices, gathered(): return lax.all_to_all(copies, axis, 0, 0, tiled=False)  9.71 us
    all_to_all x4, waiting for transfers between devices, exchanged(): return lax.all_to_all(blocks, 'ens', 0, 0, tiled=False)  8.88 us
  transfers between devices with their start and end apart: 36, of which 22 were waited for; matrix products, arithmetic and copies ran while one was open for 1% of the time, Pallas kernels for 17%

profile of v6, /device:TPU:6, one launch (start us, length us, event | category | flops | bytes accessed | tf_op | source)
XLA Modules:
  0.0 189.3 jit_solution(8360923934928015645)
XLA Ops:
  3.5 8.5 %all-to-all-start = ((f32[8,24,128]{2,1,0:T(8,128)}), f32[8,24,128]{2,1,0:T(8,128)S(1)}, u32[]{:S(2)}, u32[]{:S(2)}) async-start(f32[8,24,128]{2,1,0:T(8,128)} %pad.4), calls=%async_computation | async-start | bytes 196608 | tf_op jit(solution)/shard_map/all_to_all | solution.py:43
  12.0 3.3 %prepare.1 = (f32[11,16,1024]{2,1,0:T(8,128)}, f32[11,16,1024]{2,1,0:T(8,128)}, f32[8,384,128]{2,1,0:T(8,128)}) custom-call(f32[3,8,16,1024]{3,2,1,0:T(8,128)} %state_ref.3, f32[8,1024]{1,0:T(8,128)} %depth_ref.5, f32[384,1024]{1,0:T(8,128)} %bitcast.25), custom_call_target="tpu_custom_call" | custom-call | bytes 6193152 | tf_op jit(solution)/shard_map/prepare/pallas_call | solution.py:29
  15.3 5.4 %all-to-all-done = f32[8,24,128]{2,1,0:T(8,128)S(1)} async-done(((f32[8,24,128]{2,1,0:T(8,128)}), f32[8,24,128]{2,1,0:T(8,128)S(1)}, u32[]{:S(2)}, u32[]{:S(2)}) %all-to-all-start) | async-done | bytes 98336 | tf_op jit(solution)/shard_map/all_to_all | solution.py:43
  20.7 3.7 %all-to-all-start.1 = ((f32[8,384,128]{2,1,0:T(8,128)}), f32[8,384,128]{2,1,0:T(8,128)S(1)}, u32[]{:S(2)}, u32[]{:S(2)}) async-start(f32[8,384,128]{2,1,0:T(8,128)} %get-tuple-element.61), calls=%async_computation.1 | async-start | bytes 3145728 | tf_op jit(solution)/shard_map/all_to_all | solution.py:43
  24.4 1.9 %collective-permute-start = (f32[11,16,1024]{2,1,0:T(8,128)}, f32[11,16,1024]{2,1,0:T(8,128)}, u32[]{:S(2)}, u32[]{:S(2)}) collective-permute-start(f32[11,16,1024]{2,1,0:T(8,128)} %get-tuple-element.47), channel_id=1, source_target_pairs={{0,1},{1,2},{2,3},{3,4},{4,5},{5,6},{6,7},{7,8},{8,9},{9,10},{10,1... | collective-permute-start | bytes 2162696 | tf_op jit(solution)/shard_map/ppermute | solution.py:82
  26.4 5.8 %collective-permute-start.1 = (f32[11,16,1024]{2,1,0:T(8,128)}, f32[11,16,1024]{2,1,0:T(8,128)}, u32[]{:S(2)}, u32[]{:S(2)}) collective-permute-start(f32[11,16,1024]{2,1,0:T(8,128)} %get-tuple-element.48), channel_id=1, source_target_pairs={{1,0},{2,1},{3,2},{4,3},{5,4},{6,5},{7,6},{8,7},{9,8},{10,9},{11,1... | collective-permute-start | bytes 2162696 | tf_op jit(solution)/shard_map/ppermute | solution.py:87
  32.5 7.0 %collective-permute-done.above_ref = f32[11,16,1024]{2,1,0:T(8,128)} collective-permute-done((f32[11,16,1024]{2,1,0:T(8,128)}, f32[11,16,1024]{2,1,0:T(8,128)}, u32[]{:S(2)}, u32[]{:S(2)}) %collective-permute-start) | collective-permute-done | bytes 720928 | tf_op jit(solution)/shard_map/ppermute | solution.py:82
  39.5 1.8 collective-permute-done.1.below_ref
  41.2 5.2 %forward.1 = (f32[8,24,16,128]{3,2,1,0:T(8,128)}, f32[4,16,128]{2,1,0:T(8,128)S(1)}, f32[8,16,1024]{2,1,0:T(8,128)}, f32[8,16,1024]{2,1,0:T(8,128)}, f32[8,16,1024]{2,1,0:T(8,128)}, /*index=5*/f32[8,16,1024]{2,1,0:T(8,128)}) custom-call(f32[16]{0:T(128)S(1)} %and_convert_fusion.inside_ref, f32[3,8,16,1024]{3,2,1,0:T(8,128)S(1)} %copy-done, ...), custom_call_target="tpu_custom_call" | custom-call | flops 100000000 | bytes 6752320 | tf_op jit(solution)/shard_map/forward/pallas_call | solution.py:29
  46.5 3.2 %collective-permute-start.8 = (f32[4,16,128]{2,1,0:T(8,128)S(1)}, f32[4,16,128]{2,1,0:T(8,128)S(1)}, u32[]{:S(2)}, u32[]{:S(2)}) collective-permute-start(f32[4,16,128]{2,1,0:T(8,128)S(1)} %get-tuple-element.51.refs_0_), channel_id=1, source_target_pairs={{0,224},{32,0},{64,32},{96,64},{128,96},{160,128},{192,160},{224,1... | collective-permute-start | bytes 98312 | tf_op jit(solution)/shard_map/ppermute | solution.py:54
  49.8 2.3 %collective-permute-start.7 = (f32[4,16,128]{2,1,0:T(8,128)S(1)}, f32[4,16,128]{2,1,0:T(8,128)S(1)}, u32[]{:S(2)}, u32[]{:S(2)}) collective-permute-start(f32[4,16,128]{2,1,0:T(8,128)S(1)} %get-tuple-element.51.refs_0_), channel_id=1, source_target_pairs={{0,192},{32,224},{64,0},{96,32},{128,64},{160,96},{192,128},{224,1... | collective-permute-start | bytes 98312 | tf_op jit(solution)/shard_map/ppermute | solution.py:54
  52.1 1.4 collective-permute-start.6
  53.5 3.6 %collective-permute-start.5 = (f32[4,16,128]{2,1,0:T(8,128)S(1)}, f32[4,16,128]{2,1,0:T(8,128)S(1)}, u32[]{:S(2)}, u32[]{:S(2)}) collective-permute-start(f32[4,16,128]{2,1,0:T(8,128)S(1)} %get-tuple-element.51.refs_0_), channel_id=1, source_target_pairs={{0,128},{32,160},{64,192},{96,224},{128,0},{160,32},{192,64},{224,... | collective-permute-start | bytes 98312 | tf_op jit(solution)/shard_map/ppermute | solution.py:54
  57.4 5.8 %collective-permute-done.8.refs_7_ = f32[4,16,128]{2,1,0:T(8,128)S(1)} collective-permute-done((f32[4,16,128]{2,1,0:T(8,128)S(1)}, f32[4,16,128]{2,1,0:T(8,128)S(1)}, u32[]{:S(2)}, u32[]{:S(2)}) %collective-permute-start.8) | collective-permute-done | bytes 32800 | tf_op jit(solution)/shard_map/ppermute | solution.py:54
  63.2 4.0 %collective-permute-start.2 = (f32[4,16,128]{2,1,0:T(8,128)S(1)}, f32[4,16,128]{2,1,0:T(8,128)S(1)}, u32[]{:S(2)}, u32[]{:S(2)}) collective-permute-start(f32[4,16,128]{2,1,0:T(8,128)S(1)} %get-tuple-element.51.refs_0_), channel_id=1, source_target_pairs={{0,32},{32,64},{64,96},{96,128},{128,160},{160,192},{192,224},{224... | collective-permute-start | bytes 98312 | tf_op jit(solution)/shard_map/ppermute | solution.py:54
  67.2 2.0 %collective-permute-done.3.refs_2_ = f32[4,16,128]{2,1,0:T(8,128)S(1)} collective-permute-done((f32[4,16,128]{2,1,0:T(8,128)S(1)}, f32[4,16,128]{2,1,0:T(8,128)S(1)}, u32[]{:S(2)}, u32[]{:S(2)}) %collective-permute-start.3) | collective-permute-done | bytes 32800 | tf_op jit(solution)/shard_map/ppermute | solution.py:54
  69.8 5.9 %all-to-all-start.3 = ((f32[8,24,16,128]{3,2,1,0:T(8,128)}), f32[8,24,16,128]{3,2,1,0:T(8,128)}, u32[]{:S(2)}, u32[]{:S(2)}) async-start(f32[8,24,16,128]{3,2,1,0:T(8,128)} %get-tuple-element.62), calls=%async_computation.3 | async-start | bytes 3145728 | tf_op jit(solution)/shard_map/all_to_all | solution.py:43
  75.9 2.0 %gram.1 = (f32[4,128,128]{2,1,0:T(8,128)S(1)}, f32[4,8,128]{2,1,0:T(8,128)S(1)}, f32[136,128]{1,0:T(8,128)S(1)}) custom-call(s32[1]{0:T(128)} %bitcast.place_ref, f32[3,4,128]{2,1,0:T(4,128)S(1)} %reshape.24.params_ref, f32[4,16,128]{2,1,0:T(8,128)} %copy-done.6, f32[4,16,128]{2,1,0:T(8,128)} %copy-done.13, f32[4,16,128]{2,1,0:T(8,128)} %copy-done.12, ...), custom_call_target="tpu_custom_call" | custom-call | flops 100663296 | bytes 616452 | tf_op jit(solution)/shard_map/gram/pallas_call | solution.py:29
  79.2 3.0 %collective-permute-start.12 = (f32[136,128]{1,0:T(8,128)S(1)}, f32[136,128]{1,0:T(8,128)S(1)}, u32[]{:S(2)}, u32[]{:S(2)}) collective-permute-start(f32[136,128]{1,0:T(8,128)S(1)} %add.62), channel_id=1, source_target_pairs={{0,6},{1,7},{2,4},{3,5},{4,2},{5,3},{6,0},{7,1},{8,14},{9,15},{10,... | collective-permute-start | bytes 208904 | tf_op jit(solution)/shard_map/ppermute | solution.py:66
  83.4 2.1 %collective-permute-done.12 = f32[136,128]{1,0:T(8,128)S(1)} collective-permute-done((f32[136,128]{1,0:T(8,128)S(1)}, f32[136,128]{1,0:T(8,128)S(1)}, u32[]{:S(2)}, u32[]{:S(2)}) %collective-permute-start.12) | collective-permute-done | bytes 69664 | tf_op jit(solution)/shard_map/ppermute | solution.py:66
  85.6 2.9 %collective-permute-done.11 = f32[136,128]{1,0:T(8,128)S(1)} collective-permute-done((f32[136,128]{1,0:T(8,128)S(1)}, f32[136,128]{1,0:T(8,128)S(1)}, u32[]{:S(2)}, u32[]{:S(2)}) %collective-permute-start.11) | collective-permute-done | bytes 69664 | tf_op jit(solution)/shard_map/ppermute | solution.py:66
  89.3 2.4 %collective-permute-start.14 = (f32[136,128]{1,0:T(8,128)S(1)}, f32[136,128]{1,0:T(8,128)S(1)}, u32[]{:S(2)}, u32[]{:S(2)}) collective-permute-start(f32[136,128]{1,0:T(8,128)S(1)} %add_add_fusion.1), channel_id=1, source_target_pairs={{0,16},{1,17},{2,18},{3,19},{4,20},{5,21},{6,22},{7,23},{8,24},{9,... | collective-permute-start | bytes 208904 | tf_op jit(solution)/shard_map/ppermute | solution.py:66
  92.9 1.4 collective-permute-done.15
  96.1 11.2 %factor.1 = (f32[128,128]{1,0:T(8,128)S(1)}, f32[128,128]{1,0:T(8,128)S(1)}, f32[8,128]{1,0:T(8,128)S(1)}) custom-call(f32[136,128]{1,0:T(8,128)S(1)} %add_add_fusion.gram_ref), custom_call_target="tpu_custom_call" | custom-call | flops 1000000000 | bytes 204800 | tf_op jit(solution)/shard_map/factor/pallas_call | solution.py:29
  107.3 2.2 %mix.1 = f32[8,24,16,128]{3,2,1,0:T(8,128)} custom-call(f32[128,128]{1,0:T(8,128)S(1)} %get-tuple-element.60.mixing_ref, f32[8,24,16,128]{3,2,1,0:T(8,128)S(1)} %bitcast.23), custom_call_target="tpu_custom_call" | custom-call | flops 10000000000 | bytes 3211264 | tf_op jit(solution)/shard_map/mix/pallas_call | solution.py:29
  109.5 2.2 %all-to-all-done.3.state_ref = f32[8,24,16,128]{3,2,1,0:T(8,128)} async-done(((f32[8,24,16,128]{3,2,1,0:T(8,128)}), f32[8,24,16,128]{3,2,1,0:T(8,128)}, u32[]{:S(2)}, u32[]{:S(2)}) %all-to-all-start.3) | async-done | bytes 1572896 | tf_op jit(solution)/shard_map/all_to_all | solution.py:43
  111.7 5.0 %all-to-all-start.2 = ((f32[8,24,16,128]{3,2,1,0:T(8,128)}), f32[8,24,16,128]{3,2,1,0:T(8,128)S(1)}, u32[]{:S(2)}, u32[]{:S(2)}) async-start(f32[8,24,16,128]{3,2,1,0:T(8,128)} %mix.1), calls=%async_computation.2 | async-start | bytes 3145728 | tf_op jit(solution)/shard_map/all_to_all | solution.py:43
  117.5 3.4 %cross.1 = f32[128,128]{1,0:T(8,128)S(1)} custom-call(f32[8,24,16,128]{3,2,1,0:T(8,128)} %all-to-all-done.3.state_ref, f32[8,24,16,128]{3,2,1,0:T(8,128)S(1)} %bitcast.24), custom_call_target="tpu_custom_call" | custom-call | flops 10000000000 | bytes 3211264 | tf_op jit(solution)/shard_map/cross/pallas_call | solution.py:29
  122.3 1.4 collective-permute-start.19
  123.7 1.7 collective-permute-start.18
  126.7 1.9 %collective-permute-start.23 = (f32[4,136,64]{2,1,0:T(8,128)S(1)}, f32[4,136,64]{2,1,0:T(8,128)S(1)}, u32[]{:S(2)}, u32[]{:S(2)}) collective-permute-start(f32[4,136,64]{2,1,0:T(8,128)S(1)} %get-tuple-element.88), channel_id=1, source_target_pairs={{0,1},{1,2},{2,3},{3,4},{4,5},{5,6},{6,7},{7,8},{8,9},{9,10},{10,1... | collective-permute-start | bytes 417800 | tf_op jit(solution)/shard_map/ppermute | solution.py:82
  128.6 5.8 %collective-permute-start.24 = (f32[4,136,64]{2,1,0:T(8,128)S(1)}, f32[4,136,64]{2,1,0:T(8,128)S(1)}, u32[]{:S(2)}, u32[]{:S(2)}) collective-permute-start(f32[4,136,64]{2,1,0:T(8,128)S(1)} %get-tuple-element.89), channel_id=1, source_target_pairs={{1,0},{2,1},{3,2},{4,3},{5,4},{6,5},{7,6},{8,7},{9,8},{10,9},{11,1... | collective-permute-start | bytes 417800 | tf_op jit(solution)/shard_map/ppermute | solution.py:87
  134.5 3.2 %collective-permute-start.21 = (f32[128,128]{1,0:T(8,128)S(1)}, f32[128,128]{1,0:T(8,128)S(1)}, u32[]{:S(2)}, u32[]{:S(2)}) collective-permute-start(f32[128,128]{1,0:T(8,128)S(1)} %add_add_fusion.3), channel_id=1, source_target_pairs={{0,16},{1,17},{2,18},{3,19},{4,20},{5,21},{6,22},{7,23},{8,24},{9,... | collective-permute-start | bytes 196616 | tf_op jit(solution)/shard_map/ppermute | solution.py:66
  140.0 1.9 %collective-permute-done.21 = f32[128,128]{1,0:T(8,128)S(1)} collective-permute-done((f32[128,128]{1,0:T(8,128)S(1)}, f32[128,128]{1,0:T(8,128)S(1)}, u32[]{:S(2)}, u32[]{:S(2)}) %collective-permute-start.21) | collective-permute-done | bytes 65568 | tf_op jit(solution)/shard_map/ppermute | solution.py:66
  142.0 1.3 pullback.1
  143.3 2.1 %collective-permute-start.25 = (f32[2,40,128]{2,1,0:T(8,128)S(1)}, f32[2,40,128]{2,1,0:T(8,128)S(1)}, u32[]{:S(2)}, u32[]{:S(2)}) collective-permute-start(f32[2,40,128]{2,1,0:T(8,128)S(1)} %get-tuple-element.70), channel_id=1, source_target_pairs={{0,32},{32,0},{64,96},{96,64},{128,160},{160,128},{192,224},{224,1... | collective-permute-start | bytes 122888 | tf_op jit(solution)/shard_map/ppermute | solution.py:59
  145.4 2.4 %collective-permute-start.28 = (f32[2,40,128]{2,1,0:T(8,128)S(1)}, f32[2,40,128]{2,1,0:T(8,128)S(1)}, u32[]{:S(2)}, u32[]{:S(2)}) collective-permute-start(f32[2,40,128]{2,1,0:T(8,128)S(1)} %get-tuple-element.76), channel_id=1, source_target_pairs={{0,64},{32,96},{64,0},{96,32},{128,192},{160,224},{192,128},{224,1... | collective-permute-start | bytes 122888 | tf_op jit(solution)/shard_map/ppermute | solution.py:59
  148.6 3.6 %collective-permute-done.25 = f32[2,40,128]{2,1,0:T(8,128)S(1)} collective-permute-done((f32[2,40,128]{2,1,0:T(8,128)S(1)}, f32[2,40,128]{2,1,0:T(8,128)S(1)}, u32[]{:S(2)}, u32[]{:S(2)}) %collective-permute-start.25) | collective-permute-done | bytes 40992 | tf_op jit(solution)/shard_map/ppermute | solution.py:59
  152.2 1.3 all-to-all-done.2.back_ref
  155.1 3.1 %collective-permute-start.30 = (f32[40,128]{1,0:T(8,128)S(1)}, f32[40,128]{1,0:T(8,128)S(1)}, u32[]{:S(2)}, u32[]{:S(2)}) collective-permute-start(f32[40,128]{1,0:T(8,128)S(1)} %get-tuple-element.90), channel_id=1, source_target_pairs={{0,128},{32,160},{64,192},{96,224},{128,0},{160,32},{192,64},{224,... | collective-permute-start | bytes 61448 | tf_op jit(solution)/shard_map/ppermute | solution.py:59
  158.3 1.9 %collective-permute-start.26 = (f32[4,16,1024]{2,1,0:T(8,128)S(1)}, f32[4,16,1024]{2,1,0:T(8,128)S(1)}, u32[]{:S(2)}, u32[]{:S(2)}) collective-permute-start(f32[4,16,1024]{2,1,0:T(8,128)S(1)} %get-tuple-element.72), channel_id=1, source_target_pairs={{0,1},{1,2},{2,3},{3,4},{4,5},{5,6},{6,7},{7,8},{8,9},{9,10},{10,1... | collective-permute-start | bytes 786440 | tf_op jit(solution)/shard_map/ppermute | solution.py:82
  160.2 5.8 %collective-permute-start.27 = (f32[4,16,1024]{2,1,0:T(8,128)S(1)}, f32[4,16,1024]{2,1,0:T(8,128)S(1)}, u32[]{:S(2)}, u32[]{:S(2)}) collective-permute-start(f32[4,16,1024]{2,1,0:T(8,128)S(1)} %get-tuple-element.73), channel_id=1, source_target_pairs={{1,0},{2,1},{3,2},{4,3},{5,4},{6,5},{7,6},{8,7},{9,8},{10,9},{11,1... | collective-permute-start | bytes 786440 | tf_op jit(solution)/shard_map/ppermute | solution.py:87
  166.0 2.2 %observe.1.seen_ref = f32[16,16,1024]{2,1,0:T(8,128)S(1)} custom-call(f32[40,128]{1,0:T(8,128)S(1)} %get-tuple-element.91.refs_0_, f32[40,128]{1,0:T(8,128)S(1)} %collective-permute-done.30.refs_1_, f32[8,136,128]{2,1,0:T(8,128)S(1)} %maximum_maximum_fusion.refs_2_), custom_call_target="tpu_custom_call" | custom-call | flops 99999997952 | bytes 1646592 | tf_op jit(solution)/shard_map/observe/pallas_call | solution.py:29
  168.2 1.6 collective-permute-done.27.below_ref
  169.8 2.7 %backward.1 = (f32[8,1024]{1,0:T(8,128)S(1)}, f32[10,16,1024]{2,1,0:T(8,128)S(1)}, f32[8,16,1024]{2,1,0:T(8,128)S(1)}, f32[10,16,1024]{2,1,0:T(8,128)S(1)}) custom-call(f32[16]{0:T(128)S(1)} %and_convert_fusion.inside_ref, f32[8,24,16,128]{3,2,1,0:T(8,128)S(1)} %all-to-all-done.2.back_ref, f32[4,16,1024]{2,1,0:T(8,128)S(1)} %collective-permute-done.26.above_ref, ...), custom_call_target="tpu_custom_call" | custom-call | flops 100000000 | bytes 7176256 | tf_op jit(solution)/shard_map/backward/pallas_call | solution.py:29
  173.3 4.1 %all-to-all-start.4 = ((f32[8,8,1024]{2,1,0:T(8,128)}), f32[8,8,1024]{2,1,0:T(8,128)S(1)}, u32[]{:S(2)}, u32[]{:S(2)}) async-start(f32[8,8,1024]{2,1,0:T(8,128)} %broadcast_in_dim.14), calls=%async_computation.4 | async-start | bytes 524288 | tf_op jit(solution)/shard_map/all_to_all | solution.py:49
  177.4 1.5 finish.1
  178.9 9.7 %all-to-all-done.4 = f32[8,8,1024]{2,1,0:T(8,128)S(1)} async-done(((f32[8,8,1024]{2,1,0:T(8,128)}), f32[8,8,1024]{2,1,0:T(8,128)S(1)}, u32[]{:S(2)}, u32[]{:S(2)}) %all-to-all-start.4) | async-done | bytes 262176 | tf_op jit(solution)/shard_map/all_to_all | solution.py:49
  (95 shorter events, 20.1 us)
Async XLA Ops:
  3.5 17.2 %all-to-all-start = ((f32[8,24,128]{2,1,0:T(8,128)}), f32[8,24,128]{2,1,0:T(8,128)S(1)}, u32[]{:S(2)}, u32[]{:S(2)}) async-start(f32[8,24,128]{2,1,0:T(8,128)} %pad.4), calls=%async_computation | async-start | bytes 196608 | tf_op jit(solution)/shard_map/all_to_all | solution.py:43
  20.7 20.5 %copy-start = (f32[3,8,16,1024]{3,2,1,0:T(8,128)S(1)}, f32[3,8,16,1024]{3,2,1,0:T(8,128)}, u32[]{:S(2)}) copy-start(f32[3,8,16,1024]{3,2,1,0:T(8,128)} %state_ref.3) | copy-start | bytes 4718596
  20.7 20.5 %copy-start.1 = (f32[8,1024]{1,0:T(8,128)S(1)}, f32[8,1024]{1,0:T(8,128)}, u32[]{:S(2)}) copy-start(f32[8,1024]{1,0:T(8,128)} %depth_ref.5) | copy-start | bytes 98308
  20.7 48.5 %all-to-all-start.1 = ((f32[8,384,128]{2,1,0:T(8,128)}), f32[8,384,128]{2,1,0:T(8,128)S(1)}, u32[]{:S(2)}, u32[]{:S(2)}) async-start(f32[8,384,128]{2,1,0:T(8,128)} %get-tuple-element.61), calls=%async_computation.1 | async-start | bytes 3145728 | tf_op jit(solution)/shard_map/all_to_all | solution.py:43
  24.4 15.0 %collective-permute-start = (f32[11,16,1024]{2,1,0:T(8,128)}, f32[11,16,1024]{2,1,0:T(8,128)}, u32[]{:S(2)}, u32[]{:S(2)}) collective-permute-start(f32[11,16,1024]{2,1,0:T(8,128)} %get-tuple-element.47), channel_id=1, source_target_pairs={{0,1},{1,2},{2,3},{3,4},{4,5},{5,6},{6,7},{7,8},{8,9},{9,10},{10,1... | collective-permute-start | bytes 2162696 | tf_op jit(solution)/shard_map/ppermute | solution.py:82
  26.4 14.9 %collective-permute-start.1 = (f32[11,16,1024]{2,1,0:T(8,128)}, f32[11,16,1024]{2,1,0:T(8,128)}, u32[]{:S(2)}, u32[]{:S(2)}) collective-permute-start(f32[11,16,1024]{2,1,0:T(8,128)} %get-tuple-element.48), channel_id=1, source_target_pairs={{1,0},{2,1},{3,2},{4,3},{5,4},{6,5},{7,6},{8,7},{9,8},{10,9},{11,1... | collective-permute-start | bytes 2162696 | tf_op jit(solution)/shard_map/ppermute | solution.py:87
  46.5 22.7 %copy-start.6 = (f32[4,16,128]{2,1,0:T(8,128)}, f32[4,16,128]{2,1,0:T(8,128)S(1)}, u32[]{:S(2)}) copy-start(f32[4,16,128]{2,1,0:T(8,128)S(1)} %get-tuple-element.51.refs_0_) | copy-start | bytes 98308
  46.5 16.6 %collective-permute-start.8 = (f32[4,16,128]{2,1,0:T(8,128)S(1)}, f32[4,16,128]{2,1,0:T(8,128)S(1)}, u32[]{:S(2)}, u32[]{:S(2)}) collective-permute-start(f32[4,16,128]{2,1,0:T(8,128)S(1)} %get-tuple-element.51.refs_0_), channel_id=1, source_target_pairs={{0,224},{32,0},{64,32},{96,64},{128,96},{160,128},{192,160},{224,1... | collective-permute-start | bytes 98312 | tf_op jit(solution)/shard_map/ppermute | solution.py:54
  49.8 13.4 %collective-permute-start.7 = (f32[4,16,128]{2,1,0:T(8,128)S(1)}, f32[4,16,128]{2,1,0:T(8,128)S(1)}, u32[]{:S(2)}, u32[]{:S(2)}) collective-permute-start(f32[4,16,128]{2,1,0:T(8,128)S(1)} %get-tuple-element.51.refs_0_), channel_id=1, source_target_pairs={{0,192},{32,224},{64,0},{96,32},{128,64},{160,96},{192,128},{224,1... | collective-permute-start | bytes 98312 | tf_op jit(solution)/shard_map/ppermute | solution.py:54
  52.1 15.0 %collective-permute-start.6 = (f32[4,16,128]{2,1,0:T(8,128)S(1)}, f32[4,16,128]{2,1,0:T(8,128)S(1)}, u32[]{:S(2)}, u32[]{:S(2)}) collective-permute-start(f32[4,16,128]{2,1,0:T(8,128)S(1)} %get-tuple-element.51.refs_0_), channel_id=1, source_target_pairs={{0,160},{32,192},{64,224},{96,0},{128,32},{160,64},{192,96},{224,1... | collective-permute-start | bytes 98312 | tf_op jit(solution)/shard_map/ppermute | solution.py:54
  53.5 13.6 %collective-permute-start.5 = (f32[4,16,128]{2,1,0:T(8,128)S(1)}, f32[4,16,128]{2,1,0:T(8,128)S(1)}, u32[]{:S(2)}, u32[]{:S(2)}) collective-permute-start(f32[4,16,128]{2,1,0:T(8,128)S(1)} %get-tuple-element.51.refs_0_), channel_id=1, source_target_pairs={{0,128},{32,160},{64,192},{96,224},{128,0},{160,32},{192,64},{224,... | collective-permute-start | bytes 98312 | tf_op jit(solution)/shard_map/ppermute | solution.py:54
  57.1 10.0 %collective-permute-start.4 = (f32[4,16,128]{2,1,0:T(8,128)S(1)}, f32[4,16,128]{2,1,0:T(8,128)S(1)}, u32[]{:S(2)}, u32[]{:S(2)}) collective-permute-start(f32[4,16,128]{2,1,0:T(8,128)S(1)} %get-tuple-element.51.refs_0_), channel_id=1, source_target_pairs={{0,96},{32,128},{64,160},{96,192},{128,224},{160,0},{192,32},{224,... | collective-permute-start | bytes 98312 | tf_op jit(solution)/shard_map/ppermute | solution.py:54
  63.2 6.1 %copy-start.7 = (f32[4,16,128]{2,1,0:T(8,128)}, f32[4,16,128]{2,1,0:T(8,128)S(1)}, u32[]{:S(2)}) copy-start(f32[4,16,128]{2,1,0:T(8,128)S(1)} %collective-permute-done.8.refs_7_) | copy-start | bytes 98308
  63.2 6.0 %collective-permute-start.3 = (f32[4,16,128]{2,1,0:T(8,128)S(1)}, f32[4,16,128]{2,1,0:T(8,128)S(1)}, u32[]{:S(2)}, u32[]{:S(2)}) collective-permute-start(f32[4,16,128]{2,1,0:T(8,128)S(1)} %get-tuple-element.51.refs_0_), channel_id=1, source_target_pairs={{0,64},{32,96},{64,128},{96,160},{128,192},{160,224},{192,0},{224,... | collective-permute-start | bytes 98312 | tf_op jit(solution)/shard_map/ppermute | solution.py:54
  63.2 6.1 %copy-start.8 = (f32[4,16,128]{2,1,0:T(8,128)}, f32[4,16,128]{2,1,0:T(8,128)S(1)}, u32[]{:S(2)}) copy-start(f32[4,16,128]{2,1,0:T(8,128)S(1)} %collective-permute-done.7.refs_6_) | copy-start | bytes 98308
  63.2 6.0 %collective-permute-start.2 = (f32[4,16,128]{2,1,0:T(8,128)S(1)}, f32[4,16,128]{2,1,0:T(8,128)S(1)}, u32[]{:S(2)}, u32[]{:S(2)}) collective-permute-start(f32[4,16,128]{2,1,0:T(8,128)S(1)} %get-tuple-element.51.refs_0_), channel_id=1, source_target_pairs={{0,32},{32,64},{64,96},{96,128},{128,160},{160,192},{192,224},{224... | collective-permute-start | bytes 98312 | tf_op jit(solution)/shard_map/ppermute | solution.py:54
  67.1 2.1 %copy-start.9 = (f32[4,16,128]{2,1,0:T(8,128)}, f32[4,16,128]{2,1,0:T(8,128)S(1)}, u32[]{:S(2)}) copy-start(f32[4,16,128]{2,1,0:T(8,128)S(1)} %collective-permute-done.6.refs_5_) | copy-start | bytes 98308
  67.1 2.1 %copy-start.10 = (f32[4,16,128]{2,1,0:T(8,128)}, f32[4,16,128]{2,1,0:T(8,128)S(1)}, u32[]{:S(2)}) copy-start(f32[4,16,128]{2,1,0:T(8,128)S(1)} %collective-permute-done.5.refs_4_) | copy-start | bytes 98308
  67.2 2.1 %copy-start.11 = (f32[4,16,128]{2,1,0:T(8,128)}, f32[4,16,128]{2,1,0:T(8,128)S(1)}, u32[]{:S(2)}) copy-start(f32[4,16,128]{2,1,0:T(8,128)S(1)} %collective-permute-done.4.refs_3_) | copy-start | bytes 98308
  69.8 41.9 %all-to-all-start.3 = ((f32[8,24,16,128]{3,2,1,0:T(8,128)}), f32[8,24,16,128]{3,2,1,0:T(8,128)}, u32[]{:S(2)}, u32[]{:S(2)}) async-start(f32[8,24,16,128]{3,2,1,0:T(8,128)} %get-tuple-element.62), calls=%async_computation.3 | async-start | bytes 3145728 | tf_op jit(solution)/shard_map/all_to_all | solution.py:43
  77.9 1.3 collective-permute-start.9
  79.2 6.3 %collective-permute-start.12 = (f32[136,128]{1,0:T(8,128)S(1)}, f32[136,128]{1,0:T(8,128)S(1)}, u32[]{:S(2)}, u32[]{:S(2)}) collective-permute-start(f32[136,128]{1,0:T(8,128)S(1)} %add.62), channel_id=1, source_target_pairs={{0,6},{1,7},{2,4},{3,5},{4,2},{5,3},{6,0},{7,1},{8,14},{9,15},{10,... | collective-permute-start | bytes 208904 | tf_op jit(solution)/shard_map/ppermute | solution.py:66
  82.3 6.2 %collective-permute-start.11 = (f32[136,128]{1,0:T(8,128)S(1)}, f32[136,128]{1,0:T(8,128)S(1)}, u32[]{:S(2)}, u32[]{:S(2)}) collective-permute-start(f32[136,128]{1,0:T(8,128)S(1)} %add.62), channel_id=1, source_target_pairs={{0,4},{1,5},{2,6},{3,7},{4,0},{5,1},{6,2},{7,3},{8,12},{9,13},{10,... | collective-permute-start | bytes 208904 | tf_op jit(solution)/shard_map/ppermute | solution.py:66
  83.0 5.5 %collective-permute-start.10 = (f32[136,128]{1,0:T(8,128)S(1)}, f32[136,128]{1,0:T(8,128)S(1)}, u32[]{:S(2)}, u32[]{:S(2)}) collective-permute-start(f32[136,128]{1,0:T(8,128)S(1)} %add.62), channel_id=1, source_target_pairs={{0,2},{1,3},{2,0},{3,1},{4,6},{5,7},{6,4},{7,5},{8,10},{9,11},{10,... | collective-permute-start | bytes 208904 | tf_op jit(solution)/shard_map/ppermute | solution.py:66
  88.5 5.8 %collective-permute-start.15 = (f32[136,128]{1,0:T(8,128)S(1)}, f32[136,128]{1,0:T(8,128)S(1)}, u32[]{:S(2)}, u32[]{:S(2)}) collective-permute-start(f32[136,128]{1,0:T(8,128)S(1)} %add_add_fusion.1), channel_id=1, source_target_pairs={{0,24},{1,25},{2,26},{3,27},{4,28},{5,29},{6,30},{7,31},{8,16},{9,... | collective-permute-start | bytes 208904 | tf_op jit(solution)/shard_map/ppermute | solution.py:66
  89.3 5.8 %collective-permute-start.14 = (f32[136,128]{1,0:T(8,128)S(1)}, f32[136,128]{1,0:T(8,128)S(1)}, u32[]{:S(2)}, u32[]{:S(2)}) collective-permute-start(f32[136,128]{1,0:T(8,128)S(1)} %add_add_fusion.1), channel_id=1, source_target_pairs={{0,16},{1,17},{2,18},{3,19},{4,20},{5,21},{6,22},{7,23},{8,24},{9,... | collective-permute-start | bytes 208904 | tf_op jit(solution)/shard_map/ppermute | solution.py:66
  91.7 4.3 %collective-permute-start.13 = (f32[136,128]{1,0:T(8,128)S(1)}, f32[136,128]{1,0:T(8,128)S(1)}, u32[]{:S(2)}, u32[]{:S(2)}) collective-permute-start(f32[136,128]{1,0:T(8,128)S(1)} %add_add_fusion.1), channel_id=1, source_target_pairs={{0,8},{1,9},{2,10},{3,11},{4,12},{5,13},{6,14},{7,15},{8,0},{9,1},... | collective-permute-start | bytes 208904 | tf_op jit(solution)/shard_map/ppermute | solution.py:66
  111.7 41.7 %all-to-all-start.2 = ((f32[8,24,16,128]{3,2,1,0:T(8,128)}), f32[8,24,16,128]{3,2,1,0:T(8,128)S(1)}, u32[]{:S(2)}, u32[]{:S(2)}) async-start(f32[8,24,16,128]{3,2,1,0:T(8,128)} %mix.1), calls=%async_computation.2 | async-start | bytes 3145728 | tf_op jit(solution)/shard_map/all_to_all | solution.py:43
  121.0 1.3 collective-permute-start.16
  122.3 12.0 %collective-permute-start.19 = (f32[128,128]{1,0:T(8,128)S(1)}, f32[128,128]{1,0:T(8,128)S(1)}, u32[]{:S(2)}, u32[]{:S(2)}) collective-permute-start(f32[128,128]{1,0:T(8,128)S(1)} %add.69), channel_id=1, source_target_pairs={{0,6},{1,7},{2,4},{3,5},{4,2},{5,3},{6,0},{7,1},{8,14},{9,15},{10,... | collective-permute-start | bytes 196616 | tf_op jit(solution)/shard_map/ppermute | solution.py:66
  123.7 10.6 %collective-permute-start.18 = (f32[128,128]{1,0:T(8,128)S(1)}, f32[128,128]{1,0:T(8,128)S(1)}, u32[]{:S(2)}, u32[]{:S(2)}) collective-permute-start(f32[128,128]{1,0:T(8,128)S(1)} %add.69), channel_id=1, source_target_pairs={{0,4},{1,5},{2,6},{3,7},{4,0},{5,1},{6,2},{7,3},{8,12},{9,13},{10,... | collective-permute-start | bytes 196616 | tf_op jit(solution)/shard_map/ppermute | solution.py:66
  125.4 8.9 %collective-permute-start.17 = (f32[128,128]{1,0:T(8,128)S(1)}, f32[128,128]{1,0:T(8,128)S(1)}, u32[]{:S(2)}, u32[]{:S(2)}) collective-permute-start(f32[128,128]{1,0:T(8,128)S(1)} %add.69), channel_id=1, source_target_pairs={{0,2},{1,3},{2,0},{3,1},{4,6},{5,7},{6,4},{7,5},{8,10},{9,11},{10,... | collective-permute-start | bytes 196616 | tf_op jit(solution)/shard_map/ppermute | solution.py:66
  126.7 11.9 %collective-permute-start.23 = (f32[4,136,64]{2,1,0:T(8,128)S(1)}, f32[4,136,64]{2,1,0:T(8,128)S(1)}, u32[]{:S(2)}, u32[]{:S(2)}) collective-permute-start(f32[4,136,64]{2,1,0:T(8,128)S(1)} %get-tuple-element.88), channel_id=1, source_target_pairs={{0,1},{1,2},{2,3},{3,4},{4,5},{5,6},{6,7},{7,8},{8,9},{9,10},{10,1... | collective-permute-start | bytes 417800 | tf_op jit(solution)/shard_map/ppermute | solution.py:82
  128.6 10.5 %collective-permute-start.24 = (f32[4,136,64]{2,1,0:T(8,128)S(1)}, f32[4,136,64]{2,1,0:T(8,128)S(1)}, u32[]{:S(2)}, u32[]{:S(2)}) collective-permute-start(f32[4,136,64]{2,1,0:T(8,128)S(1)} %get-tuple-element.89), channel_id=1, source_target_pairs={{1,0},{2,1},{3,2},{4,3},{5,4},{6,5},{7,6},{8,7},{9,8},{10,9},{11,1... | collective-permute-start | bytes 417800 | tf_op jit(solution)/shard_map/ppermute | solution.py:87
  134.4 5.6 %collective-permute-start.22 = (f32[128,128]{1,0:T(8,128)S(1)}, f32[128,128]{1,0:T(8,128)S(1)}, u32[]{:S(2)}, u32[]{:S(2)}) collective-permute-start(f32[128,128]{1,0:T(8,128)S(1)} %add_add_fusion.3), channel_id=1, source_target_pairs={{0,24},{1,25},{2,26},{3,27},{4,28},{5,29},{6,30},{7,31},{8,16},{9,... | collective-permute-start | bytes 196616 | tf_op jit(solution)/shard_map/ppermute | solution.py:66
  134.5 7.4 %collective-permute-start.21 = (f32[128,128]{1,0:T(8,128)S(1)}, f32[128,128]{1,0:T(8,128)S(1)}, u32[]{:S(2)}, u32[]{:S(2)}) collective-permute-start(f32[128,128]{1,0:T(8,128)S(1)} %add_add_fusion.3), channel_id=1, source_target_pairs={{0,16},{1,17},{2,18},{3,19},{4,20},{5,21},{6,22},{7,23},{8,24},{9,... | collective-permute-start | bytes 196616 | tf_op jit(solution)/shard_map/ppermute | solution.py:66
  137.7 4.3 %collective-permute-start.20 = (f32[128,128]{1,0:T(8,128)S(1)}, f32[128,128]{1,0:T(8,128)S(1)}, u32[]{:S(2)}, u32[]{:S(2)}) collective-permute-start(f32[128,128]{1,0:T(8,128)S(1)} %add_add_fusion.3), channel_id=1, source_target_pairs={{0,8},{1,9},{2,10},{3,11},{4,12},{5,13},{6,14},{7,15},{8,0},{9,1},... | collective-permute-start | bytes 196616 | tf_op jit(solution)/shard_map/ppermute | solution.py:66
  143.3 8.9 %collective-permute-start.25 = (f32[2,40,128]{2,1,0:T(8,128)S(1)}, f32[2,40,128]{2,1,0:T(8,128)S(1)}, u32[]{:S(2)}, u32[]{:S(2)}) collective-permute-start(f32[2,40,128]{2,1,0:T(8,128)S(1)} %get-tuple-element.70), channel_id=1, source_target_pairs={{0,32},{32,0},{64,96},{96,64},{128,160},{160,128},{192,224},{224,1... | collective-permute-start | bytes 122888 | tf_op jit(solution)/shard_map/ppermute | solution.py:59
  145.4 8.7 %collective-permute-start.28 = (f32[2,40,128]{2,1,0:T(8,128)S(1)}, f32[2,40,128]{2,1,0:T(8,128)S(1)}, u32[]{:S(2)}, u32[]{:S(2)}) collective-permute-start(f32[2,40,128]{2,1,0:T(8,128)S(1)} %get-tuple-element.76), channel_id=1, source_target_pairs={{0,64},{32,96},{64,0},{96,32},{128,192},{160,224},{192,128},{224,1... | collective-permute-start | bytes 122888 | tf_op jit(solution)/shard_map/ppermute | solution.py:59
  147.7 7.3 %collective-permute-start.29 = (f32[2,40,128]{2,1,0:T(8,128)S(1)}, f32[2,40,128]{2,1,0:T(8,128)S(1)}, u32[]{:S(2)}, u32[]{:S(2)}) collective-permute-start(f32[2,40,128]{2,1,0:T(8,128)S(1)} %get-tuple-element.77), channel_id=1, source_target_pairs={{0,96},{32,64},{64,32},{96,0},{128,224},{160,192},{192,160},{224,1... | collective-permute-start | bytes 122888 | tf_op jit(solution)/shard_map/ppermute | solution.py:59
  155.1 10.9 %collective-permute-start.30 = (f32[40,128]{1,0:T(8,128)S(1)}, f32[40,128]{1,0:T(8,128)S(1)}, u32[]{:S(2)}, u32[]{:S(2)}) collective-permute-start(f32[40,128]{1,0:T(8,128)S(1)} %get-tuple-element.90), channel_id=1, source_target_pairs={{0,128},{32,160},{64,192},{96,224},{128,0},{160,32},{192,64},{224,... | collective-permute-start | bytes 61448 | tf_op jit(solution)/shard_map/ppermute | solution.py:59
  158.3 9.9 %collective-permute-start.26 = (f32[4,16,1024]{2,1,0:T(8,128)S(1)}, f32[4,16,1024]{2,1,0:T(8,128)S(1)}, u32[]{:S(2)}, u32[]{:S(2)}) collective-permute-start(f32[4,16,1024]{2,1,0:T(8,128)S(1)} %get-tuple-element.72), channel_id=1, source_target_pairs={{0,1},{1,2},{2,3},{3,4},{4,5},{5,6},{6,7},{7,8},{8,9},{9,10},{10,1... | collective-permute-start | bytes 786440 | tf_op jit(solution)/shard_map/ppermute | solution.py:82
  160.2 9.6 %collective-permute-start.27 = (f32[4,16,1024]{2,1,0:T(8,128)S(1)}, f32[4,16,1024]{2,1,0:T(8,128)S(1)}, u32[]{:S(2)}, u32[]{:S(2)}) collective-permute-start(f32[4,16,1024]{2,1,0:T(8,128)S(1)} %get-tuple-element.73), channel_id=1, source_target_pairs={{1,0},{2,1},{3,2},{4,3},{5,4},{6,5},{7,6},{8,7},{9,8},{10,9},{11,1... | collective-permute-start | bytes 786440 | tf_op jit(solution)/shard_map/ppermute | solution.py:87
  166.0 3.9 %copy-start.2 = (f32[8,16,1024]{2,1,0:T(8,128)S(1)}, f32[8,16,1024]{2,1,0:T(8,128)}, u32[]{:S(2)}) copy-start(f32[8,16,1024]{2,1,0:T(8,128)} %get-tuple-element.80.east1_ref) | copy-start | bytes 1572868
  166.0 3.9 %copy-start.3 = (f32[8,16,1024]{2,1,0:T(8,128)S(1)}, f32[8,16,1024]{2,1,0:T(8,128)}, u32[]{:S(2)}) copy-start(f32[8,16,1024]{2,1,0:T(8,128)} %get-tuple-element.81.north1_ref) | copy-start | bytes 1572868
  166.0 3.8 %copy-start.4 = (f32[8,16,1024]{2,1,0:T(8,128)S(1)}, f32[8,16,1024]{2,1,0:T(8,128)}, u32[]{:S(2)}) copy-start(f32[8,16,1024]{2,1,0:T(8,128)} %get-tuple-element.82.east2_ref) | copy-start | bytes 1572868
  166.0 3.8 %copy-start.5 = (f32[8,16,1024]{2,1,0:T(8,128)S(1)}, f32[8,16,1024]{2,1,0:T(8,128)}, u32[]{:S(2)}) copy-start(f32[8,16,1024]{2,1,0:T(8,128)} %get-tuple-element.83.north2_ref) | copy-start | bytes 1572868
  173.3 15.3 %all-to-all-start.4 = ((f32[8,8,1024]{2,1,0:T(8,128)}), f32[8,8,1024]{2,1,0:T(8,128)S(1)}, u32[]{:S(2)}, u32[]{:S(2)}) async-start(f32[8,8,1024]{2,1,0:T(8,128)} %broadcast_in_dim.14), calls=%async_computation.4 | async-start | bytes 524288 | tf_op jit(solution)/shard_map/all_to_all | solution.py:49
  (2 other events, 1.2 us)
